TPU v7x, 512 devices: a whole 4x8x8 slice. The times are simulated.
512 devices in a mesh: dp: 64 (over z, x, core), mp: 8 (over y).
Axes of the slice: x: 4, y: 8, z: 8, core: 2. Of those that a mesh axis runs over, the one named last changes fastest.
Arguments:
- activations: bfloat16 [8192, 4096], P('dp', 'mp'), may hold values from -6 to 6
- cotangent: bfloat16 [8192, 14336], P(('dp', 'mp')), may hold values from -0.0625 to 0.0625
- master: float32 [14336, 4096], P('dp', 'mp'), may hold values from -6 to 6
- first_moment: float32 [14336, 4096], P('dp', 'mp'), may hold values from -6 to 6
- second_moment: float32 [14336, 4096], P('dp', 'mp'), may hold values from 0.25 to 4
- new_owner: int32 [7168], P('dp'), may hold values from 0 to 63, as said below
- new_slot: int32 [7168], P('dp'), may hold values from 0 to 113, as said below
Outputs:
- new_master: float32 [14592, 4096], P('dp', 'mp')
- new_moment1: float32 [14592, 4096], P('dp', 'mp')
- new_moment2: float32 [14592, 4096], P('dp', 'mp')
- new_weights: bfloat16 [14592, 4096], P('dp')
Inputs may be any that keep to these rules, and one draw needn't show every extreme that they name: `new_owner`: one index of dp, the departing one, owns no piece. Every index of dp sends 2 or 1 of its pieces to every other surviving index and to itself if it survives, none to the departing one; every surviving index ends with 114 or 113 pieces. `new_slot`: the slots of the pieces of one new owner are distinct.
All inputs are finite; a program needn't handle non-finite values.
Results may differ from a plain program's by a relative error of at most 0.001.
Values may be sent and summed in bfloat16 or wider, within the bound.
No kernel may reach another device: no remote copies, remote signals or barrier semaphores. Data moves between devices by JAX's collectives and lax.ppermute only.
A program may use at most 64 MiB of HBM per device.

v0:
```python
import jax
import jax.numpy as jnp
from jax import lax
from jax.sharding import PartitionSpec as P

beta_one = 0.9
beta_two = 0.95
learn_rate = 0.1
adam_eps = 1e-08
adam_step = 1000
fix_one = 1.0 - beta_one**adam_step
fix_two = 1.0 - beta_two**adam_step


def adam_update(master, first_moment, second_moment, grad):
    moment1_next = beta_one * first_moment + (1.0 - beta_one) * grad
    moment2_next = beta_two * second_moment + (1.0 - beta_two) * grad * grad
    update = learn_rate * (moment1_next / fix_one) / (jnp.sqrt(moment2_next / fix_two) + adam_eps)
    return (master - update, moment1_next, moment2_next)


def shards(activations, cotangent, master, first_moment, second_moment, new_owner, new_slot):
    dp_count = lax.axis_size("dp")
    rows_dev, width_dev = master.shape
    blocks = new_owner.shape[0]
    piece_rows = rows_dev // blocks
    pair_most = (blocks + dp_count - 2) // (dp_count - 1)
    capacity = (blocks * dp_count + dp_count - 2) // (dp_count - 1)
    shared = lax.all_to_all(cotangent[None], "dp", split_axis=2, concat_axis=0, tiled=True)
    cotangent_all = lax.all_gather(shared, "mp", axis=1, tiled=True)
    cotangent_all = cotangent_all.reshape(-1, rows_dev)
    grad = lax.dot_general(
        cotangent_all,
        lax.all_gather(activations, "dp", axis=0, tiled=True),
        (((0,), (0,)), ((), ())),
        preferred_element_type=jnp.float32,
    )
    matching = new_owner[:, None] == new_owner[None, :]
    counter = jnp.arange(blocks, dtype=jnp.int32)
    earlier = counter[None, :] < counter[:, None]
    rank_number = jnp.sum((matching & earlier).astype(jnp.int32), axis=1)
    position = new_owner * pair_most + rank_number
    slot_buffer = jnp.full((dp_count * pair_most,), capacity, jnp.int32).at[position].set(new_slot)
    slot_buffer = slot_buffer.reshape(dp_count, pair_most)

    def to_buffer(field):
        flat = field.reshape(blocks, piece_rows * width_dev)
        filled = (
            jnp.zeros((dp_count * pair_most, piece_rows * width_dev), field.dtype)
            .at[position]
            .set(flat)
        )
        return filled.reshape(dp_count, pair_most, piece_rows * width_dev)

    def from_buffer(received, state_slots):
        flat = received.reshape(dp_count * pair_most, piece_rows * width_dev)
        placed = jnp.zeros((capacity, piece_rows * width_dev), received.dtype)
        placed = placed.at[state_slots.reshape(-1)].set(flat, mode="drop")
        return placed.reshape(capacity * piece_rows, width_dev)

    master_next, moment1_next, moment2_next = adam_update(master, first_moment, second_moment, grad)
    arrived = (
        lax.all_to_all(to_buffer(master_next), "dp", split_axis=0, concat_axis=0, tiled=True),
        lax.all_to_all(to_buffer(moment1_next), "dp", split_axis=0, concat_axis=0, tiled=True),
        lax.all_to_all(to_buffer(moment2_next), "dp", split_axis=0, concat_axis=0, tiled=True),
        lax.all_to_all(slot_buffer, "dp", split_axis=0, concat_axis=0, tiled=True),
    )
    new_master = from_buffer(arrived[0], arrived[3])
    new_moment1 = from_buffer(arrived[1], arrived[3])
    new_moment2 = from_buffer(arrived[2], arrived[3])
    new_weights = lax.all_gather(new_master.astype(jnp.bfloat16), "mp", axis=1, tiled=True)
    return (new_master, new_moment1, new_moment2, new_weights)


def solution(mesh):
    in_specs = (
        P("dp", "mp"),
        P(("dp", "mp"), None),
        P("dp", "mp"),
        P("dp", "mp"),
        P("dp", "mp"),
        P("dp"),
        P("dp"),
    )
    out_specs = (P("dp", "mp"), P("dp", "mp"), P("dp", "mp"), P("dp", None))
    return jax.shard_map(shards, mesh=mesh, in_specs=in_specs, out_specs=out_specs, check_vma=False)
```

profile of v0, /device:TPU:1, one launch (start us, length us, event | category | flops | bytes accessed | tf_op | source)
XLA Modules:
  0.0 405.9 jit_solution(3722686728019806352)
XLA Ops:
  7.2 0.0 all-gather.9.cloned.1.call-start
  7.2 13.7 %copy.22 = bf16[1,16,14336]{1,0,2:T(2,128)(2,1)} copy(bf16[1,16,14336]{2,1,0:T(8,128)(2,1)} %bitcast.23) | data formatting | bytes 917504 | tf_op jit(solution)/shard_map/broadcast_in_dim | solution.py:29
  21.0 0.5 broadcast.73
  21.5 79.8 %reduce.4 = bf16[14336,16]{1,0:T(8,128)(2,1)} reduce(bf16[14336,1,16]{2,1,0:T(2,128)(2,1)} %bitcast.19, bf16[]{:T(256)} %broadcast.73), dimensions={1}, to_apply=%bitcast.14.reduce_sub_computation | reduce | bytes 917506
  101.3 5.3 %reshape.186 = bf16[64,2,1792]{2,1,0:T(2,128)(2,1)S(1)} reshape(bf16[14336,16]{1,0:T(8,128)(2,1)} %reduce.4) | data formatting | bytes 917504
  106.6 31.0 %all_to_all.42 = bf16[64,2,1792]{2,1,0:T(2,128)(2,1)S(1)} all-to-all(bf16[64,2,1792]{2,1,0:T(2,128)(2,1)S(1)} %reshape.186), channel_id=1, replica_groups=mesh['dp'=64,'mp'=8] {'dp'}, dimensions={0} | all-to-all | bytes 917504 | tf_op jit(solution)/shard_map/all_to_all | solution.py:29
  137.7 9.3 %reshape.187 = bf16[14336,1,16]{2,1,0:T(2,128)(2,1)} reshape(bf16[64,2,1792]{2,1,0:T(2,128)(2,1)S(1)} %all_to_all.42) | data formatting | bytes 917504
  147.0 0.0 copy-start.4
  147.0 13.5 %copy.23 = bf16[1,16,14336]{2,1,0:T(8,128)(2,1)S(1)} copy(bf16[1,16,14336]{1,0,2:T(2,128)(2,1)} %bitcast.20) | data formatting | bytes 917504 | tf_op jit(solution)/shard_map/all_to_all | solution.py:29
  160.5 1.5 all_to_all.31
  162.0 0.0 all-gather.9.cloned.1.call-update
  162.1 0.0 all-gather.5.cloned.1.call-start
  162.1 0.7 all-gather.5.cloned.1.call-update
  162.8 0.0 copy-done.4
  162.8 0.2 convert_reduce_fusion
  163.0 1.1 scatter_custom_fusion
  164.1 0.8 all_to_all.28
  164.8 5.7 %all-to-all-start = ((s32[64,1,2]{2,1,0:T(1,128)}), s32[64,1,2]{2,1,0:T(1,128)S(1)}, u32[]{:S(2)}, u32[]{:S(2)}) async-start(s32[64,1,2]{2,1,0:T(1,128)} %bitcast), calls=%async_computation | async-start | bytes 65536 | tf_op jit(solution)/shard_map/all_to_all | solution.py:66
  170.5 0.0 copy-start.1
  170.5 0.0 copy-start.2
  170.5 0.0 copy-start.3
  170.5 45.1 %all-gather.9.cloned.1.call-done = bf16[64,1,128,224]{3,0,1,2:T(8,128)(2,1)} async-done(((bf16[64,1,16,224]{3,0,1,2:T(8,128)(2,1)}), bf16[64,1,128,224]{3,0,1,2:T(8,128)(2,1)}) %all-gather.9.cloned.1.call-update) | async-done | bytes 3670032 | tf_op jit(solution)/shard_map/all_gather | solution.py:30
  215.7 7.3 %copy.25 = bf16[64,1,128,224]{2,0,3,1:T(8,128)(2,1)} copy(bf16[64,1,128,224]{3,0,1,2:T(8,128)(2,1)} %all-gather.9.cloned.1.call-done) | data formatting | bytes 7340032 | tf_op jit(solution)/shard_map/all_gather | solution.py:30
  222.9 85.4 %all-gather.5.cloned.1.call-done = bf16[8192,512]{1,0:T(8,128)(2,1)} async-done(((bf16[128,512]{1,0:T(8,128)(2,1)}), bf16[8192,512]{1,0:T(8,128)(2,1)}) %all-gather.5.cloned.1.call-update) | async-done | bytes 8388624 | tf_op jit(solution)/shard_map/all_gather | solution.py:34
  308.3 0.0 copy-done.1
  308.3 0.0 copy-done.2
  308.3 0.0 copy-done.3
  308.3 8.6 %divide_subtract_fusion = (f32[224,512]{1,0:T(8,128)S(1)}, f32[224,512]{1,0:T(8,128)S(1)}, f32[224,512]{1,0:T(8,128)S(1)}) fusion(f32[224,512]{1,0:T(8,128)S(1)} %copy-done.1, f32[224,512]{1,0:T(8,128)S(1)} %copy-done.2, f32[224,512]{1,0:T(8,128)S(1)} %copy-done.3, bf16[8192,512]{1,0:T(8,128)(2,1)} %all-gather.5.cloned.1.call-done, ...), kind=kOutput, calls=%fused_computation.12 | convolution fusion | flops 1880309760 | bytes 14811136 | tf_op jit(solution)/shard_map/dot_general | solution.py:32
  316.8 0.1 reshape.113
  317.0 1.1 scatter_custom_fusion.1
  318.1 1.1 reshape.90
  319.2 0.0 all-to-all-done
  319.2 5.5 %all-to-all-start.2 = ((f32[64,2,1024]{2,1,0:T(2,128)}), f32[64,2,1024]{2,1,0:T(2,128)S(1)}, u32[]{:S(2)}, u32[]{:S(2)}) async-start(f32[64,2,1024]{2,1,0:T(2,128)} %reshape.90), calls=%async_computation.2 | async-start | bytes 1048576 | tf_op jit(solution)/shard_map/all_to_all | solution.py:63
  324.7 0.0 all-gather.7.cloned.1.call-start
  324.7 0.5 broadcast.71
  325.3 0.7 reduce.3
  326.0 0.1 reshape.87
  326.1 16.3 %all-to-all-done.2 = f32[64,2,1024]{2,1,0:T(2,128)S(1)} async-done(((f32[64,2,1024]{2,1,0:T(2,128)}), f32[64,2,1024]{2,1,0:T(2,128)S(1)}, u32[]{:S(2)}, u32[]{:S(2)}) %all-to-all-start.2) | async-done | bytes 524320 | tf_op jit(solution)/shard_map/all_to_all | solution.py:63
  342.4 0.4 reshape.121
  342.8 1.1 scatter_custom_fusion.2
  343.9 0.1 reshape.92
  344.0 0.0 copy-start
  344.0 0.8 convert_element_type.7
  344.8 0.0 all-gather.7.cloned.1.call-update
  344.8 0.1 reshape.145
  345.0 1.1 scatter_custom_fusion.5
  346.1 1.1 reshape.98
  347.2 5.7 %all-to-all-start.4 = ((f32[64,2,1024]{2,1,0:T(2,128)}), f32[64,2,1024]{2,1,0:T(2,128)S(1)}, u32[]{:S(2)}, u32[]{:S(2)}) async-start(f32[64,2,1024]{2,1,0:T(2,128)} %reshape.98), calls=%async_computation.4 | async-start | bytes 1048576 | tf_op jit(solution)/shard_map/all_to_all | solution.py:65
  352.9 0.1 reshape.129
  353.1 1.1 scatter_custom_fusion.3
  354.2 1.1 reshape.94
  355.3 15.4 %all-to-all-done.4 = f32[64,2,1024]{2,1,0:T(2,128)S(1)} async-done(((f32[64,2,1024]{2,1,0:T(2,128)}), f32[64,2,1024]{2,1,0:T(2,128)S(1)}, u32[]{:S(2)}, u32[]{:S(2)}) %all-to-all-start.4) | async-done | bytes 524320 | tf_op jit(solution)/shard_map/all_to_all | solution.py:65
  370.6 0.0 copy-done
  370.6 5.7 %all-to-all-start.3 = ((f32[64,2,1024]{2,1,0:T(2,128)}), f32[64,2,1024]{2,1,0:T(2,128)S(1)}, u32[]{:S(2)}, u32[]{:S(2)}) async-start(f32[64,2,1024]{2,1,0:T(2,128)} %reshape.94), calls=%async_computation.3 | async-start | bytes 1048576 | tf_op jit(solution)/shard_map/all_to_all | solution.py:64
  376.4 0.4 reshape.153
  376.7 1.1 scatter_custom_fusion.6
  377.9 0.8 reshape.100
  378.7 15.4 %all-to-all-done.3 = f32[64,2,1024]{2,1,0:T(2,128)S(1)} async-done(((f32[64,2,1024]{2,1,0:T(2,128)}), f32[64,2,1024]{2,1,0:T(2,128)S(1)}, u32[]{:S(2)}, u32[]{:S(2)}) %all-to-all-start.3) | async-done | bytes 524320 | tf_op jit(solution)/shard_map/all_to_all | solution.py:64
  394.1 0.4 reshape.137
  394.5 1.1 scatter_custom_fusion.4
  395.6 0.8 reshape.96
  396.4 0.0 all-gather.7.cloned.1.call-done
  396.4 3.0 copy.34
  (2 shorter events, 0.0 us)
Async XLA Ops:
  7.2 208.5 %all-gather.9.cloned.1.call-start = ((), (), s32[]{:S(2)}) async-start(), calls=%async_computation.7 | async-start | bytes 4718592 | tf_op jit(solution)/shard_map/all_gather | solution.py:30
  147.0 15.8 %copy-start.4 = (s32[112]{0:T(128)S(1)}, s32[112]{0:T(128)}, u32[]{:S(2)}) copy-start(s32[112]{0:T(128)} %param.12) | copy-start | bytes 1348
  162.1 146.2 %all-gather.5.cloned.1.call-start = ((), (), s32[]{:S(2)}) async-start(), calls=%async_computation.5 | async-start | bytes 8519680 | tf_op jit(solution)/shard_map/all_gather | solution.py:34
  164.8 154.4 %all-to-all-start = ((s32[64,1,2]{2,1,0:T(1,128)}), s32[64,1,2]{2,1,0:T(1,128)S(1)}, u32[]{:S(2)}, u32[]{:S(2)}) async-start(s32[64,1,2]{2,1,0:T(1,128)} %bitcast), calls=%async_computation | async-start | bytes 65536 | tf_op jit(solution)/shard_map/all_to_all | solution.py:66
  170.5 137.8 %copy-start.1 = (f32[224,512]{1,0:T(8,128)S(1)}, f32[224,512]{1,0:T(8,128)}, u32[]{:S(2)}) copy-start(f32[224,512]{1,0:T(8,128)} %param.9) | copy-start | bytes 1376260
  170.5 137.7 %copy-start.2 = (f32[224,512]{1,0:T(8,128)S(1)}, f32[224,512]{1,0:T(8,128)}, u32[]{:S(2)}) copy-start(f32[224,512]{1,0:T(8,128)} %param.10) | copy-start | bytes 1376260
  170.5 137.7 %copy-start.3 = (f32[224,512]{1,0:T(8,128)S(1)}, f32[224,512]{1,0:T(8,128)}, u32[]{:S(2)}) copy-start(f32[224,512]{1,0:T(8,128)} %param.11) | copy-start | bytes 1376260
  319.2 23.2 %all-to-all-start.2 = ((f32[64,2,1024]{2,1,0:T(2,128)}), f32[64,2,1024]{2,1,0:T(2,128)S(1)}, u32[]{:S(2)}, u32[]{:S(2)}) async-start(f32[64,2,1024]{2,1,0:T(2,128)} %reshape.90), calls=%async_computation.2 | async-start | bytes 1048576 | tf_op jit(solution)/shard_map/all_to_all | solution.py:63
  324.7 71.8 %all-gather.7.cloned.1.call-start = ((), (), s32[]{:S(2)}) async-start(), calls=%async_computation.6 | async-start | bytes 2138112 | tf_op jit(solution)/shard_map/all_gather | solution.py:71
  344.0 26.7 %copy-start = (f32[228,512]{1,0:T(8,128)}, f32[228,512]{1,0:T(8,128)S(1)}, u32[]{:S(2)}) copy-start(f32[228,512]{1,0:T(8,128)S(1)} %reshape.92) | copy-start | bytes 1400836
  347.2 23.4 %all-to-all-start.4 = ((f32[64,2,1024]{2,1,0:T(2,128)}), f32[64,2,1024]{2,1,0:T(2,128)S(1)}, u32[]{:S(2)}, u32[]{:S(2)}) async-start(f32[64,2,1024]{2,1,0:T(2,128)} %reshape.98), calls=%async_computation.4 | async-start | bytes 1048576 | tf_op jit(solution)/shard_map/all_to_all | solution.py:65
  370.6 23.4 %all-to-all-start.3 = ((f32[64,2,1024]{2,1,0:T(2,128)}), f32[64,2,1024]{2,1,0:T(2,128)S(1)}, u32[]{:S(2)}, u32[]{:S(2)}) async-start(f32[64,2,1024]{2,1,0:T(2,128)} %reshape.94), calls=%async_computation.3 | async-start | bytes 1048576 | tf_op jit(solution)/shard_map/all_to_all | solution.py:64
Sparse Core Ops, SparseCore 0:
  162.2 53.4 all-gather.8
  219.0 89.2 all-gather.4
  344.9 35.0 all-gather.6
where the time goes:
time: 408 us; the launch traced here: 406 us
  waiting for transfers between devices  178 us (44%)
  other arithmetic  81.5 us (20%)
  local copies, waits for them, and re-layouts  70 us (17%)
  blocking collectives  31 us (8%)
  starting transfers between devices  22.7 us (6%)
  between operations  14 us (3%)
  matrix products  8.56 us (2%)
    all_gather x1, waiting for transfers between devices, shards(): lax.all_gather(activations, 'dp', axis=0, tiled=True)  85.4 us
    unnamed x1, other arithmetic  79.8 us
    all_gather x1, waiting for transfers between devices, shards(): cotangent_all = lax.all_gather(shared, 'mp', axis=1, tiled=True)  45.1 us
    all_to_all x1, blocking collectives, shards(): lax.all_to_all(cotangent[None], 'dp', split_axis=2, concat_axis=0, tiled=...  31 us
    unnamed x14, local copies, waits for them, and re-layouts  18.2 us
    all_to_all x1, waiting for transfers between devices, shards(): lax.all_to_all(to_buffer(master_next), 'dp', split_axis=0, concat_axis=0,...  16.3 us
    all_to_all x1, waiting for transfers between devices, shards(): lax.all_to_all(to_buffer(moment2_next), 'dp', split_axis=0, concat_axis=0...  15.4 us
    all_to_all x1, waiting for transfers between devices, shards(): lax.all_to_all(to_buffer(moment1_next), 'dp', split_axis=0, concat_axis=0...  15.4 us
  transfers between devices with their start and end apart: 7, of which 5 were waited for; matrix products, arithmetic and copies ran while one was open for 7% of the time, Pallas kernels for 0%

commit v1 on v0

v1 whole, which is shorter than its diff:
```python
import functools

import jax
import jax.numpy as jnp
import numpy as np
from jax import lax
from jax.experimental import pallas as pl
from jax.experimental.pallas import tpu as pltpu
from jax.sharding import Mesh, PartitionSpec as P

beta_one = 0.9
beta_two = 0.95
learn_rate = 0.1
adam_eps = 1e-08
adam_step = 1000
fix_one = 1.0 - beta_one**adam_step
fix_two = 1.0 - beta_two**adam_step

Z, X, CORES, Y = 8, 4, 2, 8
CHIPS = Z * X
DP = CHIPS * CORES
ROWS = 224
PAD = 256
PIECES = 112
PAIR = 2
CAP = 114
WIDTH = 512

VMEM = pl.BlockSpec(memory_space=pltpu.VMEM)
SMEM = pl.BlockSpec(memory_space=pltpu.SMEM)
LIMIT = 56 * 1024 * 1024


def call(kernel, out_shape, in_specs, out_specs, **kw):
    return pl.pallas_call(
        kernel,
        out_shape=out_shape,
        in_specs=in_specs,
        out_specs=out_specs,
        compiler_params=pltpu.CompilerParams(vmem_limit_bytes=LIMIT),
        **kw,
    )


def pack_cotangent(core_ref, cot_ref, out_ref):
    tokens = cot_ref.shape[0]
    blank = jnp.zeros((tokens, PAD - ROWS), jnp.bfloat16)

    def fill(flip):
        for chip in range(CHIPS):
            for core in range(CORES):
                start = ROWS * (CORES * chip + core)
                block = jnp.concatenate([cot_ref[:, start : start + ROWS], blank], axis=1)
                place = PAD * (core ^ flip)
                out_ref[chip, :, place : place + PAD] = block

    @pl.when(core_ref[0] == 0)
    def _():
        fill(0)

    @pl.when(core_ref[0] == 1)
    def _():
        fill(1)


def pack_pieces(position_ref, field_ref, out_ref):
    out_ref[...] = jnp.zeros_like(out_ref)
    for piece in range(PIECES):
        out_ref[position_ref[piece]] = field_ref[PAIR * piece : PAIR * piece + PAIR, :]


def pack_states(position_ref, a_ref, b_ref, c_ref, out_ref):
    out_ref[...] = jnp.zeros_like(out_ref)
    for piece in range(PIECES):
        place = position_ref[piece]
        for index, ref in enumerate((a_ref, b_ref, c_ref)):
            out_ref[place, :, WIDTH * index : WIDTH * (index + 1)] = ref[PAIR * piece : PAIR * piece + PAIR, :]


def pack_grad(position_ref, mine_ref, theirs_ref, out_ref):
    out_ref[...] = jnp.zeros_like(out_ref)
    for piece in range(PIECES):
        rows = slice(PAIR * piece, PAIR * piece + PAIR)
        out_ref[position_ref[piece]] = mine_ref[rows, :] + theirs_ref[rows, :]


def partial_grad(me_ref, cot_ref, own_ref, left_ref, low_ref, high_ref, right_ref, after_ref, mine_ref, theirs_ref):
    step = pl.program_id(0)
    me = me_ref[0]

    def tokens(offset):
        return cot_ref[0, :, lax.rem(me + offset, X)].reshape(Z * 16, 2 * PAD)

    cot = jnp.concatenate([tokens(0), tokens(X - 1), tokens(2), tokens(1)], axis=0)
    parts = (own_ref, left_ref, low_ref, high_ref, right_ref)
    act = jnp.concatenate([ref[...].reshape(-1, WIDTH) for ref in parts], axis=0)
    part = lax.dot_general(cot, act, (((0,), (0,)), ((), ())), preferred_element_type=jnp.float32)

    @pl.when(step == 0)
    def _():
        mine_ref[...] = part[:ROWS]
        theirs_ref[...] = part[PAD : PAD + ROWS]

    @pl.when(step > 0)
    def _():
        mine_ref[...] += part[:ROWS]
        theirs_ref[...] += part[PAD : PAD + ROWS]


def place_states(slot_ref, arrived_ref, a_ref, b_ref, c_ref, placed):
    placed[...] = jnp.zeros_like(placed)
    for entry in range(DP * PAIR):
        placed[slot_ref[entry]] = arrived_ref[entry]
    for index, ref in enumerate((a_ref, b_ref, c_ref)):
        ref[...] = placed[:CAP, :, WIDTH * index : WIDTH * (index + 1)].reshape(PAIR * CAP, WIDTH)


def finish(slot_ref, grad_ref, master_ref, moment1_ref, moment2_ref, a_ref, b_ref, c_ref, w_ref, placed):
    placed[...] = jnp.zeros_like(placed)
    for entry in range(DP * PAIR):
        placed[slot_ref[entry]] = grad_ref[entry]
    grad = placed[:CAP].reshape(PAIR * CAP, WIDTH)
    moment1 = beta_one * moment1_ref[...] + (1.0 - beta_one) * grad
    moment2 = beta_two * moment2_ref[...] + (1.0 - beta_two) * grad * grad
    update = learn_rate * (moment1 / fix_one) / (jnp.sqrt(moment2 / fix_two) + adam_eps)
    master = master_ref[...] - update
    a_ref[...] = master
    b_ref[...] = moment1
    c_ref[...] = moment2
    w_ref[...] = master.astype(jnp.bfloat16)


def f32(*shape):
    return jax.ShapeDtypeStruct(shape, jnp.float32)


def bf16(*shape):
    return jax.ShapeDtypeStruct(shape, jnp.bfloat16)


def shards(activations, cotangent, master, first_moment, second_moment, new_owner, new_slot):
    core = lax.axis_index("c").astype(jnp.int32).reshape(1)
    act_z = lax.all_gather(activations, "z", axis=0, tiled=True)
    right = [(i, (i + 1) % X) for i in range(X)]
    left = [(i, (i - 1) % X) for i in range(X)]
    half = act_z.shape[0] // 2
    from_left = lax.ppermute(act_z, "x", right)
    from_right = lax.ppermute(act_z, "x", left)
    far_low = lax.ppermute(from_left[:half], "x", right)
    far_high = lax.ppermute(from_right[half:], "x", left)

    packed = call(pack_cotangent, bf16(CHIPS, 16, 2 * PAD), [SMEM, VMEM], VMEM)(core, cotangent)
    shared = lax.all_to_all(packed, ("z", "x"), split_axis=0, concat_axis=0, tiled=True)
    cotangent_all = lax.all_gather(shared.reshape(CHIPS * 16, 2 * PAD), "y", axis=0)

    matching = new_owner[:, None] == new_owner[None, :]
    counter = jnp.arange(PIECES, dtype=jnp.int32)
    earlier = counter[None, :] < counter[:, None]
    rank_number = jnp.sum((matching & earlier).astype(jnp.int32), axis=1)
    position = new_owner * PAIR + rank_number
    hits = position[None, :] == jnp.arange(DP * PAIR, dtype=jnp.int32)[:, None]
    slots = jnp.sum(jnp.where(hits, new_slot[None, :] - CAP, 0), axis=1) + CAP
    dp_axes = ("z", "x", "c")
    slots = lax.all_to_all(slots.reshape(DP, 1, PAIR), dp_axes, split_axis=0, concat_axis=0, tiled=True)
    slots = slots.reshape(DP * PAIR)

    states = call(pack_states, f32(DP * PAIR, PAIR, 3 * WIDTH), [SMEM, VMEM, VMEM, VMEM], VMEM)(
        position, master, first_moment, second_moment
    )
    arrived = lax.all_to_all(states, dp_axes, split_axis=0, concat_axis=0, tiled=True)
    placed = call(place_states, (f32(PAIR * CAP, WIDTH),) * 3, [SMEM, VMEM], (VMEM,) * 3, scratch_shapes=[pltpu.VMEM((CAP + 1, PAIR, 3 * WIDTH), jnp.float32)])(
        slots, arrived
    )

    me = lax.axis_index("x").astype(jnp.int32).reshape(1)
    full = pl.BlockSpec((Z, 1, 16, WIDTH), lambda i: (0, i, 0, 0))
    some = pl.BlockSpec((Z // 2, 1, 16, WIDTH), lambda i: (0, i, 0, 0))
    mine, theirs = pl.pallas_call(
        partial_grad,
        grid=(Y,),
        out_shape=(f32(ROWS, WIDTH),) * 2,
        in_specs=[
            SMEM,
            pl.BlockSpec((1, Z, X, 16, 2 * PAD), lambda i: (i, 0, 0, 0, 0)),
            full,
            full,
            some,
            some,
            full,
            pl.BlockSpec(memory_space=pl.ANY),
        ],
        out_specs=[pl.BlockSpec((ROWS, WIDTH), lambda i: (0, 0))] * 2,
        compiler_params=pltpu.CompilerParams(vmem_limit_bytes=LIMIT),
    )(
        me,
        cotangent_all.reshape(Y, Z, X, 16, 2 * PAD),
        *[part.reshape(-1, Y, 16, WIDTH) for part in (act_z, from_left, far_low, far_high, from_right)],
        placed[0],
    )
    theirs = lax.ppermute(theirs, "c", [(0, 1), (1, 0)])
    grads = call(pack_grad, f32(DP * PAIR, PAIR, WIDTH), [SMEM, VMEM, VMEM], VMEM)(position, mine, theirs)
    grads = lax.all_to_all(grads, dp_axes, split_axis=0, concat_axis=0, tiled=True)
    new_master, new_moment1, new_moment2, weights = call(
        finish,
        (f32(PAIR * CAP, WIDTH),) * 3 + (bf16(PAIR * CAP, WIDTH),),
        [SMEM] + [VMEM] * 4,
        (VMEM,) * 4,
        scratch_shapes=[pltpu.VMEM((CAP + 1, PAIR, WIDTH), jnp.float32)],
    )(slots, grads, *placed)
    new_weights = lax.all_gather(weights, "y", axis=1, tiled=True)
    return (new_master, new_moment1, new_moment2, new_weights)


def solution(mesh):
    fine = Mesh(np.asarray(mesh.devices).reshape(Z, X, CORES, Y), ("z", "x", "c", "y"))
    dp = ("z", "x", "c")
    in_specs = (
        P(dp, "y"),
        P(dp + ("y",), None),
        P(dp, "y"),
        P(dp, "y"),
        P(dp, "y"),
        P(dp),
        P(dp),
    )
    out_specs = (P(dp, "y"), P(dp, "y"), P(dp, "y"), P(dp, None))
    return jax.shard_map(shards, mesh=fine, in_specs=in_specs, out_specs=out_specs, check_vma=False)
```

time: 408 us -> 226 us (0.55)
  the two profiles are of different devices: /device:TPU:1 before, /device:TPU:8 now
where the time goes in v1:
time: 226 us; the launch traced here: 225 us
  waiting for transfers between devices  90.5 us (40%)
  blocking collectives  62.5 us (28%)
  starting transfers between devices  25.8 us (11%)
  Pallas kernels  21.5 us (10%)
  between operations  13.9 us (6%)
  local copies, waits for them, and re-layouts  9.61 us (4%)
    all_gather x1, waiting for transfers between devices, shards(): new_weights = lax.all_gather(weights, 'y', axis=1, tiled=True)  39.9 us
    ppermute x1, waiting for transfers between devices, shards(): from_left = lax.ppermute(act_z, 'x', right)  36 us
    all_to_all x1, blocking collectives, shards(): lax.all_to_all(packed, ('z', 'x'), split_axis=0, concat_axis=0, tiled=True)  33.7 us
    all_to_all x1, blocking collectives, shards(): lax.all_to_all(grads, dp_axes, split_axis=0, concat_axis=0, tiled=True)  28.8 us
    pallas_call x1, Pallas kernels, shards(): pl.pallas_call(partial_grad, grid=(Y,), out_shape=(f32(ROWS, WIDTH),) * 2...  8.77 us
    all_to_all x1, waiting for transfers between devices, shards(): lax.all_to_all(slots.reshape(DP, 1, PAIR), dp_axes, split_axis=0, concat_...  6.8 us
    unnamed x17, local copies, waits for them, and re-layouts  5.87 us
    ppermute x1, starting transfers between devices, shards(): far_high = lax.ppermute(from_right[half:], 'x', left)  5.12 us
  transfers between devices with their start and end apart: 10, of which 6 were waited for; matrix products, arithmetic and copies ran while one was open for 2% of the time, Pallas kernels for 3%

profile of v1, /device:TPU:8, one launch (start us, length us, event | category | flops | bytes accessed | tf_op | source)
XLA Modules:
  0.0 224.9 jit_solution(3616144653279452099)
XLA Ops:
  7.2 0.0 copy-start.6
  7.2 0.0 copy-start.7
  7.2 0.0 all-gather.6.cloned.1.call-start
  7.2 0.7 all-gather.6.cloned.1.call-update
  7.9 0.0 all-gather.4.cloned.1.call-start
  8.0 2.0 shard_map.102
  10.0 33.7 %all_to_all.20 = bf16[32,16,512]{2,1,0:T(8,128)(2,1)} all-to-all(bf16[32,16,512]{2,1,0:T(8,128)(2,1)} %shard_map.102), channel_id=1, replica_groups=mesh['z'=8,'x'=4,'c'=2,'y'=8] {'z','x'}, dimensions={0} | all-to-all | bytes 1048576 | tf_op jit(solution)/shard_map/all_to_all | solution.py:153
  43.7 0.0 all-gather.4.cloned.1.call-update
  43.7 0.0 copy-done.6
  43.7 0.2 convert_reduce_fusion
  43.9 0.0 copy-done.7
  43.9 0.0 copy-start.5
  43.9 0.1 select_reduce_fusion
  44.1 0.8 add.24
  44.8 5.1 %all-to-all-start = ((s32[64,1,2]{2,1,0:T(1,128)}), s32[64,1,2]{2,1,0:T(1,128)S(1)}, u32[]{:S(2)}, u32[]{:S(2)}) async-start(s32[64,1,2]{2,1,0:T(1,128)} %bitcast), calls=%async_computation | async-start | bytes 65536 | tf_op jit(solution)/shard_map/all_to_all | solution.py:164
  49.9 0.0 copy-done.5
  49.9 2.8 %shard_map.103 = f32[128,2,1536]{2,1,0:T(2,128)} custom-call(s32[112]{0:T(128)} %copy-done.5, f32[224,512]{1,0:T(8,128)} %a_ref.1, f32[224,512]{1,0:T(8,128)} %b_ref.1, f32[224,512]{1,0:T(8,128)} %c_ref.1), custom_call_target="tpu_custom_call" | custom-call | tf_op jit(solution)/shard_map/pallas_call | solution.py:167
  52.7 6.8 %all-to-all-done = s32[64,1,2]{2,1,0:T(1,128)S(1)} async-done(((s32[64,1,2]{2,1,0:T(1,128)}), s32[64,1,2]{2,1,0:T(1,128)S(1)}, u32[]{:S(2)}, u32[]{:S(2)}) %all-to-all-start) | async-done | bytes 544 | tf_op jit(solution)/shard_map/all_to_all | solution.py:164
  59.5 4.7 %all-to-all-start.2 = ((f32[128,2,1536]{2,1,0:T(2,128)}), f32[128,2,1536]{2,1,0:T(2,128)S(1)}, u32[]{:S(2)}, u32[]{:S(2)}) async-start(f32[128,2,1536]{2,1,0:T(2,128)} %shard_map.103), calls=%async_computation.2 | async-start | bytes 3145728 | tf_op jit(solution)/shard_map/all_to_all | solution.py:170
  64.2 0.0 all-gather.8.cloned.1.call-start
  64.2 0.0 all-gather.6.cloned.1.call-done
  64.2 3.4 %collective-permute-start = (bf16[1024,512]{1,0:T(8,128)(2,1)}, bf16[1024,512]{1,0:T(8,128)(2,1)S(1)}, u32[]{:S(2)}, u32[]{:S(2)}) collective-permute-start(bf16[1024,512]{1,0:T(8,128)(2,1)} %all-gather.6.cloned.1.call-done), channel_id=1, source_target_pairs={{0,16},{16,32},{32,48},{48,0},{1,17},{17,33},{33,49},{49,1},{2,18}... | collective-permute-start | bytes 3145736 | tf_op jit(solution)/shard_map/ppermute | solution.py:147
  67.6 3.7 %collective-permute-start.2 = (bf16[1024,512]{1,0:T(8,128)(2,1)}, bf16[1024,512]{1,0:T(8,128)(2,1)S(1)}, u32[]{:S(2)}, u32[]{:S(2)}) collective-permute-start(bf16[1024,512]{1,0:T(8,128)(2,1)} %all-gather.6.cloned.1.call-done), channel_id=1, source_target_pairs={{0,48},{16,0},{32,16},{48,32},{1,49},{17,1},{33,17},{49,33},{2,50}... | collective-permute-start | bytes 3145736 | tf_op jit(solution)/shard_map/ppermute | solution.py:148
  71.3 36.0 %collective-permute-done = bf16[1024,512]{1,0:T(8,128)(2,1)S(1)} collective-permute-done((bf16[1024,512]{1,0:T(8,128)(2,1)}, bf16[1024,512]{1,0:T(8,128)(2,1)S(1)}, u32[]{:S(2)}, u32[]{:S(2)}) %collective-permute-start) | collective-permute-done | bytes 1048608 | tf_op jit(solution)/shard_map/ppermute | solution.py:147
  107.3 0.0 copy-start.1
  107.3 0.9 slice.8
  108.2 1.9 collective-permute-start.1
  110.2 0.0 collective-permute-done.2
  110.2 0.0 copy-start.2
  110.2 1.0 copy-done.2
  111.2 0.9 slice.9
  112.0 5.1 %collective-permute-start.3 = (bf16[512,512]{1,0:T(8,128)(2,1)}, bf16[512,512]{1,0:T(8,128)(2,1)}, u32[]{:S(2)}, u32[]{:S(2)}) collective-permute-start(bf16[512,512]{1,0:T(8,128)(2,1)} %slice.9), channel_id=1, source_target_pairs={{0,48},{16,0},{32,16},{48,32},{1,49},{17,1},{33,17},{49,33},{2,50}... | collective-permute-start | bytes 1572872 | tf_op jit(solution)/shard_map/ppermute | solution.py:150
  117.1 0.5 broadcast.22
  117.7 0.7 reduce.3
  118.4 0.7 reshape.53.slot_ref
  119.1 0.0 all-to-all-done.2.arrived_ref
  119.1 0.0 copy-start
  119.1 1.1 copy-done
  120.2 2.8 %shard_map.104 = (f32[228,512]{1,0:T(8,128)}, f32[228,512]{1,0:T(8,128)}, f32[228,512]{1,0:T(8,128)}) custom-call(s32[128]{0:T(128)} %reshape.53.slot_ref, f32[128,2,1536]{2,1,0:T(2,128)} %copy-done), custom_call_target="tpu_custom_call" | custom-call | tf_op jit(solution)/shard_map/pallas_call | solution.py:171
  123.0 1.9 collective-permute-done.1
  124.9 0.0 copy-start.3
  124.9 3.1 %collective-permute-done.3 = bf16[512,512]{1,0:T(8,128)(2,1)} collective-permute-done((bf16[512,512]{1,0:T(8,128)(2,1)}, bf16[512,512]{1,0:T(8,128)(2,1)}, u32[]{:S(2)}, u32[]{:S(2)}) %collective-permute-start.3) | collective-permute-done | bytes 524320 | tf_op jit(solution)/shard_map/ppermute | solution.py:150
  128.0 0.0 all-gather.4.cloned.1.call-done
  128.0 0.0 copy-done.1
  128.0 0.0 copy-done.3
  128.0 8.8 %shard_map.105 = (f32[224,512]{1,0:T(8,128)}, f32[224,512]{1,0:T(8,128)}) custom-call(s32[1]{0:T(128)} %bitcast.1.me_ref, bf16[8,8,4,16,512]{4,3,2,1,0:T(8,128)(2,1)} %bitcast.10, bf16[8,8,16,512]{3,2,1,0:T(8,128)(2,1)} %bitcast.14, bf16[8,8,16,512]{3,2,1,0:T(8,128)(2,1)} %bitcast.11, bf16[4,8,16,512]{3,2,1,0:T(8,128)(2,1)} %bitcast.15, ...), custom_call_target="tpu_custom_call" | custom-call | tf_op jit(solution)/shard_map/pallas_call | solution.py:178
  136.8 1.9 collective-permute-start.4
  138.7 2.0 collective-permute-done.4.theirs_ref
  140.7 0.0 copy-start.4
  140.7 0.8 copy-done.4
  141.5 2.2 shard_map.106
  143.6 28.8 %all_to_all.21.grad_ref = f32[128,2,512]{2,1,0:T(2,128)} all-to-all(f32[128,2,512]{2,1,0:T(2,128)} %shard_map.106), channel_id=1, replica_groups=mesh['z'=8,'x'=4,'c'=2,'y'=8] {'z','x','c'}, dimensions={0} | all-to-all | bytes 1048576 | tf_op jit(solution)/shard_map/all_to_all | solution.py:202
  172.4 3.0 %shard_map.107 = (f32[228,512]{1,0:T(8,128)}, f32[228,512]{1,0:T(8,128)}, f32[228,512]{1,0:T(8,128)}, bf16[228,512]{1,0:T(8,128)(2,1)}) custom-call(s32[128]{0:T(128)} %reshape.53.slot_ref, f32[128,2,512]{2,1,0:T(2,128)} %all_to_all.21.grad_ref, f32[228,512]{1,0:T(8,128)} %get-tuple-element.13.after_ref.master_ref, ...), custom_call_target="tpu_custom_call" | custom-call | tf_op jit(solution)/shard_map/pallas_call | solution.py:203
  175.4 0.0 all-gather.8.cloned.1.call-update
  175.4 39.9 %all-gather.8.cloned.1.call-done = bf16[228,4096]{1,0:T(8,128)(2,1)} async-done(((bf16[228,512]{1,0:T(8,128)(2,1)}), bf16[228,4096]{1,0:T(8,128)(2,1)}) %all-gather.8.cloned.1.call-update) | async-done | bytes 1867792 | tf_op jit(solution)/shard_map/all_gather | solution.py:210
  215.4 3.0 %copy.14 = bf16[228,4096]{1,0:T(8,128)(2,1)} copy(bf16[228,4096]{1,0:T(8,128)(2,1)} %all-gather.8.cloned.1.call-done) | data formatting | bytes 3735552
  (2 shorter events, 0.0 us)
Async XLA Ops:
  7.2 36.6 %copy-start.6 = (s32[112]{0:T(128)S(1)}, s32[112]{0:T(128)}, u32[]{:S(2)}) copy-start(s32[112]{0:T(128)} %param.12) | copy-start | bytes 1348
  7.2 36.7 %copy-start.7 = (s32[112]{0:T(128)S(1)}, s32[112]{0:T(128)}, u32[]{:S(2)}) copy-start(s32[112]{0:T(128)} %param.13) | copy-start | bytes 1348
  7.2 57.0 %all-gather.6.cloned.1.call-start = ((), (), s32[]{:S(2)}) async-start(), calls=%async_computation.5 | async-start | bytes 1179648 | tf_op jit(solution)/shard_map/all_gather | solution.py:143
  7.9 120.1 %all-gather.4.cloned.1.call-start = ((), (), s32[]{:S(2)}) async-start(), calls=%async_computation.4 | async-start | bytes 4718592 | tf_op jit(solution)/shard_map/all_gather | solution.py:154
  43.9 6.0 %copy-start.5 = (s32[112]{0:T(128)}, s32[112]{0:T(128)S(1)}, u32[]{:S(2)}) copy-start(s32[112]{0:T(128)S(1)} %get-tuple-element.22.position_ref) | copy-start | bytes 1348
  44.8 14.7 %all-to-all-start = ((s32[64,1,2]{2,1,0:T(1,128)}), s32[64,1,2]{2,1,0:T(1,128)S(1)}, u32[]{:S(2)}, u32[]{:S(2)}) async-start(s32[64,1,2]{2,1,0:T(1,128)} %bitcast), calls=%async_computation | async-start | bytes 65536 | tf_op jit(solution)/shard_map/all_to_all | solution.py:164
  59.5 59.6 %all-to-all-start.2 = ((f32[128,2,1536]{2,1,0:T(2,128)}), f32[128,2,1536]{2,1,0:T(2,128)S(1)}, u32[]{:S(2)}, u32[]{:S(2)}) async-start(f32[128,2,1536]{2,1,0:T(2,128)} %shard_map.103), calls=%async_computation.2 | async-start | bytes 3145728 | tf_op jit(solution)/shard_map/all_to_all | solution.py:170
  64.2 151.2 %all-gather.8.cloned.1.call-start = ((), (), s32[]{:S(2)}) async-start(), calls=%async_computation.6 | async-start | bytes 2138112 | tf_op jit(solution)/shard_map/all_gather | solution.py:210
  64.2 43.1 %collective-permute-start = (bf16[1024,512]{1,0:T(8,128)(2,1)}, bf16[1024,512]{1,0:T(8,128)(2,1)S(1)}, u32[]{:S(2)}, u32[]{:S(2)}) collective-permute-start(bf16[1024,512]{1,0:T(8,128)(2,1)} %all-gather.6.cloned.1.call-done), channel_id=1, source_target_pairs={{0,16},{16,32},{32,48},{48,0},{1,17},{17,33},{33,49},{49,1},{2,18}... | collective-permute-start | bytes 3145736 | tf_op jit(solution)/shard_map/ppermute | solution.py:147
  67.6 42.6 %collective-permute-start.2 = (bf16[1024,512]{1,0:T(8,128)(2,1)}, bf16[1024,512]{1,0:T(8,128)(2,1)S(1)}, u32[]{:S(2)}, u32[]{:S(2)}) collective-permute-start(bf16[1024,512]{1,0:T(8,128)(2,1)} %all-gather.6.cloned.1.call-done), channel_id=1, source_target_pairs={{0,48},{16,0},{32,16},{48,32},{1,49},{17,1},{33,17},{49,33},{2,50}... | collective-permute-start | bytes 3145736 | tf_op jit(solution)/shard_map/ppermute | solution.py:148
  107.3 20.7 %copy-start.1 = (bf16[1024,512]{1,0:T(8,128)(2,1)}, bf16[1024,512]{1,0:T(8,128)(2,1)S(1)}, u32[]{:S(2)}) copy-start(bf16[1024,512]{1,0:T(8,128)(2,1)S(1)} %collective-permute-done) | copy-start | bytes 3145732
  108.2 16.6 %collective-permute-start.1 = (bf16[512,512]{1,0:T(8,128)(2,1)}, bf16[512,512]{1,0:T(8,128)(2,1)S(1)}, u32[]{:S(2)}, u32[]{:S(2)}) collective-permute-start(bf16[512,512]{1,0:T(8,128)(2,1)} %slice.8), channel_id=1, source_target_pairs={{0,16},{16,32},{32,48},{48,0},{1,17},{17,33},{33,49},{49,1},{2,18}... | collective-permute-start | bytes 1572872 | tf_op jit(solution)/shard_map/ppermute | solution.py:149
  110.2 1.0 copy-start.2
  112.0 16.0 %collective-permute-start.3 = (bf16[512,512]{1,0:T(8,128)(2,1)}, bf16[512,512]{1,0:T(8,128)(2,1)}, u32[]{:S(2)}, u32[]{:S(2)}) collective-permute-start(bf16[512,512]{1,0:T(8,128)(2,1)} %slice.9), channel_id=1, source_target_pairs={{0,48},{16,0},{32,16},{48,32},{1,49},{17,1},{33,17},{49,33},{2,50}... | collective-permute-start | bytes 1572872 | tf_op jit(solution)/shard_map/ppermute | solution.py:150
  119.1 1.1 copy-start
  124.9 3.1 %copy-start.3 = (bf16[512,512]{1,0:T(8,128)(2,1)}, bf16[512,512]{1,0:T(8,128)(2,1)S(1)}, u32[]{:S(2)}) copy-start(bf16[512,512]{1,0:T(8,128)(2,1)S(1)} %collective-permute-done.1) | copy-start | bytes 1572868
  136.8 3.9 %collective-permute-start.4 = (f32[224,512]{1,0:T(8,128)}, f32[224,512]{1,0:T(8,128)S(1)}, u32[]{:S(2)}, u32[]{:S(2)}) collective-permute-start(f32[224,512]{1,0:T(8,128)} %get-tuple-element.15), channel_id=1, source_target_pairs={{0,8},{8,0},{1,9},{9,1},{2,10},{10,2},{3,11},{11,3},{4,12},{12,4},... | collective-permute-start | bytes 1376264 | tf_op jit(solution)/shard_map/ppermute | solution.py:200
  140.7 0.8 copy-start.4
Sparse Core Ops, SparseCore 0:
  10.1 48.7 all-gather.5
  61.0 54.0 all-gather.3
  175.5 39.7 all-gather.7

commit v2 on v1

v2 whole, which is shorter than its diff:
```python
import jax
import jax.numpy as jnp
import numpy as np
from jax import lax
from jax.experimental import pallas as pl
from jax.experimental.pallas import tpu as pltpu
from jax.sharding import Mesh, PartitionSpec as P

beta_one = 0.9
beta_two = 0.95
learn_rate = 0.1
adam_eps = 1e-08
adam_step = 1000
fix_one = 1.0 - beta_one**adam_step
fix_two = 1.0 - beta_two**adam_step

Z, X, CORES, Y = 8, 4, 2, 8
CHIPS = Z * X
DP = CHIPS * CORES
ROWS = 224
PAD = 256
PIECES = 112
PAIR = 2
CAP = 114
WIDTH = 512
LANES = 128
SCALES = (1024.0, 64.0, 0.0625)

VMEM = pl.BlockSpec(memory_space=pltpu.VMEM)
SMEM = pl.BlockSpec(memory_space=pltpu.SMEM)
ANY = pl.BlockSpec(memory_space=pl.ANY)
LIMIT = 16 * 1024 * 1024


def call(kernel, out_shape, in_specs, out_specs, flops=0, **kw):
    return pl.pallas_call(
        kernel,
        out_shape=out_shape,
        in_specs=in_specs,
        out_specs=out_specs,
        cost_estimate=pl.CostEstimate(flops=flops, bytes_accessed=4 << 20, transcendentals=0),
        compiler_params=pltpu.CompilerParams(vmem_limit_bytes=LIMIT),
        **kw,
    )


def pack_cotangent(core_ref, cot_ref, out_ref):
    blank = jnp.zeros((cot_ref.shape[0], PAD - ROWS), jnp.bfloat16)

    def fill(flip):
        for device in range(DP):
            start = ROWS * device
            block = jnp.concatenate([cot_ref[:, start : start + ROWS], blank], axis=1)
            place = PAD * ((device % CORES) ^ flip)
            out_ref[device // CORES, :, place : place + PAD] = block

    @pl.when(core_ref[0] == 0)
    def _():
        fill(0)

    @pl.when(core_ref[0] == 1)
    def _():
        fill(1)


def plan(owner_ref, slot_ref, position_ref, entry_slot_ref):
    shape = (LANES, LANES)

    def padded(ref):
        return jnp.concatenate([ref[...], jnp.full((1, LANES - PIECES), -1, jnp.int32)], axis=1)

    def column(row):
        return jnp.broadcast_to(row.astype(jnp.float32), shape).T.astype(jnp.int32)

    owner = padded(owner_ref)
    first, second = (lax.broadcasted_iota(jnp.int32, shape, dim) for dim in (0, 1))
    same = jnp.where((column(owner) == owner) & (first < second), 1, 0)
    rank = jnp.sum(same, axis=0, keepdims=True)
    lane = lax.broadcasted_iota(jnp.int32, (1, LANES), 1)
    position = jnp.where(lane < PIECES, owner * PAIR + rank, -1)
    position_ref[...] = position
    found = jnp.where(column(position) == second, column(padded(slot_ref)) - CAP, 0)
    entry_slot_ref[...] = jnp.sum(found, axis=0, keepdims=True) + CAP


def add_blocks(total, scratch, me_ref, parts, blocks):
    cot_buf, act_buf, cot_sem, act_sem = scratch
    me, x = me_ref[0], me_ref[1]
    half = Z // 2
    places = [(0, Z, 0), (0, Z, X - 1), (0, Z, 1), (0, half, 2), (half, half, 2)]
    plans, number = [], 0
    for block, (step, refs) in enumerate(blocks):
        index = lax.rem(me + (Y + step), Y)
        copies, start = [], 0
        for part, (low, count, offset) in enumerate(places):
            target = act_buf.at[block, pl.ds(low, count), lax.rem(x + offset, X)]
            copies.append(pltpu.make_async_copy(parts[part].at[:, index], target, act_sem.at[block, part]))
        for ref in refs:
            target = cot_buf.at[block, pl.ds(start, ref.shape[0])]
            copies.append(pltpu.make_async_copy(ref, target, cot_sem.at[number]))
            start, number = start + ref.shape[0], number + 1
        plans.append(copies)
    for copies in plans:
        for copy in copies:
            copy.start()
    for block, copies in enumerate(plans):
        for copy in copies:
            copy.wait()
        act = act_buf[block].reshape(CHIPS * 16, WIDTH)
        part = lax.dot_general(
            cot_buf[block], act, (((0,), (0,)), ((), ())), preferred_element_type=jnp.float32
        )
        total = part if total is None else total + part
    return total


def first_blocks(me_ref, a0, a1, a2, a3, a4, own, down1, up1, down2, up2, after_ref, out_ref, *scratch):
    blocks = [(0, [own]), (-1, [down1]), (1, [up1]), (-2, [down2]), (2, [up2])]
    out_ref[...] = add_blocks(None, scratch, me_ref, (a0, a1, a2, a3, a4), blocks)


def last_blocks(me_ref, a0, a1, a2, a3, a4, before_ref, down3, up3, upper, lower, mine_ref, theirs_ref, *scratch):
    blocks = [(-3, [down3]), (3, [up3]), (4, [upper, lower])]
    total = add_blocks(before_ref[...], scratch, me_ref, (a0, a1, a2, a3, a4), blocks)
    mine_ref[...] = total[:ROWS]
    theirs_ref[...] = total[PAD : PAD + ROWS]


def block_scratch(blocks, copies):
    return [
        pltpu.VMEM((blocks, CHIPS * 16, 2 * PAD), jnp.bfloat16),
        pltpu.VMEM((blocks, Z, X, 16, WIDTH), jnp.bfloat16),
        pltpu.SemaphoreType.DMA((copies,)),
        pltpu.SemaphoreType.DMA((blocks, 5)),
    ]


def update_state(mine_ref, theirs_ref, master_ref, moment1_ref, moment2_ref):
    grad = mine_ref[...] + theirs_ref[...]
    moment1 = beta_one * moment1_ref[...] + (1.0 - beta_one) * grad
    moment2 = beta_two * moment2_ref[...] + (1.0 - beta_two) * grad * grad
    update = learn_rate * (moment1 / fix_one) / (jnp.sqrt(moment2 / fix_two) + adam_eps)
    return master_ref[...] - update, moment1, moment2


def step_weights(position_ref, mine_ref, theirs_ref, master_ref, moment1_ref, moment2_ref, out_ref, master):
    master[...] = update_state(mine_ref, theirs_ref, master_ref, moment1_ref, moment2_ref)[0]
    out_ref[...] = jnp.zeros_like(out_ref)
    for piece in range(PIECES):
        rows = master[PAIR * piece : PAIR * piece + PAIR, :]
        out_ref[position_ref[0, piece]] = rows.astype(jnp.bfloat16)


def step_states(position_ref, mine_ref, theirs_ref, master_ref, moment1_ref, moment2_ref, out_ref, state):
    fields = update_state(mine_ref, theirs_ref, master_ref, moment1_ref, moment2_ref)
    for index, field in enumerate(fields):
        state[index] = field * SCALES[index]
    out_ref[...] = jnp.zeros_like(out_ref)
    for piece in range(PIECES):
        place = position_ref[0, piece]
        for index in range(3):
            rows = state[index, PAIR * piece : PAIR * piece + PAIR, :]
            out_ref[place, :, WIDTH * index : WIDTH * (index + 1)] = rows


def place_states(slot_ref, arrived_ref, a_ref, b_ref, c_ref, placed):
    placed[...] = jnp.zeros_like(placed)
    for entry in range(DP * PAIR):
        placed[slot_ref[entry]] = arrived_ref[entry]
    for index, ref in enumerate((a_ref, b_ref, c_ref)):
        rows = placed[:CAP, :, WIDTH * index : WIDTH * (index + 1)].reshape(PAIR * CAP, WIDTH)
        ref[...] = rows * (1.0 / SCALES[index])


def place_weights(slot_ref, arrived_ref, out_ref, placed):
    placed[...] = jnp.zeros_like(placed)
    for entry in range(DP * PAIR):
        placed[slot_ref[entry]] = arrived_ref[entry].astype(jnp.float32)
    out_ref[...] = placed[:CAP].reshape(PAIR * CAP, WIDTH).astype(jnp.bfloat16)


def hold(value_ref, after_ref, out_ref):
    del value_ref, after_ref, out_ref


def f32(*shape):
    return jax.ShapeDtypeStruct(shape, jnp.float32)


def int32(*shape):
    return jax.ShapeDtypeStruct(shape, jnp.int32)


def bf16(*shape):
    return jax.ShapeDtypeStruct(shape, jnp.bfloat16)


def shards(activations, cotangent, master, first_moment, second_moment, new_owner, new_slot):
    dp_axes = ("z", "x", "c")
    core = lax.axis_index("c").astype(jnp.int32).reshape(1)
    packed = call(pack_cotangent, bf16(CHIPS, 16, 2 * PAD), [SMEM, VMEM], VMEM)(core, cotangent)
    shared = lax.all_to_all(packed, ("z", "x"), split_axis=0, concat_axis=0, tiled=True)
    shared = shared.reshape(CHIPS * 16, 2 * PAD)

    act = lax.all_gather(activations, "z", axis=0, tiled=True)
    right = [(i, (i + 1) % X) for i in range(X)]
    left = [(i, (i - 1) % X) for i in range(X)]
    half = act.shape[0] // 2
    acts = [act, lax.ppermute(act, "x", right), lax.ppermute(act, "x", left)]
    acts += [lax.ppermute(acts[1][:half], "x", right), lax.ppermute(acts[2][half:], "x", left)]
    acts = [part.reshape(-1, Y, 16, WIDTH) for part in acts]

    right = [(i, (i + 1) % Y) for i in range(Y)]
    left = [(i, (i - 1) % Y) for i in range(Y)]
    down, up = [shared], [shared]
    for _ in range(Y // 2 - 1):
        down.append(lax.ppermute(down[-1], "y", right))
        up.append(lax.ppermute(up[-1], "y", left))
    far = [lax.ppermute(down[-1][:PAD], "y", right), lax.ppermute(up[-1][PAD:], "y", left)]

    position, slots = call(plan, (int32(1, LANES),) * 2, [VMEM] * 2, (VMEM,) * 2)(
        new_owner.reshape(1, PIECES), new_slot.reshape(1, PIECES)
    )
    slots = lax.all_to_all(slots.reshape(DP, 1, PAIR), dp_axes, split_axis=0, concat_axis=0, tiled=True)
    slots = slots.reshape(DP * PAIR)

    me = jnp.stack([lax.axis_index("y"), lax.axis_index("x")]).astype(jnp.int32)
    partial = call(
        first_blocks,
        f32(2 * PAD, WIDTH),
        [SMEM] + [ANY] * 11,
        VMEM,
        flops=5 << 29,
        scratch_shapes=block_scratch(5, 5),
    )(me, *acts, shared, down[1], up[1], down[2], up[2], slots)
    mine, theirs = call(
        last_blocks,
        (f32(ROWS, WIDTH),) * 2,
        [SMEM] + [ANY] * 5 + [VMEM] + [ANY] * 4,
        (VMEM,) * 2,
        flops=3 << 29,
        scratch_shapes=block_scratch(3, 4),
    )(me, *acts, partial, down[3], up[3], *far)
    theirs = lax.ppermute(theirs, "c", [(0, 1), (1, 0)])
    step = (position, mine, theirs, master, first_moment, second_moment)
    weights = call(
        step_weights,
        bf16(DP * PAIR, PAIR, WIDTH),
        [SMEM] + [VMEM] * 5,
        VMEM,
        scratch_shapes=[pltpu.VMEM((ROWS, WIDTH), jnp.float32)],
    )(*step)

    weights = lax.all_to_all(weights, dp_axes, split_axis=0, concat_axis=0, tiled=True)
    weights = call(
        place_weights,
        bf16(PAIR * CAP, WIDTH),
        [SMEM, VMEM],
        VMEM,
        scratch_shapes=[pltpu.VMEM((CAP + 1, PAIR, WIDTH), jnp.float32)],
    )(slots, weights)
    new_weights = lax.all_gather(weights, "y", axis=1, tiled=True)

    states = call(
        step_states,
        f32(DP * PAIR, PAIR, 3 * WIDTH),
        [SMEM] + [VMEM] * 5,
        VMEM,
        flops=1 << 31,
        scratch_shapes=[pltpu.VMEM((3, ROWS, WIDTH), jnp.float32)],
    )(*step)
    states = call(hold, f32(*states.shape), [ANY, ANY], ANY, input_output_aliases={0: 0})(states, weights)
    states = states.astype(jnp.float16)
    arrived = lax.all_to_all(states, dp_axes, split_axis=0, concat_axis=0, tiled=True)
    placed = call(
        place_states,
        (f32(PAIR * CAP, WIDTH),) * 3,
        [SMEM, VMEM],
        (VMEM,) * 3,
        scratch_shapes=[pltpu.VMEM((CAP + 1, PAIR, 3 * WIDTH), jnp.float32)],
    )(slots, arrived.astype(jnp.float32))
    return (*placed, new_weights)


def solution(mesh):
    fine = Mesh(np.asarray(mesh.devices).reshape(Z, X, CORES, Y), ("z", "x", "c", "y"))
    dp = ("z", "x", "c")
    in_specs = (
        P(dp, "y"),
        P(dp + ("y",), None),
        P(dp, "y"),
        P(dp, "y"),
        P(dp, "y"),
        P(dp),
        P(dp),
    )
    out_specs = (P(dp, "y"), P(dp, "y"), P(dp, "y"), P(dp, None))
    return jax.shard_map(shards, mesh=fine, in_specs=in_specs, out_specs=out_specs, check_vma=False)
```

time: 226 us -> 202 us (0.89)
  waiting for transfers between devices: 90.5 us -> 26.7 us
  blocking collectives: 62.5 us -> 83.3 us
  starting transfers between devices: 25.8 us -> 46.2 us
  Pallas kernels: 21.5 us -> 13.2 us
  local copies, waits for them, and re-layouts: 9.61 us -> 14.6 us
    ppermute x4 -> x12, waiting for transfers between devices: 41 us -> 6.24 us  [the longest x3 5.46 us: shards(): down.append(lax.ppermute(down[-1], 'y', right))]
    all_gather x1, waiting for transfers between devices: 39.9 us -> 7.48 us  [shards(): new_weights = lax.all_gather(weights, 'y', axis=1, tiled=True)]
    ppermute x4 -> x12, starting transfers between devices: 14.1 us -> 38.6 us  [the longest x3 10.3 us: shards(): down.append(lax.ppermute(down[-1], 'y', right))]
    all_to_all x1 -> x2, blocking collectives: 28.8 us -> 50.6 us  [the longest x1 28 us: shards(): lax.all_to_all(states, dp_axes, split_axis=0, concat_axis=0, tiled=True)]
    all_gather x2 -> x1, waiting for transfers between devices: 0.02 us -> 9.66 us  [shards(): act = lax.all_gather(activations, 'z', axis=0, tiled=True)]
    all_to_all x1, waiting for transfers between devices: 6.8 us -> 0.84 us  [shards(): lax.all_to_all(slots.reshape(DP, 1, PAIR), dp_axes, split_axis=0, concat_...]
    pallas_call x4 -> x7, Pallas kernels: 16.7 us -> 11.1 us  [the longest x1 3.71 us: shards(): call(first_blocks, f32(2 * PAD, WIDTH), [SMEM] + [ANY] * 11, VMEM, flops=...]
    all_to_all x1 -> x0, starting transfers between devices: 4.68 us -> none  [shards(): lax.all_to_all(states, dp_axes, split_axis=0, concat_axis=0, tiled=True)]
  transfers between devices with their start and end apart: 10 -> 16, of which waited for: 6 -> 6; matrix products, arithmetic and copies ran while one was open for 2% -> 4% of each run, Pallas kernels for 3% -> 4%
where the time goes in v2:
time: 202 us; the launch traced here: 201 us
  blocking collectives  83.3 us (41%)
  starting transfers between devices  46.2 us (23%)
  waiting for transfers between devices  26.7 us (13%)
  local copies, waits for them, and re-layouts  14.6 us (7%)
  between operations  14.5 us (7%)
  Pallas kernels  13.2 us (7%)
  other arithmetic  2.64 us (1%)
    all_to_all x1, blocking collectives, shards(): lax.all_to_all(packed, ('z', 'x'), split_axis=0, concat_axis=0, tiled=True)  32.6 us
    all_to_all x1, blocking collectives, shards(): lax.all_to_all(states, dp_axes, split_axis=0, concat_axis=0, tiled=True)  28 us
    all_to_all x1, blocking collectives, shards(): lax.all_to_all(weights, dp_axes, split_axis=0, concat_axis=0, tiled=True)  22.7 us
    ppermute x3, starting transfers between devices, shards(): down.append(lax.ppermute(down[-1], 'y', right))  10.3 us
    unnamed x33, local copies, waits for them, and re-layouts  9.95 us
    all_gather x1, waiting for transfers between devices, shards(): act = lax.all_gather(activations, 'z', axis=0, tiled=True)  9.66 us
    all_gather x1, waiting for transfers between devices, shards(): new_weights = lax.all_gather(weights, 'y', axis=1, tiled=True)  7.48 us
    ppermute x3, starting transfers between devices, shards(): up.append(lax.ppermute(up[-1], 'y', left))  7.17 us
  transfers between devices with their start and end apart: 16, of which 6 were waited for; matrix products, arithmetic and copies ran while one was open for 4% of the time, Pallas kernels for 4%

profile of v2, /device:TPU:8, one launch (start us, length us, event | category | flops | bytes accessed | tf_op | source)
XLA Modules:
  0.0 201.0 jit_solution(1096933494584077607)
XLA Ops:
  7.2 0.0 all-gather.3.cloned.1.call-start
  7.2 0.7 all-gather.3.cloned.1.call-update
  7.9 1.0 copy-done.3
  8.9 0.2 shard_map.103
  9.1 0.0 copy-start.14
  9.2 0.0 copy-start.15
  9.2 32.6 %all_to_all.20 = bf16[32,16,512]{2,1,0:T(8,128)(2,1)S(1)} all-to-all(bf16[32,16,512]{2,1,0:T(8,128)(2,1)S(1)} %shard_map.103), channel_id=1, replica_groups=mesh['z'=8,'x'=4,'c'=2,'y'=8] {'z','x'}, dimensions={0} | all-to-all | bytes 1048576 | tf_op jit(solution)/shard_map/all_to_all | solution.py:202
  41.8 3.5 %collective-permute-start.4 = (bf16[512,512]{1,0:T(8,128)(2,1)S(1)}, bf16[512,512]{1,0:T(8,128)(2,1)S(1)}, u32[]{:S(2)}, u32[]{:S(2)}) collective-permute-start(bf16[512,512]{1,0:T(8,128)(2,1)S(1)} %bitcast.18), channel_id=1, source_target_pairs={{0,1},{1,2},{2,3},{3,4},{4,5},{5,6},{6,7},{7,0},{8,9},{9,10},{10,1... | collective-permute-start | bytes 1572872 | tf_op jit(solution)/shard_map/ppermute | solution.py:217
  45.3 2.3 %collective-permute-start.5 = (bf16[512,512]{1,0:T(8,128)(2,1)S(1)}, bf16[512,512]{1,0:T(8,128)(2,1)}, u32[]{:S(2)}, u32[]{:S(2)}) collective-permute-start(bf16[512,512]{1,0:T(8,128)(2,1)S(1)} %bitcast.19), channel_id=1, source_target_pairs={{0,7},{1,0},{2,1},{3,2},{4,3},{5,4},{6,5},{7,6},{8,15},{9,8},{10,9... | collective-permute-start | bytes 1572872 | tf_op jit(solution)/shard_map/ppermute | solution.py:218
  47.6 0.8 copy-done.1
  48.4 9.7 %all-gather.3.cloned.1.call-done = bf16[1024,512]{1,0:T(8,128)(2,1)} async-done(((bf16[128,512]{1,0:T(8,128)(2,1)}), bf16[1024,512]{1,0:T(8,128)(2,1)}) %all-gather.3.cloned.1.call-update) | async-done | bytes 1048592 | tf_op jit(solution)/shard_map/all_gather | solution.py:205
  58.1 3.6 %collective-permute-start = (bf16[1024,512]{1,0:T(8,128)(2,1)}, bf16[1024,512]{1,0:T(8,128)(2,1)S(1)}, u32[]{:S(2)}, u32[]{:S(2)}) collective-permute-start(bf16[1024,512]{1,0:T(8,128)(2,1)} %all-gather.3.cloned.1.call-done), channel_id=1, source_target_pairs={{0,16},{16,32},{32,48},{48,0},{1,17},{17,33},{33,49},{49,1},{2,18}... | collective-permute-start | bytes 3145736 | tf_op jit(solution)/shard_map/ppermute | solution.py:209
  61.7 3.5 %collective-permute-start.1 = (bf16[1024,512]{1,0:T(8,128)(2,1)}, bf16[1024,512]{1,0:T(8,128)(2,1)S(1)}, u32[]{:S(2)}, u32[]{:S(2)}) collective-permute-start(bf16[1024,512]{1,0:T(8,128)(2,1)} %all-gather.3.cloned.1.call-done), channel_id=1, source_target_pairs={{0,48},{16,0},{32,16},{48,32},{1,49},{17,1},{33,17},{49,33},{2,50}... | collective-permute-start | bytes 3145736 | tf_op jit(solution)/shard_map/ppermute | solution.py:209
  65.2 3.2 %collective-permute-start.6 = (bf16[512,512]{1,0:T(8,128)(2,1)S(1)}, bf16[512,512]{1,0:T(8,128)(2,1)}, u32[]{:S(2)}, u32[]{:S(2)}) collective-permute-start(bf16[512,512]{1,0:T(8,128)(2,1)S(1)} %collective-permute-done.4.down1), channel_id=1, source_target_pairs={{0,1},{1,2},{2,3},{3,4},{4,5},{5,6},{6,7},{7,0},{8,9},{9,10},{10,1... | collective-permute-start | bytes 1572872 | tf_op jit(solution)/shard_map/ppermute | solution.py:217
  68.4 0.8 copy-done.12
  69.2 2.6 %collective-permute-start.7 = (bf16[512,512]{1,0:T(8,128)(2,1)}, bf16[512,512]{1,0:T(8,128)(2,1)}, u32[]{:S(2)}, u32[]{:S(2)}) collective-permute-start(bf16[512,512]{1,0:T(8,128)(2,1)} %collective-permute-done.5.up1), channel_id=1, source_target_pairs={{0,7},{1,0},{2,1},{3,2},{4,3},{5,4},{6,5},{7,6},{8,15},{9,8},{10,9... | collective-permute-start | bytes 1572872 | tf_op jit(solution)/shard_map/ppermute | solution.py:218
  71.8 5.5 %collective-permute-done.6.down2 = bf16[512,512]{1,0:T(8,128)(2,1)} collective-permute-done((bf16[512,512]{1,0:T(8,128)(2,1)S(1)}, bf16[512,512]{1,0:T(8,128)(2,1)}, u32[]{:S(2)}, u32[]{:S(2)}) %collective-permute-start.6) | collective-permute-done | bytes 524320 | tf_op jit(solution)/shard_map/ppermute | solution.py:217
  77.3 3.5 %collective-permute-start.8 = (bf16[512,512]{1,0:T(8,128)(2,1)}, bf16[512,512]{1,0:T(8,128)(2,1)S(1)}, u32[]{:S(2)}, u32[]{:S(2)}) collective-permute-start(bf16[512,512]{1,0:T(8,128)(2,1)} %collective-permute-done.6.down2), channel_id=1, source_target_pairs={{0,1},{1,2},{2,3},{3,4},{4,5},{5,6},{6,7},{7,0},{8,9},{9,10},{10,1... | collective-permute-start | bytes 1572872 | tf_op jit(solution)/shard_map/ppermute | solution.py:217
  80.8 0.8 collective-permute-done.7.up2
  81.6 2.3 %collective-permute-start.9 = (bf16[512,512]{1,0:T(8,128)(2,1)}, bf16[512,512]{1,0:T(8,128)(2,1)S(1)}, u32[]{:S(2)}, u32[]{:S(2)}) collective-permute-start(bf16[512,512]{1,0:T(8,128)(2,1)} %collective-permute-done.7.up2), channel_id=1, source_target_pairs={{0,7},{1,0},{2,1},{3,2},{4,3},{5,4},{6,5},{7,6},{8,15},{9,8},{10,9... | collective-permute-start | bytes 1572872 | tf_op jit(solution)/shard_map/ppermute | solution.py:218
  83.9 0.8 slice.16
  84.7 2.2 %collective-permute-start.2 = (bf16[512,512]{1,0:T(8,128)(2,1)}, bf16[512,512]{1,0:T(8,128)(2,1)}, u32[]{:S(2)}, u32[]{:S(2)}) collective-permute-start(bf16[512,512]{1,0:T(8,128)(2,1)} %slice.16), channel_id=1, source_target_pairs={{0,16},{16,32},{32,48},{48,0},{1,17},{17,33},{33,49},{49,1},{2,18}... | collective-permute-start | bytes 1572872 | tf_op jit(solution)/shard_map/ppermute | solution.py:210
  86.9 0.9 slice.17
  87.8 4.8 %collective-permute-start.3 = (bf16[512,512]{1,0:T(8,128)(2,1)}, bf16[512,512]{1,0:T(8,128)(2,1)}, u32[]{:S(2)}, u32[]{:S(2)}) collective-permute-start(bf16[512,512]{1,0:T(8,128)(2,1)} %slice.17), channel_id=1, source_target_pairs={{0,48},{16,0},{32,16},{48,32},{1,49},{17,1},{33,17},{49,33},{2,50}... | collective-permute-start | bytes 1572872 | tf_op jit(solution)/shard_map/ppermute | solution.py:210
  92.7 0.2 shard_map.102
  92.9 0.6 broadcast.6
  93.5 0.7 reduce.6
  94.2 0.8 reshape.43
  94.9 5.6 %all-to-all-start = ((s32[64,1,2]{2,1,0:T(1,128)}), s32[64,1,2]{2,1,0:T(1,128)S(1)}, u32[]{:S(2)}, u32[]{:S(2)}) async-start(s32[64,1,2]{2,1,0:T(1,128)} %bitcast.2), calls=%async_computation | async-start | bytes 65536 | tf_op jit(solution)/shard_map/all_to_all | solution.py:224
  100.5 0.0 all-gather.5.cloned.1.call-start
  100.6 0.7 slice.18
  101.3 4.1 %collective-permute-start.10 = (bf16[256,512]{1,0:T(8,128)(2,1)}, bf16[256,512]{1,0:T(8,128)(2,1)S(1)}, u32[]{:S(2)}, u32[]{:S(2)}) collective-permute-start(bf16[256,512]{1,0:T(8,128)(2,1)} %slice.18), channel_id=1, source_target_pairs={{0,1},{1,2},{2,3},{3,4},{4,5},{5,6},{6,7},{7,0},{8,9},{9,10},{10,1... | collective-permute-start | bytes 786440 | tf_op jit(solution)/shard_map/ppermute | solution.py:219
  105.5 0.7 slice.19
  106.2 2.9 %collective-permute-start.11 = (bf16[256,512]{1,0:T(8,128)(2,1)}, bf16[256,512]{1,0:T(8,128)(2,1)}, u32[]{:S(2)}, u32[]{:S(2)}) collective-permute-start(bf16[256,512]{1,0:T(8,128)(2,1)} %slice.19), channel_id=1, source_target_pairs={{0,7},{1,0},{2,1},{3,2},{4,3},{5,4},{6,5},{7,6},{8,15},{9,8},{10,9... | collective-permute-start | bytes 786440 | tf_op jit(solution)/shard_map/ppermute | solution.py:219
  109.1 0.1 pad_add_fusion.me_ref
  109.2 0.8 all-to-all-done
  110.0 0.8 reduce.7
  110.8 0.1 reshape.44.after_ref.slot_ref
  111.0 1.2 copy-done
  112.2 1.0 copy-done.2
  113.3 1.0 copy-done.13
  114.3 3.7 %shard_map.104.before_ref = f32[512,512]{1,0:T(8,128)S(1)} custom-call(s32[2]{0:T(128)S(1)} %pad_add_fusion.me_ref, bf16[8,8,16,512]{3,2,1,0:T(8,128)(2,1)S(1)} %bitcast.16, bf16[8,8,16,512]{3,2,1,0:T(8,128)(2,1)S(1)} %bitcast.12, bf16[8,8,16,512]{3,2,1,0:T(8,128)(2,1)S(1)} %bitcast.14, bf16[4,8,16,512]{3,2,1,0:T(8,128)(2,1)} %bitcast.8.a3, ...), custom_call_target="tpu_custom_call" | custom-call | flops 2684354560 | bytes 4194304 | tf_op jit(solution)/shard_map/pallas_call | solution.py:228
  118.0 0.0 copy-start.4
  118.0 0.0 copy-start.6
  118.0 0.0 copy-start.8
  118.1 3.1 %shard_map.105 = (f32[224,512]{1,0:T(8,128)S(1)}, f32[224,512]{1,0:T(8,128)S(1)}) custom-call(s32[2]{0:T(128)S(1)} %pad_add_fusion.me_ref, bf16[8,8,16,512]{3,2,1,0:T(8,128)(2,1)S(1)} %bitcast.17, bf16[8,8,16,512]{3,2,1,0:T(8,128)(2,1)S(1)} %bitcast.13, bf16[8,8,16,512]{3,2,1,0:T(8,128)(2,1)S(1)} %bitcast.15, bf16[4,8,16,512]{3,2,1,0:T(8,128)(2,1)} %bitcast.8.a3, ...), custom_call_target="tpu_custom_call" | custom-call | flops 1610612736 | bytes 4194304 | tf_op jit(solution)/shard_map/pallas_call | solution.py:236
  121.2 0.0 copy-start.10
  121.2 1.9 collective-permute-start.12
  123.1 1.8 collective-permute-done.12.theirs_ref
  124.9 0.0 copy-start.5
  125.0 0.0 copy-start.7
  125.0 0.0 copy-start.9
  125.0 1.2 shard_map.107
  126.2 22.7 %all_to_all.21.arrived_ref = bf16[128,2,512]{2,1,0:T(2,128)(2,1)S(1)} all-to-all(bf16[128,2,512]{2,1,0:T(2,128)(2,1)S(1)} %shard_map.107), channel_id=1, replica_groups=mesh['z'=8,'x'=4,'c'=2,'y'=8] {'z','x','c'}, dimensions={0} | all-to-all | bytes 524288 | tf_op jit(solution)/shard_map/all_to_all | solution.py:254
  148.8 1.4 shard_map.108.after_ref
  150.2 0.0 all-gather.5.cloned.1.call-update
  150.3 1.0 copy-done.11
  151.3 1.4 shard_map.106.value_ref
  152.7 0.5 convert_element_type.6
  153.3 28.0 %all_to_all.22 = f16[128,2,1536]{2,1,0:T(2,128)(2,1)S(1)} all-to-all(f16[128,2,1536]{2,1,0:T(2,128)(2,1)S(1)} %convert_element_type.6), channel_id=1, replica_groups=mesh['z'=8,'x'=4,'c'=2,'y'=8] {'z','x','c'}, dimensions={0} | all-to-all | bytes 1572864 | tf_op jit(solution)/shard_map/all_to_all | solution.py:274
  181.3 0.5 convert_element_type.7.arrived_ref
  181.8 1.9 shard_map.110
  183.7 7.5 %all-gather.5.cloned.1.call-done = bf16[228,4096]{1,0:T(8,128)(2,1)} async-done(((bf16[228,512]{1,0:T(8,128)(2,1)}), bf16[228,4096]{1,0:T(8,128)(2,1)}) %all-gather.5.cloned.1.call-update) | async-done | bytes 1867792 | tf_op jit(solution)/shard_map/all_gather | solution.py:262
  191.2 3.0 %copy.15 = bf16[228,4096]{1,0:T(8,128)(2,1)} copy(bf16[228,4096]{1,0:T(8,128)(2,1)} %all-gather.5.cloned.1.call-done) | data formatting | bytes 3735552
  (27 shorter events, 0.1 us)
Async XLA Ops:
  7.2 50.9 %all-gather.3.cloned.1.call-start = ((), (), s32[]{:S(2)}) async-start(), calls=%async_computation.4 | async-start | bytes 1179648 | tf_op jit(solution)/shard_map/all_gather | solution.py:205
  7.9 1.0 copy-start.3
  9.1 83.5 %copy-start.14 = (s32[112]{0:T(128)S(1)}, s32[112]{0:T(128)}, u32[]{:S(2)}) copy-start(s32[112]{0:T(128)} %param.12) | copy-start | bytes 1348
  9.2 83.5 %copy-start.15 = (s32[112]{0:T(128)S(1)}, s32[112]{0:T(128)}, u32[]{:S(2)}) copy-start(s32[112]{0:T(128)} %param.13) | copy-start | bytes 1348
  41.8 23.4 %collective-permute-start.4 = (bf16[512,512]{1,0:T(8,128)(2,1)S(1)}, bf16[512,512]{1,0:T(8,128)(2,1)S(1)}, u32[]{:S(2)}, u32[]{:S(2)}) collective-permute-start(bf16[512,512]{1,0:T(8,128)(2,1)S(1)} %bitcast.18), channel_id=1, source_target_pairs={{0,1},{1,2},{2,3},{3,4},{4,5},{5,6},{6,7},{7,0},{8,9},{9,10},{10,1... | collective-permute-start | bytes 1572872 | tf_op jit(solution)/shard_map/ppermute | solution.py:217
  45.3 23.9 %collective-permute-start.5 = (bf16[512,512]{1,0:T(8,128)(2,1)S(1)}, bf16[512,512]{1,0:T(8,128)(2,1)}, u32[]{:S(2)}, u32[]{:S(2)}) collective-permute-start(bf16[512,512]{1,0:T(8,128)(2,1)S(1)} %bitcast.19), channel_id=1, source_target_pairs={{0,7},{1,0},{2,1},{3,2},{4,3},{5,4},{6,5},{7,6},{8,15},{9,8},{10,9... | collective-permute-start | bytes 1572872 | tf_op jit(solution)/shard_map/ppermute | solution.py:218
  47.6 0.8 copy-start.1
  58.1 25.8 %collective-permute-start = (bf16[1024,512]{1,0:T(8,128)(2,1)}, bf16[1024,512]{1,0:T(8,128)(2,1)S(1)}, u32[]{:S(2)}, u32[]{:S(2)}) collective-permute-start(bf16[1024,512]{1,0:T(8,128)(2,1)} %all-gather.3.cloned.1.call-done), channel_id=1, source_target_pairs={{0,16},{16,32},{32,48},{48,0},{1,17},{17,33},{33,49},{49,1},{2,18}... | collective-permute-start | bytes 3145736 | tf_op jit(solution)/shard_map/ppermute | solution.py:209
  61.7 25.3 %collective-permute-start.1 = (bf16[1024,512]{1,0:T(8,128)(2,1)}, bf16[1024,512]{1,0:T(8,128)(2,1)S(1)}, u32[]{:S(2)}, u32[]{:S(2)}) collective-permute-start(bf16[1024,512]{1,0:T(8,128)(2,1)} %all-gather.3.cloned.1.call-done), channel_id=1, source_target_pairs={{0,48},{16,0},{32,16},{48,32},{1,49},{17,1},{33,17},{49,33},{2,50}... | collective-permute-start | bytes 3145736 | tf_op jit(solution)/shard_map/ppermute | solution.py:209
  65.2 12.1 %collective-permute-start.6 = (bf16[512,512]{1,0:T(8,128)(2,1)S(1)}, bf16[512,512]{1,0:T(8,128)(2,1)}, u32[]{:S(2)}, u32[]{:S(2)}) collective-permute-start(bf16[512,512]{1,0:T(8,128)(2,1)S(1)} %collective-permute-done.4.down1), channel_id=1, source_target_pairs={{0,1},{1,2},{2,3},{3,4},{4,5},{5,6},{6,7},{7,0},{8,9},{9,10},{10,1... | collective-permute-start | bytes 1572872 | tf_op jit(solution)/shard_map/ppermute | solution.py:217
  68.4 0.8 copy-start.12
  69.2 12.4 %collective-permute-start.7 = (bf16[512,512]{1,0:T(8,128)(2,1)}, bf16[512,512]{1,0:T(8,128)(2,1)}, u32[]{:S(2)}, u32[]{:S(2)}) collective-permute-start(bf16[512,512]{1,0:T(8,128)(2,1)} %collective-permute-done.5.up1), channel_id=1, source_target_pairs={{0,7},{1,0},{2,1},{3,2},{4,3},{5,4},{6,5},{7,6},{8,15},{9,8},{10,9... | collective-permute-start | bytes 1572872 | tf_op jit(solution)/shard_map/ppermute | solution.py:218
  77.3 23.3 %collective-permute-start.8 = (bf16[512,512]{1,0:T(8,128)(2,1)}, bf16[512,512]{1,0:T(8,128)(2,1)S(1)}, u32[]{:S(2)}, u32[]{:S(2)}) collective-permute-start(bf16[512,512]{1,0:T(8,128)(2,1)} %collective-permute-done.6.down2), channel_id=1, source_target_pairs={{0,1},{1,2},{2,3},{3,4},{4,5},{5,6},{6,7},{7,0},{8,9},{9,10},{10,1... | collective-permute-start | bytes 1572872 | tf_op jit(solution)/shard_map/ppermute | solution.py:217
  81.6 23.9 %collective-permute-start.9 = (bf16[512,512]{1,0:T(8,128)(2,1)}, bf16[512,512]{1,0:T(8,128)(2,1)S(1)}, u32[]{:S(2)}, u32[]{:S(2)}) collective-permute-start(bf16[512,512]{1,0:T(8,128)(2,1)} %collective-permute-done.7.up2), channel_id=1, source_target_pairs={{0,7},{1,0},{2,1},{3,2},{4,3},{5,4},{6,5},{7,6},{8,15},{9,8},{10,9... | collective-permute-start | bytes 1572872 | tf_op jit(solution)/shard_map/ppermute | solution.py:218
  84.7 26.3 %collective-permute-start.2 = (bf16[512,512]{1,0:T(8,128)(2,1)}, bf16[512,512]{1,0:T(8,128)(2,1)}, u32[]{:S(2)}, u32[]{:S(2)}) collective-permute-start(bf16[512,512]{1,0:T(8,128)(2,1)} %slice.16), channel_id=1, source_target_pairs={{0,16},{16,32},{32,48},{48,0},{1,17},{17,33},{33,49},{49,1},{2,18}... | collective-permute-start | bytes 1572872 | tf_op jit(solution)/shard_map/ppermute | solution.py:210
  87.8 23.2 %collective-permute-start.3 = (bf16[512,512]{1,0:T(8,128)(2,1)}, bf16[512,512]{1,0:T(8,128)(2,1)}, u32[]{:S(2)}, u32[]{:S(2)}) collective-permute-start(bf16[512,512]{1,0:T(8,128)(2,1)} %slice.17), channel_id=1, source_target_pairs={{0,48},{16,0},{32,16},{48,32},{1,49},{17,1},{33,17},{49,33},{2,50}... | collective-permute-start | bytes 1572872 | tf_op jit(solution)/shard_map/ppermute | solution.py:210
  94.9 15.1 %all-to-all-start = ((s32[64,1,2]{2,1,0:T(1,128)}), s32[64,1,2]{2,1,0:T(1,128)S(1)}, u32[]{:S(2)}, u32[]{:S(2)}) async-start(s32[64,1,2]{2,1,0:T(1,128)} %bitcast.2), calls=%async_computation | async-start | bytes 65536 | tf_op jit(solution)/shard_map/all_to_all | solution.py:224
  100.5 90.7 %all-gather.5.cloned.1.call-start = ((), (), s32[]{:S(2)}) async-start(), calls=%async_computation.5 | async-start | bytes 2138112 | tf_op jit(solution)/shard_map/all_gather | solution.py:262
  101.3 16.7 %collective-permute-start.10 = (bf16[256,512]{1,0:T(8,128)(2,1)}, bf16[256,512]{1,0:T(8,128)(2,1)S(1)}, u32[]{:S(2)}, u32[]{:S(2)}) collective-permute-start(bf16[256,512]{1,0:T(8,128)(2,1)} %slice.18), channel_id=1, source_target_pairs={{0,1},{1,2},{2,3},{3,4},{4,5},{5,6},{6,7},{7,0},{8,9},{9,10},{10,1... | collective-permute-start | bytes 786440 | tf_op jit(solution)/shard_map/ppermute | solution.py:219
  106.2 11.9 %collective-permute-start.11 = (bf16[256,512]{1,0:T(8,128)(2,1)}, bf16[256,512]{1,0:T(8,128)(2,1)}, u32[]{:S(2)}, u32[]{:S(2)}) collective-permute-start(bf16[256,512]{1,0:T(8,128)(2,1)} %slice.19), channel_id=1, source_target_pairs={{0,7},{1,0},{2,1},{3,2},{4,3},{5,4},{6,5},{7,6},{8,15},{9,8},{10,9... | collective-permute-start | bytes 786440 | tf_op jit(solution)/shard_map/ppermute | solution.py:219
  111.0 1.2 copy-start
  112.2 1.0 copy-start.2
  113.3 1.0 copy-start.13
  118.0 6.9 %copy-start.4 = (f32[224,512]{1,0:T(8,128)S(1)}, f32[224,512]{1,0:T(8,128)}, u32[]{:S(2)}) copy-start(f32[224,512]{1,0:T(8,128)} %master_ref.3) | copy-start | bytes 1376260
  118.0 6.9 %copy-start.6 = (f32[224,512]{1,0:T(8,128)S(1)}, f32[224,512]{1,0:T(8,128)}, u32[]{:S(2)}) copy-start(f32[224,512]{1,0:T(8,128)} %moment1_ref.3) | copy-start | bytes 1376260
  118.0 6.9 %copy-start.8 = (f32[224,512]{1,0:T(8,128)S(1)}, f32[224,512]{1,0:T(8,128)}, u32[]{:S(2)}) copy-start(f32[224,512]{1,0:T(8,128)} %moment2_ref.3) | copy-start | bytes 1376260
  121.2 27.6 %copy-start.10 = (f32[224,512]{1,0:T(8,128)}, f32[224,512]{1,0:T(8,128)S(1)}, u32[]{:S(2)}) copy-start(f32[224,512]{1,0:T(8,128)S(1)} %get-tuple-element.13.mine_ref) | copy-start | bytes 1376260
  121.2 3.7 %collective-permute-start.12 = (f32[224,512]{1,0:T(8,128)S(1)}, f32[224,512]{1,0:T(8,128)S(1)}, u32[]{:S(2)}, u32[]{:S(2)}) collective-permute-start(f32[224,512]{1,0:T(8,128)S(1)} %get-tuple-element.14), channel_id=1, source_target_pairs={{0,8},{8,0},{1,9},{9,1},{2,10},{10,2},{3,11},{11,3},{4,12},{12,4},... | collective-permute-start | bytes 1376264 | tf_op jit(solution)/shard_map/ppermute | solution.py:244
  124.9 25.3 %copy-start.5 = (f32[224,512]{1,0:T(8,128)S(1)}, f32[224,512]{1,0:T(8,128)}, u32[]{:S(2)}) copy-start(f32[224,512]{1,0:T(8,128)} %master_ref.3) | copy-start | bytes 1376260
  125.0 25.3 %copy-start.7 = (f32[224,512]{1,0:T(8,128)S(1)}, f32[224,512]{1,0:T(8,128)}, u32[]{:S(2)}) copy-start(f32[224,512]{1,0:T(8,128)} %moment1_ref.3) | copy-start | bytes 1376260
  125.0 25.3 %copy-start.9 = (f32[224,512]{1,0:T(8,128)S(1)}, f32[224,512]{1,0:T(8,128)}, u32[]{:S(2)}) copy-start(f32[224,512]{1,0:T(8,128)} %moment2_ref.3) | copy-start | bytes 1376260
  150.3 1.0 copy-start.11
Sparse Core Ops, SparseCore 0:
  10.1 47.9 all-gather.2
  150.4 40.7 all-gather.4

commit v3 on v2

v3 whole, which is shorter than its diff:
```python
import jax
import jax.numpy as jnp
import numpy as np
from jax import lax
from jax.experimental import pallas as pl
from jax.experimental.pallas import tpu as pltpu
from jax.sharding import Mesh, PartitionSpec as P

beta_one = 0.9
beta_two = 0.95
learn_rate = 0.1
adam_eps = 1e-08
adam_step = 1000
fix_one = 1.0 - beta_one**adam_step
fix_two = 1.0 - beta_two**adam_step

Z, X, CORES, Y = 8, 4, 2, 8
CHIPS = Z * X
DP = CHIPS * CORES
ROWS = 224
PAD = 256
PIECES = 112
PAIR = 2
CAP = 114
WIDTH = 512
LANES = 128
AHEAD = 3
SCALES = (1024.0, 64.0, 0.0625)

VMEM = pl.BlockSpec(memory_space=pltpu.VMEM)
SMEM = pl.BlockSpec(memory_space=pltpu.SMEM)
ANY = pl.BlockSpec(memory_space=pl.ANY)
LIMIT = 16 * 1024 * 1024
WIDE_LIMIT = 60 * 1024 * 1024


def call(kernel, out_shape, in_specs, out_specs, flops=0, limit=LIMIT, **kw):
    return pl.pallas_call(
        kernel,
        out_shape=out_shape,
        in_specs=in_specs,
        out_specs=out_specs,
        cost_estimate=pl.CostEstimate(flops=flops, bytes_accessed=4 << 20, transcendentals=0),
        compiler_params=pltpu.CompilerParams(vmem_limit_bytes=limit),
        **kw,
    )


def plan(owner_ref, slot_ref):
    shape = (LANES, LANES)

    def padded(ref):
        return jnp.concatenate([ref[...], jnp.full((1, LANES - PIECES), -1, jnp.int32)], axis=1)

    def column(row):
        return jnp.broadcast_to(row.astype(jnp.float32), shape).T.astype(jnp.int32)

    owner = padded(owner_ref)
    first, second = (lax.broadcasted_iota(jnp.int32, shape, dim) for dim in (0, 1))
    same = jnp.where((column(owner) == owner) & (first < second), 1, 0)
    rank = jnp.sum(same, axis=0, keepdims=True)
    lane = lax.broadcasted_iota(jnp.int32, (1, LANES), 1)
    position = jnp.where(lane < PIECES, owner * PAIR + rank, -1)
    found = jnp.where(column(position) == second, column(padded(slot_ref)) - CAP, 0)
    return position, jnp.sum(found, axis=0, keepdims=True) + CAP


def pack_cotangent(core_ref, owner_ref, slot_ref, cot_ref, out_ref, position_ref):
    position, slots = plan(owner_ref, slot_ref)
    position_ref[...] = position
    tokens = cot_ref.shape[0]
    slots = jnp.broadcast_to(slots.astype(jnp.float32), (tokens, LANES))
    spare = PAD - ROWS
    tail = lax.broadcasted_iota(jnp.int32, (tokens, LANES), 1) >= LANES - spare

    def fill(flip):
        for device in range(DP):
            start = ROWS * device
            entries = pltpu.roll(slots, (LANES - spare - PAIR * device) % LANES, 1)
            last = jnp.concatenate([cot_ref[:, start + LANES : start + ROWS], jnp.zeros((tokens, spare), jnp.bfloat16)], axis=1)
            last = jnp.where(tail, entries, last.astype(jnp.float32)).astype(jnp.bfloat16)
            place = PAD * ((device % CORES) ^ flip)
            out_ref[device // CORES, :, place : place + LANES] = cot_ref[:, start : start + LANES]
            out_ref[device // CORES, :, place + LANES : place + PAD] = last

    @pl.when(core_ref[0] == 0)
    def _():
        fill(0)

    @pl.when(core_ref[0] == 1)
    def _():
        fill(1)


def partial_grad(me_ref, act_ref, *refs):
    *parts, mine_ref, theirs_ref, slots_ref, cot_buf, act_buf, cot_sem, act_sem = refs
    steps = [0, -1, 1, -2, 2, -3, 3, 4]
    plans = []
    for block, step in enumerate(steps):
        index = lax.rem(me_ref[0] + (Y + step), Y)
        plans.append([pltpu.make_async_copy(act_ref.at[:, index], act_buf.at[block], act_sem.at[block])])
    for number, ref in enumerate(parts):
        block, start = min(number, Y - 1), PAD if number == Y else 0
        target = cot_buf.at[block, pl.ds(start, ref.shape[0])]
        plans[block].append(pltpu.make_async_copy(ref, target, cot_sem.at[number]))
    for copies in plans[:AHEAD]:
        for copy in copies:
            copy.start()
    total = None
    for block, copies in enumerate(plans):
        for copy in copies:
            copy.wait()
        for copy in plans[block + AHEAD] if block + AHEAD < Y else ():
            copy.start()
        act = act_buf[block].reshape(CHIPS * 16, WIDTH)
        part = lax.dot_general(
            cot_buf[block], act, (((0,), (0,)), ((), ())), preferred_element_type=jnp.float32
        )
        total = part if total is None else total + part
    mine_ref[...] = total[:ROWS]
    theirs_ref[:ROWS] = total[PAD : PAD + ROWS]

    def received(start):
        tile = cot_buf[0, :, start + LANES : start + PAD].astype(jnp.float32).reshape(CHIPS, 16, LANES)[:, 0]
        square = jnp.concatenate([tile, jnp.zeros((LANES - CHIPS, LANES), jnp.float32)], axis=0)
        return square.T[LANES - (PAD - ROWS) :][:8]

    slots_ref[...] = received(0)
    theirs_ref[ROWS:, :LANES] = received(PAD)
    theirs_ref[ROWS:, LANES:] = jnp.zeros((8, WIDTH - LANES), jnp.float32)


def update_state(mine_ref, theirs_ref, master_ref, moment1_ref, moment2_ref):
    grad = mine_ref[...] + theirs_ref[:ROWS]
    moment1 = beta_one * moment1_ref[...] + (1.0 - beta_one) * grad
    moment2 = beta_two * moment2_ref[...] + (1.0 - beta_two) * grad * grad
    update = learn_rate * (moment1 / fix_one) / (jnp.sqrt(moment2 / fix_two) + adam_eps)
    return master_ref[...] - update, moment1, moment2


def step_weights(
    position_ref, mine_ref, theirs_ref, master_ref, moment1_ref, moment2_ref, core_ref, slots_ref, out_ref, table_ref, master
):
    for core in range(CORES):
        rows = jnp.where(core_ref[0] == core, slots_ref[:PAIR], theirs_ref[ROWS : ROWS + PAIR, :LANES])
        table_ref[PAIR * core : PAIR * core + PAIR] = rows.astype(jnp.int32)
    master[...] = update_state(mine_ref, theirs_ref, master_ref, moment1_ref, moment2_ref)[0]
    out_ref[...] = jnp.zeros_like(out_ref)
    for piece in range(PIECES):
        rows = master[PAIR * piece : PAIR * piece + PAIR, :]
        out_ref[position_ref[0, piece]] = rows.astype(jnp.bfloat16)


def step_states(position_ref, mine_ref, theirs_ref, master_ref, moment1_ref, moment2_ref, out_ref, state):
    fields = update_state(mine_ref, theirs_ref, master_ref, moment1_ref, moment2_ref)
    for index, field in enumerate(fields):
        state[index] = field * SCALES[index]
    out_ref[...] = jnp.zeros_like(out_ref)
    for piece in range(PIECES):
        place = position_ref[0, piece]
        for index in range(3):
            rows = state[index, PAIR * piece : PAIR * piece + PAIR, :]
            out_ref[place, :, WIDTH * index : WIDTH * (index + 1)] = rows


def place_states(slot_ref, arrived_ref, a_ref, b_ref, c_ref, placed):
    placed[...] = jnp.zeros_like(placed)
    for entry in range(DP * PAIR):
        placed[slot_ref[entry % 4, entry // 4]] = arrived_ref[entry]
    for index, ref in enumerate((a_ref, b_ref, c_ref)):
        rows = placed[:CAP, :, WIDTH * index : WIDTH * (index + 1)].reshape(PAIR * CAP, WIDTH)
        ref[...] = rows * (1.0 / SCALES[index])


def place_weights(slot_ref, arrived_ref, out_ref, placed):
    placed[...] = jnp.zeros_like(placed)
    for entry in range(DP * PAIR):
        placed[slot_ref[entry % 4, entry // 4]] = arrived_ref[entry].astype(jnp.float32)
    out_ref[...] = placed[:CAP].reshape(PAIR * CAP, WIDTH).astype(jnp.bfloat16)


def hold(value_ref, after_ref, out_ref):
    del value_ref, after_ref, out_ref


def f32(*shape):
    return jax.ShapeDtypeStruct(shape, jnp.float32)


def int32(*shape):
    return jax.ShapeDtypeStruct(shape, jnp.int32)


def bf16(*shape):
    return jax.ShapeDtypeStruct(shape, jnp.bfloat16)


def shards(activations, cotangent, master, first_moment, second_moment, new_owner, new_slot):
    dp_axes = ("z", "x", "c")
    core = lax.axis_index("c").astype(jnp.int32).reshape(1)
    packed, position = call(
        pack_cotangent, (bf16(CHIPS, 16, 2 * PAD), int32(1, LANES)), [SMEM] + [VMEM] * 3, (VMEM,) * 2
    )(core, new_owner.reshape(1, PIECES), new_slot.reshape(1, PIECES), cotangent)
    shared = lax.all_to_all(packed, ("z", "x"), split_axis=0, concat_axis=0, tiled=True)
    shared = shared.reshape(CHIPS * 16, 2 * PAD)

    act = lax.all_gather(activations, ("z", "x"), axis=0, tiled=True).reshape(CHIPS, Y, 16, WIDTH)

    right = [(i, (i + 1) % Y) for i in range(Y)]
    left = [(i, (i - 1) % Y) for i in range(Y)]
    down, up = [shared], [shared]
    for _ in range(Y // 2 - 1):
        down.append(lax.ppermute(down[-1], "y", right))
        up.append(lax.ppermute(up[-1], "y", left))
    far = [lax.ppermute(down[-1][:PAD], "y", right), lax.ppermute(up[-1][PAD:], "y", left)]

    me = lax.axis_index("y").astype(jnp.int32).reshape(1)
    mine, theirs, slots = call(
        partial_grad,
        (f32(ROWS, WIDTH), f32(ROWS + 8, WIDTH), f32(8, LANES)),
        [SMEM] + [ANY] * 10,
        (VMEM,) * 3,
        flops=1 << 32,
        limit=WIDE_LIMIT,
        scratch_shapes=[
            pltpu.VMEM((Y, CHIPS * 16, 2 * PAD), jnp.bfloat16),
            pltpu.VMEM((Y, CHIPS, 16, WIDTH), jnp.bfloat16),
            pltpu.SemaphoreType.DMA((Y + 1,)),
            pltpu.SemaphoreType.DMA((Y,)),
        ],
    )(me, act, shared, down[1], up[1], down[2], up[2], down[3], up[3], *far)
    theirs = lax.ppermute(theirs, "c", [(0, 1), (1, 0)])
    step = (position, mine, theirs, master, first_moment, second_moment)
    weights, slots = call(
        step_weights,
        (bf16(DP * PAIR, PAIR, WIDTH), int32(CORES * PAIR, LANES)),
        [SMEM] + [VMEM] * 5 + [SMEM, VMEM],
        (VMEM,) * 2,
        scratch_shapes=[pltpu.VMEM((ROWS, WIDTH), jnp.float32)],
    )(*step, core, slots)

    weights = lax.all_to_all(weights, dp_axes, split_axis=0, concat_axis=0, tiled=True)
    weights = call(
        place_weights,
        bf16(PAIR * CAP, WIDTH),
        [SMEM, VMEM],
        VMEM,
        scratch_shapes=[pltpu.VMEM((CAP + 1, PAIR, WIDTH), jnp.float32)],
    )(slots, weights)
    new_weights = lax.all_gather(weights, "y", axis=1, tiled=True)

    states = call(
        step_states,
        f32(DP * PAIR, PAIR, 3 * WIDTH),
        [SMEM] + [VMEM] * 5,
        VMEM,
        flops=1 << 31,
        scratch_shapes=[pltpu.VMEM((3, ROWS, WIDTH), jnp.float32)],
    )(*step)
    states = call(hold, f32(*states.shape), [ANY, ANY], ANY, input_output_aliases={0: 0})(states, weights)
    states = states.astype(jnp.float16)
    arrived = lax.all_to_all(states, dp_axes, split_axis=0, concat_axis=0, tiled=True)
    placed = call(
        place_states,
        (f32(PAIR * CAP, WIDTH),) * 3,
        [SMEM, VMEM],
        (VMEM,) * 3,
        scratch_shapes=[pltpu.VMEM((CAP + 1, PAIR, 3 * WIDTH), jnp.float32)],
    )(slots, arrived.astype(jnp.float32))
    return (*placed, new_weights)


def solution(mesh):
    fine = Mesh(np.asarray(mesh.devices).reshape(Z, X, CORES, Y), ("z", "x", "c", "y"))
    dp = ("z", "x", "c")
    in_specs = (
        P(dp, "y"),
        P(dp + ("y",), None),
        P(dp, "y"),
        P(dp, "y"),
        P(dp, "y"),
        P(dp),
        P(dp),
    )
    out_specs = (P(dp, "y"), P(dp, "y"), P(dp, "y"), P(dp, None))
    return jax.shard_map(shards, mesh=fine, in_specs=in_specs, out_specs=out_specs, check_vma=False)
```

time: 202 us -> 187 us (0.926)
  starting transfers between devices: 46.2 us -> 26.5 us
  waiting for transfers between devices: 26.7 us -> 46.1 us
  local copies, waits for them, and re-layouts: 14.6 us -> 7.07 us
  blocking collectives: 83.3 us -> 78.1 us
    ppermute x3, waiting for transfers between devices: 0.76 us -> 18.3 us  [shards(): up.append(lax.ppermute(up[-1], 'y', left))]
    ppermute x4 -> x0, starting transfers between devices: 14.1 us -> none  [the longest x2 7.04 us: shards(): acts = [act, lax.ppermute(act, 'x', right), lax.ppermute(act, 'x', left)]]
    ppermute x1, waiting for transfers between devices: 0.01 us -> 5.88 us  [shards(): lax.ppermute(down[-1][:PAD], 'y', right)]
    all_to_all x1 -> x0, starting transfers between devices: 5.57 us -> none  [shards(): lax.all_to_all(slots.reshape(DP, 1, PAIR), dp_axes, split_axis=0, concat_...]
    all_to_all x1, blocking collectives: 22.7 us -> 18.5 us  [shards(): lax.all_to_all(weights, dp_axes, split_axis=0, concat_axis=0, tiled=True)]
    ppermute x3, waiting for transfers between devices: 5.46 us -> 1.44 us  [shards(): down.append(lax.ppermute(down[-1], 'y', right))]
    ppermute x3, starting transfers between devices: 7.17 us -> 10.4 us  [shards(): up.append(lax.ppermute(up[-1], 'y', left))]
    ppermute x3, starting transfers between devices: 10.3 us -> 7.34 us  [shards(): down.append(lax.ppermute(down[-1], 'y', right))]
  transfers between devices with their start and end apart: 16 -> 11, of which waited for: 6 -> 11; matrix products, arithmetic and copies ran while one was open for 4% -> 1% of each run, Pallas kernels for 4% -> 2%
where the time goes in v3:
time: 187 us; the launch traced here: 186 us
  blocking collectives  78.1 us (42%)
  waiting for transfers between devices  46.1 us (25%)
  starting transfers between devices  26.5 us (14%)
  between operations  14.3 us (8%)
  Pallas kernels  12.7 us (7%)
  local copies, waits for them, and re-layouts  7.07 us (4%)
    all_to_all x1, blocking collectives, shards(): lax.all_to_all(packed, ('z', 'x'), split_axis=0, concat_axis=0, tiled=True)  31.6 us
    all_to_all x1, blocking collectives, shards(): lax.all_to_all(states, dp_axes, split_axis=0, concat_axis=0, tiled=True)  28 us
    all_to_all x1, blocking collectives, shards(): lax.all_to_all(weights, dp_axes, split_axis=0, concat_axis=0, tiled=True)  18.5 us
    ppermute x3, waiting for transfers between devices, shards(): up.append(lax.ppermute(up[-1], 'y', left))  18.3 us
    ppermute x3, starting transfers between devices, shards(): up.append(lax.ppermute(up[-1], 'y', left))  10.4 us
    all_gather x1, waiting for transfers between devices, shards(): lax.all_gather(activations, ('z', 'x'), axis=0, tiled=True)  10.1 us
    ppermute x3, starting transfers between devices, shards(): down.append(lax.ppermute(down[-1], 'y', right))  7.34 us
    unnamed x33, local copies, waits for them, and re-layouts  7.04 us
  transfers between devices with their start and end apart: 11, of which 11 were waited for; matrix products, arithmetic and copies ran while one was open for 1% of the time, Pallas kernels for 2%

profile of v3, /device:TPU:8, one launch (start us, length us, event | category | flops | bytes accessed | tf_op | source)
XLA Modules:
  0.0 185.9 jit_solution(9006061587497182340)
XLA Ops:
  7.2 0.0 all-gather.3.cloned.1.call-start
  7.2 0.7 all-gather.3.cloned.1.call-update
  7.9 0.0 all-gather.5.cloned.1.call-start
  8.0 0.0 copy-start
  8.0 1.0 copy-done
  9.0 0.0 copy-start.7
  9.0 0.7 copy-done.7
  9.6 0.0 copy-start.8
  9.6 0.7 copy-done.8
  10.3 0.6 shard_map.102
  10.8 31.6 %all_to_all.15 = bf16[32,16,512]{2,1,0:T(8,128)(2,1)S(1)} all-to-all(bf16[32,16,512]{2,1,0:T(8,128)(2,1)S(1)} %get-tuple-element.15), channel_id=1, replica_groups=mesh['z'=8,'x'=4,'c'=2,'y'=8] {'z','x'}, dimensions={0} | all-to-all | bytes 1048576 | tf_op jit(solution)/shard_map/all_to_all | solution.py:204
  42.5 0.0 copy-start.9
  42.5 2.4 %collective-permute-start.1 = (bf16[512,512]{1,0:T(8,128)(2,1)S(1)}, bf16[512,512]{1,0:T(8,128)(2,1)S(1)}, u32[]{:S(2)}, u32[]{:S(2)}) collective-permute-start(bf16[512,512]{1,0:T(8,128)(2,1)S(1)} %bitcast.8), channel_id=1, source_target_pairs={{0,7},{1,0},{2,1},{3,2},{4,3},{5,4},{6,5},{7,6},{8,15},{9,8},{10,9... | collective-permute-start | bytes 1572872 | tf_op jit(solution)/shard_map/ppermute | solution.py:214
  44.9 3.4 %collective-permute-start = (bf16[512,512]{1,0:T(8,128)(2,1)S(1)}, bf16[512,512]{1,0:T(8,128)(2,1)S(1)}, u32[]{:S(2)}, u32[]{:S(2)}) collective-permute-start(bf16[512,512]{1,0:T(8,128)(2,1)S(1)} %bitcast.9), channel_id=1, source_target_pairs={{0,1},{1,2},{2,3},{3,4},{4,5},{5,6},{6,7},{7,0},{8,9},{9,10},{10,1... | collective-permute-start | bytes 1572872 | tf_op jit(solution)/shard_map/ppermute | solution.py:213
  48.3 7.0 %collective-permute-done.1.refs_2_ = bf16[512,512]{1,0:T(8,128)(2,1)S(1)} collective-permute-done((bf16[512,512]{1,0:T(8,128)(2,1)S(1)}, bf16[512,512]{1,0:T(8,128)(2,1)S(1)}, u32[]{:S(2)}, u32[]{:S(2)}) %collective-permute-start.1) | collective-permute-done | bytes 524320 | tf_op jit(solution)/shard_map/ppermute | solution.py:214
  55.3 0.0 copy-start.12
  55.3 3.4 %collective-permute-start.3 = (bf16[512,512]{1,0:T(8,128)(2,1)S(1)}, bf16[512,512]{1,0:T(8,128)(2,1)S(1)}, u32[]{:S(2)}, u32[]{:S(2)}) collective-permute-start(bf16[512,512]{1,0:T(8,128)(2,1)S(1)} %collective-permute-done.1.refs_2_), channel_id=1, source_target_pairs={{0,7},{1,0},{2,1},{3,2},{4,3},{5,4},{6,5},{7,6},{8,15},{9,8},{10,9... | collective-permute-start | bytes 1572872 | tf_op jit(solution)/shard_map/ppermute | solution.py:214
  58.7 0.5 collective-permute-done.refs_1_
  59.2 0.0 copy-start.13
  59.2 2.0 %collective-permute-start.2 = (bf16[512,512]{1,0:T(8,128)(2,1)S(1)}, bf16[512,512]{1,0:T(8,128)(2,1)S(1)}, u32[]{:S(2)}, u32[]{:S(2)}) collective-permute-start(bf16[512,512]{1,0:T(8,128)(2,1)S(1)} %collective-permute-done.refs_1_), channel_id=1, source_target_pairs={{0,1},{1,2},{2,3},{3,4},{4,5},{5,6},{6,7},{7,0},{8,9},{9,10},{10,1... | collective-permute-start | bytes 1572872 | tf_op jit(solution)/shard_map/ppermute | solution.py:213
  61.2 6.1 %collective-permute-done.3.refs_4_ = bf16[512,512]{1,0:T(8,128)(2,1)S(1)} collective-permute-done((bf16[512,512]{1,0:T(8,128)(2,1)S(1)}, bf16[512,512]{1,0:T(8,128)(2,1)S(1)}, u32[]{:S(2)}, u32[]{:S(2)}) %collective-permute-start.3) | collective-permute-done | bytes 524320 | tf_op jit(solution)/shard_map/ppermute | solution.py:214
  67.3 0.0 copy-start.14
  67.3 4.6 %collective-permute-start.5 = (bf16[512,512]{1,0:T(8,128)(2,1)S(1)}, bf16[512,512]{1,0:T(8,128)(2,1)S(1)}, u32[]{:S(2)}, u32[]{:S(2)}) collective-permute-start(bf16[512,512]{1,0:T(8,128)(2,1)S(1)} %collective-permute-done.3.refs_4_), channel_id=1, source_target_pairs={{0,7},{1,0},{2,1},{3,2},{4,3},{5,4},{6,5},{7,6},{8,15},{9,8},{10,9... | collective-permute-start | bytes 1572872 | tf_op jit(solution)/shard_map/ppermute | solution.py:214
  72.0 0.5 collective-permute-done.2.refs_3_
  72.5 0.0 copy-start.15
  72.5 1.9 %collective-permute-start.4 = (bf16[512,512]{1,0:T(8,128)(2,1)S(1)}, bf16[512,512]{1,0:T(8,128)(2,1)S(1)}, u32[]{:S(2)}, u32[]{:S(2)}) collective-permute-start(bf16[512,512]{1,0:T(8,128)(2,1)S(1)} %collective-permute-done.2.refs_3_), channel_id=1, source_target_pairs={{0,1},{1,2},{2,3},{3,4},{4,5},{5,6},{6,7},{7,0},{8,9},{9,10},{10,1... | collective-permute-start | bytes 1572872 | tf_op jit(solution)/shard_map/ppermute | solution.py:213
  74.4 0.0 copy-done.12
  74.4 0.0 copy-done.13
  74.4 5.1 %collective-permute-done.5.refs_6_ = bf16[512,512]{1,0:T(8,128)(2,1)S(1)} collective-permute-done((bf16[512,512]{1,0:T(8,128)(2,1)S(1)}, bf16[512,512]{1,0:T(8,128)(2,1)S(1)}, u32[]{:S(2)}, u32[]{:S(2)}) %collective-permute-start.5) | collective-permute-done | bytes 524320 | tf_op jit(solution)/shard_map/ppermute | solution.py:214
  79.6 4.8 %collective-permute-start.7 = (bf16[256,512]{1,0:T(8,128)(2,1)S(1)}, bf16[256,512]{1,0:T(8,128)(2,1)}, u32[]{:S(2)}, u32[]{:S(2)}) collective-permute-start(bf16[256,512]{1,0:T(8,128)(2,1)S(1)} %slice.9), channel_id=1, source_target_pairs={{0,7},{1,0},{2,1},{3,2},{4,3},{5,4},{6,5},{7,6},{8,15},{9,8},{10,9... | collective-permute-start | bytes 786440 | tf_op jit(solution)/shard_map/ppermute | solution.py:215
  84.4 0.5 collective-permute-done.4.refs_5_
  84.9 1.9 %collective-permute-start.6 = (bf16[256,512]{1,0:T(8,128)(2,1)S(1)}, bf16[256,512]{1,0:T(8,128)(2,1)}, u32[]{:S(2)}, u32[]{:S(2)}) collective-permute-start(bf16[256,512]{1,0:T(8,128)(2,1)S(1)} %slice.8), channel_id=1, source_target_pairs={{0,1},{1,2},{2,3},{3,4},{4,5},{5,6},{6,7},{7,0},{8,9},{9,10},{10,1... | collective-permute-start | bytes 786440 | tf_op jit(solution)/shard_map/ppermute | solution.py:215
  86.8 1.8 collective-permute-done.7.refs_8_
  88.6 5.9 %collective-permute-done.6.refs_7_ = bf16[256,512]{1,0:T(8,128)(2,1)} collective-permute-done((bf16[256,512]{1,0:T(8,128)(2,1)S(1)}, bf16[256,512]{1,0:T(8,128)(2,1)}, u32[]{:S(2)}, u32[]{:S(2)}) %collective-permute-start.6) | collective-permute-done | bytes 262176 | tf_op jit(solution)/shard_map/ppermute | solution.py:215
  94.5 10.1 %all-gather.3.cloned.1.call-done = bf16[4096,512]{1,0:T(8,128)(2,1)} async-done(((bf16[128,512]{1,0:T(8,128)(2,1)}), bf16[4096,512]{1,0:T(8,128)(2,1)}) %all-gather.3.cloned.1.call-update) | async-done | bytes 4194320 | tf_op jit(solution)/shard_map/all_gather | solution.py:207
  104.6 0.0 copy-done.14
  104.6 0.0 copy-done.15
  104.6 0.0 copy-done.11
  104.6 0.0 copy-done.9
  104.6 0.0 copy-done.10
  104.6 0.0 copy-start.1
  104.6 0.0 copy-start.2
  104.6 0.0 copy-start.3
  104.6 6.2 %shard_map.103 = (f32[224,512]{1,0:T(8,128)}, f32[232,512]{1,0:T(8,128)}, f32[8,128]{1,0:T(8,128)}) custom-call(s32[1]{0:T(128)} %bitcast.3.me_ref, bf16[32,8,16,512]{3,2,1,0:T(8,128)(2,1)} %bitcast.11, bf16[512,512]{1,0:T(8,128)(2,1)} %bitcast.10, bf16[512,512]{1,0:T(8,128)(2,1)} %copy-done.13, bf16[512,512]{1,0:T(8,128)(2,1)} %copy-done.12, ...), custom_call_target="tpu_custom_call" | custom-call | flops 4294967296 | bytes 4194304 | tf_op jit(solution)/shard_map/pallas_call | solution.py:218
  110.8 1.9 %collective-permute-start.8 = (f32[232,512]{1,0:T(8,128)}, f32[232,512]{1,0:T(8,128)S(1)}, u32[]{:S(2)}, u32[]{:S(2)}) collective-permute-start(f32[232,512]{1,0:T(8,128)} %get-tuple-element.17), channel_id=1, source_target_pairs={{0,8},{8,0},{1,9},{9,1},{2,10},{10,2},{3,11},{11,3},{4,12},{12,4},... | collective-permute-start | bytes 1425416 | tf_op jit(solution)/shard_map/ppermute | solution.py:232
  112.7 2.0 %collective-permute-done.8.theirs_ref = f32[232,512]{1,0:T(8,128)S(1)} collective-permute-done((f32[232,512]{1,0:T(8,128)}, f32[232,512]{1,0:T(8,128)S(1)}, u32[]{:S(2)}, u32[]{:S(2)}) %collective-permute-start.8) | collective-permute-done | bytes 475168 | tf_op jit(solution)/shard_map/ppermute | solution.py:232
  114.8 0.0 copy-done.1
  114.8 0.0 copy-done.2
  114.8 0.0 copy-done.3
  114.8 0.0 copy-start.4
  114.8 1.0 copy-done.4
  115.8 0.7 copy-done.6
  116.5 1.2 shard_map.104
  117.7 18.5 %all_to_all.16.arrived_ref = bf16[128,2,512]{2,1,0:T(2,128)(2,1)S(1)} all-to-all(bf16[128,2,512]{2,1,0:T(2,128)(2,1)S(1)} %get-tuple-element.20), channel_id=1, replica_groups=mesh['z'=8,'x'=4,'c'=2,'y'=8] {'z','x','c'}, dimensions={0} | all-to-all | bytes 524288 | tf_op jit(solution)/shard_map/all_to_all | solution.py:242
  136.2 1.4 shard_map.106.after_ref
  137.6 0.0 all-gather.5.cloned.1.call-update
  137.6 0.0 copy-done.5
  137.6 1.4 shard_map.105.value_ref
  139.1 0.5 convert_element_type.6
  139.6 28.0 %all_to_all.17 = f16[128,2,1536]{2,1,0:T(2,128)(2,1)S(1)} all-to-all(f16[128,2,1536]{2,1,0:T(2,128)(2,1)S(1)} %convert_element_type.6), channel_id=1, replica_groups=mesh['z'=8,'x'=4,'c'=2,'y'=8] {'z','x','c'}, dimensions={0} | all-to-all | bytes 1572864 | tf_op jit(solution)/shard_map/all_to_all | solution.py:262
  167.6 0.5 convert_element_type.7.arrived_ref
  168.1 2.0 %shard_map.108 = (f32[228,512]{1,0:T(8,128)}, f32[228,512]{1,0:T(8,128)}, f32[228,512]{1,0:T(8,128)}) custom-call(s32[4,128]{1,0:T(4,128)S(1)} %get-tuple-element.19.slot_ref, f32[128,2,1536]{2,1,0:T(2,128)S(1)} %convert_element_type.7.arrived_ref), custom_call_target="tpu_custom_call" | custom-call | bytes 4194304 | tf_op jit(solution)/shard_map/pallas_call | solution.py:263
  170.1 6.0 %all-gather.5.cloned.1.call-done = bf16[228,4096]{1,0:T(8,128)(2,1)} async-done(((bf16[228,512]{1,0:T(8,128)(2,1)}), bf16[228,4096]{1,0:T(8,128)(2,1)}) %all-gather.5.cloned.1.call-update) | async-done | bytes 1867792 | tf_op jit(solution)/shard_map/all_gather | solution.py:250
  176.1 3.0 %copy.14 = bf16[228,4096]{1,0:T(8,128)(2,1)} copy(bf16[228,4096]{1,0:T(8,128)(2,1)} %all-gather.5.cloned.1.call-done) | data formatting | bytes 3735552
  (7 shorter events, 0.0 us)
Async XLA Ops:
  7.2 97.4 %all-gather.3.cloned.1.call-start = ((), (), s32[]{:S(2)}) async-start(), calls=%async_computation.3 | async-start | bytes 4325376 | tf_op jit(solution)/shard_map/all_gather | solution.py:207
  7.9 168.2 %all-gather.5.cloned.1.call-start = ((), (), s32[]{:S(2)}) async-start(), calls=%async_computation.4 | async-start | bytes 2138112 | tf_op jit(solution)/shard_map/all_gather | solution.py:250
  8.0 1.0 copy-start
  9.0 0.7 copy-start.7
  9.6 0.7 copy-start.8
  42.5 62.1 %copy-start.9 = (bf16[32,16,512]{2,1,0:T(8,128)(2,1)}, bf16[32,16,512]{2,1,0:T(8,128)(2,1)S(1)}, u32[]{:S(2)}) copy-start(bf16[32,16,512]{2,1,0:T(8,128)(2,1)S(1)} %all_to_all.15) | copy-start | bytes 1572868
  42.5 12.8 %collective-permute-start.1 = (bf16[512,512]{1,0:T(8,128)(2,1)S(1)}, bf16[512,512]{1,0:T(8,128)(2,1)S(1)}, u32[]{:S(2)}, u32[]{:S(2)}) collective-permute-start(bf16[512,512]{1,0:T(8,128)(2,1)S(1)} %bitcast.8), channel_id=1, source_target_pairs={{0,7},{1,0},{2,1},{3,2},{4,3},{5,4},{6,5},{7,6},{8,15},{9,8},{10,9... | collective-permute-start | bytes 1572872 | tf_op jit(solution)/shard_map/ppermute | solution.py:214
  44.9 14.3 %collective-permute-start = (bf16[512,512]{1,0:T(8,128)(2,1)S(1)}, bf16[512,512]{1,0:T(8,128)(2,1)S(1)}, u32[]{:S(2)}, u32[]{:S(2)}) collective-permute-start(bf16[512,512]{1,0:T(8,128)(2,1)S(1)} %bitcast.9), channel_id=1, source_target_pairs={{0,1},{1,2},{2,3},{3,4},{4,5},{5,6},{6,7},{7,0},{8,9},{9,10},{10,1... | collective-permute-start | bytes 1572872 | tf_op jit(solution)/shard_map/ppermute | solution.py:213
  55.3 19.1 %copy-start.12 = (bf16[512,512]{1,0:T(8,128)(2,1)}, bf16[512,512]{1,0:T(8,128)(2,1)S(1)}, u32[]{:S(2)}) copy-start(bf16[512,512]{1,0:T(8,128)(2,1)S(1)} %collective-permute-done.1.refs_2_) | copy-start | bytes 1572868
  55.3 12.0 %collective-permute-start.3 = (bf16[512,512]{1,0:T(8,128)(2,1)S(1)}, bf16[512,512]{1,0:T(8,128)(2,1)S(1)}, u32[]{:S(2)}, u32[]{:S(2)}) collective-permute-start(bf16[512,512]{1,0:T(8,128)(2,1)S(1)} %collective-permute-done.1.refs_2_), channel_id=1, source_target_pairs={{0,7},{1,0},{2,1},{3,2},{4,3},{5,4},{6,5},{7,6},{8,15},{9,8},{10,9... | collective-permute-start | bytes 1572872 | tf_op jit(solution)/shard_map/ppermute | solution.py:214
  59.2 15.2 %copy-start.13 = (bf16[512,512]{1,0:T(8,128)(2,1)}, bf16[512,512]{1,0:T(8,128)(2,1)S(1)}, u32[]{:S(2)}) copy-start(bf16[512,512]{1,0:T(8,128)(2,1)S(1)} %collective-permute-done.refs_1_) | copy-start | bytes 1572868
  59.2 13.3 %collective-permute-start.2 = (bf16[512,512]{1,0:T(8,128)(2,1)S(1)}, bf16[512,512]{1,0:T(8,128)(2,1)S(1)}, u32[]{:S(2)}, u32[]{:S(2)}) collective-permute-start(bf16[512,512]{1,0:T(8,128)(2,1)S(1)} %collective-permute-done.refs_1_), channel_id=1, source_target_pairs={{0,1},{1,2},{2,3},{3,4},{4,5},{5,6},{6,7},{7,0},{8,9},{9,10},{10,1... | collective-permute-start | bytes 1572872 | tf_op jit(solution)/shard_map/ppermute | solution.py:213
  67.3 37.2 %copy-start.14 = (bf16[512,512]{1,0:T(8,128)(2,1)}, bf16[512,512]{1,0:T(8,128)(2,1)S(1)}, u32[]{:S(2)}) copy-start(bf16[512,512]{1,0:T(8,128)(2,1)S(1)} %collective-permute-done.3.refs_4_) | copy-start | bytes 1572868
  67.3 12.2 %collective-permute-start.5 = (bf16[512,512]{1,0:T(8,128)(2,1)S(1)}, bf16[512,512]{1,0:T(8,128)(2,1)S(1)}, u32[]{:S(2)}, u32[]{:S(2)}) collective-permute-start(bf16[512,512]{1,0:T(8,128)(2,1)S(1)} %collective-permute-done.3.refs_4_), channel_id=1, source_target_pairs={{0,7},{1,0},{2,1},{3,2},{4,3},{5,4},{6,5},{7,6},{8,15},{9,8},{10,9... | collective-permute-start | bytes 1572872 | tf_op jit(solution)/shard_map/ppermute | solution.py:214
  72.5 32.1 %copy-start.15 = (bf16[512,512]{1,0:T(8,128)(2,1)}, bf16[512,512]{1,0:T(8,128)(2,1)S(1)}, u32[]{:S(2)}) copy-start(bf16[512,512]{1,0:T(8,128)(2,1)S(1)} %collective-permute-done.2.refs_3_) | copy-start | bytes 1572868
  72.5 12.4 %collective-permute-start.4 = (bf16[512,512]{1,0:T(8,128)(2,1)S(1)}, bf16[512,512]{1,0:T(8,128)(2,1)S(1)}, u32[]{:S(2)}, u32[]{:S(2)}) collective-permute-start(bf16[512,512]{1,0:T(8,128)(2,1)S(1)} %collective-permute-done.2.refs_3_), channel_id=1, source_target_pairs={{0,1},{1,2},{2,3},{3,4},{4,5},{5,6},{6,7},{7,0},{8,9},{9,10},{10,1... | collective-permute-start | bytes 1572872 | tf_op jit(solution)/shard_map/ppermute | solution.py:213
  79.5 25.0 %copy-start.10 = (bf16[512,512]{1,0:T(8,128)(2,1)}, bf16[512,512]{1,0:T(8,128)(2,1)S(1)}, u32[]{:S(2)}) copy-start(bf16[512,512]{1,0:T(8,128)(2,1)S(1)} %collective-permute-done.5.refs_6_) | copy-start | bytes 1572868
  79.6 9.0 %collective-permute-start.7 = (bf16[256,512]{1,0:T(8,128)(2,1)S(1)}, bf16[256,512]{1,0:T(8,128)(2,1)}, u32[]{:S(2)}, u32[]{:S(2)}) collective-permute-start(bf16[256,512]{1,0:T(8,128)(2,1)S(1)} %slice.9), channel_id=1, source_target_pairs={{0,7},{1,0},{2,1},{3,2},{4,3},{5,4},{6,5},{7,6},{8,15},{9,8},{10,9... | collective-permute-start | bytes 786440 | tf_op jit(solution)/shard_map/ppermute | solution.py:215
  84.8 19.7 %copy-start.11 = (bf16[512,512]{1,0:T(8,128)(2,1)}, bf16[512,512]{1,0:T(8,128)(2,1)S(1)}, u32[]{:S(2)}) copy-start(bf16[512,512]{1,0:T(8,128)(2,1)S(1)} %collective-permute-done.4.refs_5_) | copy-start | bytes 1572868
  84.9 9.6 %collective-permute-start.6 = (bf16[256,512]{1,0:T(8,128)(2,1)S(1)}, bf16[256,512]{1,0:T(8,128)(2,1)}, u32[]{:S(2)}, u32[]{:S(2)}) collective-permute-start(bf16[256,512]{1,0:T(8,128)(2,1)S(1)} %slice.8), channel_id=1, source_target_pairs={{0,1},{1,2},{2,3},{3,4},{4,5},{5,6},{6,7},{7,0},{8,9},{9,10},{10,1... | collective-permute-start | bytes 786440 | tf_op jit(solution)/shard_map/ppermute | solution.py:215
  104.6 10.2 %copy-start.1 = (f32[224,512]{1,0:T(8,128)S(1)}, f32[224,512]{1,0:T(8,128)}, u32[]{:S(2)}) copy-start(f32[224,512]{1,0:T(8,128)} %master_ref.3) | copy-start | bytes 1376260
  104.6 10.2 %copy-start.2 = (f32[224,512]{1,0:T(8,128)S(1)}, f32[224,512]{1,0:T(8,128)}, u32[]{:S(2)}) copy-start(f32[224,512]{1,0:T(8,128)} %moment1_ref.3) | copy-start | bytes 1376260
  104.6 10.2 %copy-start.3 = (f32[224,512]{1,0:T(8,128)S(1)}, f32[224,512]{1,0:T(8,128)}, u32[]{:S(2)}) copy-start(f32[224,512]{1,0:T(8,128)} %moment2_ref.3) | copy-start | bytes 1376260
  110.8 3.9 %collective-permute-start.8 = (f32[232,512]{1,0:T(8,128)}, f32[232,512]{1,0:T(8,128)S(1)}, u32[]{:S(2)}, u32[]{:S(2)}) collective-permute-start(f32[232,512]{1,0:T(8,128)} %get-tuple-element.17), channel_id=1, source_target_pairs={{0,8},{8,0},{1,9},{9,1},{2,10},{10,2},{3,11},{11,3},{4,12},{12,4},... | collective-permute-start | bytes 1425416 | tf_op jit(solution)/shard_map/ppermute | solution.py:232
  114.8 1.0 copy-start.4
  115.8 0.7 copy-start.6
  116.5 21.1 %copy-start.5 = (f32[224,512]{1,0:T(8,128)S(1)}, f32[224,512]{1,0:T(8,128)}, u32[]{:S(2)}) copy-start(f32[224,512]{1,0:T(8,128)} %get-tuple-element.16.mine_ref) | copy-start | bytes 1376260
Sparse Core Ops, SparseCore 0:
  11.2 93.3 all-gather.2
  137.7 38.2 all-gather.4

commit v4 on v3

--- a/solution.py
+++ b/solution.py
@@ -24,7 +24,7 @@
 CAP = 114
 WIDTH = 512
 LANES = 128
-AHEAD = 3
+STEPS = (0, -1, 1, -2, 2, -3, 3, 4)
 SCALES = (1024.0, 64.0, 0.0625)
 
 VMEM = pl.BlockSpec(memory_space=pltpu.VMEM)
@@ -92,42 +92,53 @@
         fill(1)
 
 
-def partial_grad(me_ref, act_ref, *refs):
-    *parts, mine_ref, theirs_ref, slots_ref, cot_buf, act_buf, cot_sem, act_sem = refs
-    steps = [0, -1, 1, -2, 2, -3, 3, 4]
-    plans = []
-    for block, step in enumerate(steps):
-        index = lax.rem(me_ref[0] + (Y + step), Y)
-        plans.append([pltpu.make_async_copy(act_ref.at[:, index], act_buf.at[block], act_sem.at[block])])
+def turn(me_ref, *refs):
+    *parts, own_ref, other_ref, mine_ref, theirs_ref, tokens = refs
+    half = CHIPS // 2
     for number, ref in enumerate(parts):
-        block, start = min(number, Y - 1), PAD if number == Y else 0
-        target = cot_buf.at[block, pl.ds(start, ref.shape[0])]
-        plans[block].append(pltpu.make_async_copy(ref, target, cot_sem.at[number]))
-    for copies in plans[:AHEAD]:
-        for copy in copies:
-            copy.start()
-    total = None
-    for block, copies in enumerate(plans):
-        for copy in copies:
-            copy.wait()
-        for copy in plans[block + AHEAD] if block + AHEAD < Y else ():
-            copy.start()
-        act = act_buf[block].reshape(CHIPS * 16, WIDTH)
-        part = lax.dot_general(
-            cot_buf[block], act, (((0,), (0,)), ((), ())), preferred_element_type=jnp.float32
-        )
-        total = part if total is None else total + part
-    mine_ref[...] = total[:ROWS]
-    theirs_ref[:ROWS] = total[PAD : PAD + ROWS]
+        index = lax.rem(me_ref[0] + (Y + STEPS[(number + 1) // 2]), Y)
+        count = ref.shape[0] // 16
+        first = half * ((number + 1) % 2) if number else 0
+        tokens[first : first + count, index] = ref[...].reshape(count, 16, 2 * PAD)
+    own_ref[...] = tokens[:, :, :, :PAD].reshape(CHIPS * Y * 16, PAD).T[:ROWS]
+    other_ref[...] = tokens[:, :, :, PAD:].reshape(CHIPS * Y * 16, PAD).T[:ROWS]
 
     def received(start):
-        tile = cot_buf[0, :, start + LANES : start + PAD].astype(jnp.float32).reshape(CHIPS, 16, LANES)[:, 0]
+        tile = parts[0][:, start + LANES : start + PAD].astype(jnp.float32).reshape(CHIPS, 16, LANES)[:, 0]
         square = jnp.concatenate([tile, jnp.zeros((LANES - CHIPS, LANES), jnp.float32)], axis=0)
         return square.T[LANES - (PAD - ROWS) :][:8]
 
-    slots_ref[...] = received(0)
-    theirs_ref[ROWS:, :LANES] = received(PAD)
-    theirs_ref[ROWS:, LANES:] = jnp.zeros((8, WIDTH - LANES), jnp.float32)
+    mine_ref[...] = received(0)
+    theirs_ref[...] = received(PAD)
+
+
+def mine_grad(cot_ref, act_ref, out_ref):
+    out_ref[...] = jnp.dot(cot_ref[...], act_ref[...], preferred_element_type=jnp.float32)
+
+
+def theirs_grad(cot_ref, act_ref, slots_ref, out_ref):
+    out_ref[:ROWS] = jnp.dot(cot_ref[...], act_ref[...], preferred_element_type=jnp.float32)
+    out_ref[ROWS:, :LANES] = slots_ref[...]
+    out_ref[ROWS:, LANES:] = jnp.zeros((8, WIDTH - LANES), jnp.float32)
+
+
+def copy_columns(in_ref, out_ref, held, in_sem, out_sem):
+    copies = []
+    for part in range(Y):
+        columns = pl.ds(WIDTH * part, WIDTH)
+        copies.append(
+            (
+                pltpu.make_async_copy(in_ref.at[:, columns], held.at[part], in_sem.at[part]),
+                pltpu.make_async_copy(held.at[part], out_ref.at[:, columns], out_sem.at[part]),
+            )
+        )
+    for arrive, _ in copies:
+        arrive.start()
+    for arrive, leave in copies:
+        arrive.wait()
+        leave.start()
+    for _, leave in copies:
+        leave.wait()
 
 
 def update_state(mine_ref, theirs_ref, master_ref, moment1_ref, moment2_ref):
@@ -199,37 +210,34 @@
     dp_axes = ("z", "x", "c")
     core = lax.axis_index("c").astype(jnp.int32).reshape(1)
     packed, position = call(
-        pack_cotangent, (bf16(CHIPS, 16, 2 * PAD), int32(1, LANES)), [SMEM] + [VMEM] * 3, (VMEM,) * 2
+        pack_cotangent, (bf16(CHIPS, 16, 2 * PAD), int32(1, LANES)), [SMEM] + [VMEM] * 3, (VMEM,) * 2, limit=WIDE_LIMIT
     )(core, new_owner.reshape(1, PIECES), new_slot.reshape(1, PIECES), cotangent)
     shared = lax.all_to_all(packed, ("z", "x"), split_axis=0, concat_axis=0, tiled=True)
     shared = shared.reshape(CHIPS * 16, 2 * PAD)
 
-    act = lax.all_gather(activations, ("z", "x"), axis=0, tiled=True).reshape(CHIPS, Y, 16, WIDTH)
+    act = lax.all_gather(activations, ("z", "x"), axis=0, tiled=True)
 
     right = [(i, (i + 1) % Y) for i in range(Y)]
     left = [(i, (i - 1) % Y) for i in range(Y)]
-    down, up = [shared], [shared]
+    down, up = [[shared[:PAD], shared[PAD:]]], [[shared[:PAD], shared[PAD:]]]
     for _ in range(Y // 2 - 1):
-        down.append(lax.ppermute(down[-1], "y", right))
-        up.append(lax.ppermute(up[-1], "y", left))
-    far = [lax.ppermute(down[-1][:PAD], "y", right), lax.ppermute(up[-1][PAD:], "y", left)]
+        down.append([lax.ppermute(half, "y", right) for half in down[-1]])
+        up.append([lax.ppermute(half, "y", left) for half in up[-1]])
+    far = [lax.ppermute(down[-1][0], "y", right), lax.ppermute(up[-1][1], "y", left)]
+    parts = [shared] + [half for step in range(1, Y // 2) for way in (down, up) for half in way[step]] + far
 
     me = lax.axis_index("y").astype(jnp.int32).reshape(1)
-    mine, theirs, slots = call(
-        partial_grad,
-        (f32(ROWS, WIDTH), f32(ROWS + 8, WIDTH), f32(8, LANES)),
-        [SMEM] + [ANY] * 10,
-        (VMEM,) * 3,
-        flops=1 << 32,
-        limit=WIDE_LIMIT,
-        scratch_shapes=[
-            pltpu.VMEM((Y, CHIPS * 16, 2 * PAD), jnp.bfloat16),
-            pltpu.VMEM((Y, CHIPS, 16, WIDTH), jnp.bfloat16),
-            pltpu.SemaphoreType.DMA((Y + 1,)),
-            pltpu.SemaphoreType.DMA((Y,)),
-        ],
-    )(me, act, shared, down[1], up[1], down[2], up[2], down[3], up[3], *far)
+    turned, turned_theirs, slots, slots_theirs = call(
+        turn,
+        (bf16(ROWS, Y * CHIPS * 16),) * 2 + (f32(8, LANES),) * 2,
+        [SMEM] + [VMEM] * len(parts),
+        (VMEM,) * 4,
+        flops=1 << 28,
+        scratch_shapes=[pltpu.VMEM((CHIPS, Y, 16, 2 * PAD), jnp.bfloat16)],
+    )(me, *parts)
+    theirs = call(theirs_grad, f32(ROWS + 8, WIDTH), [VMEM] * 3, VMEM, flops=1 << 31)(turned_theirs, act, slots_theirs)
     theirs = lax.ppermute(theirs, "c", [(0, 1), (1, 0)])
+    mine = call(mine_grad, f32(ROWS, WIDTH), [VMEM] * 2, VMEM, flops=1 << 31)(turned, act)
     step = (position, mine, theirs, master, first_moment, second_moment)
     weights, slots = call(
         step_weights,
@@ -248,6 +256,18 @@
         scratch_shapes=[pltpu.VMEM((CAP + 1, PAIR, WIDTH), jnp.float32)],
     )(slots, weights)
     new_weights = lax.all_gather(weights, "y", axis=1, tiled=True)
+    new_weights = call(
+        copy_columns,
+        bf16(*new_weights.shape),
+        [ANY],
+        ANY,
+        limit=WIDE_LIMIT,
+        scratch_shapes=[
+            pltpu.VMEM((Y, PAIR * CAP, WIDTH), jnp.bfloat16),
+            pltpu.SemaphoreType.DMA((Y,)),
+            pltpu.SemaphoreType.DMA((Y,)),
+        ],
+    )(new_weights)
 
     states = call(
         step_states,

time: 187 us -> 183 us (0.979)
  waiting for transfers between devices: 46.1 us -> 17.3 us
  starting transfers between devices: 26.5 us -> 48.7 us
  Pallas kernels: 12.7 us -> 15.7 us
    ppermute x8 -> x14, starting transfers between devices: 24.5 us -> 46.7 us  [the longest x6 22.8 us: shards(): down.append([lax.ppermute(half, 'y', right) for half in down[-1]])]
    ppermute x8 -> x14, waiting for transfers between devices: 27.4 us -> 6.56 us  [the longest x1 4.04 us: shards(): lax.ppermute(up[-1][1], 'y', left)]
    all_gather x1, waiting for transfers between devices: 10.1 us -> 3.45 us  [shards(): act = lax.all_gather(activations, ('z', 'x'), axis=0, tiled=True)]
    pallas_call x1 -> x4, Pallas kernels: 6.2 us -> 7.3 us  [the longest x1 2.61 us: shards(): call(turn, (bf16(ROWS, Y * CHIPS * 16),) * 2 + (f32(8, LANES),) * 2, [SME...]
    unnamed x33 -> x18, local copies, waits for them, and re-layouts: 7.04 us -> 6.22 us
  transfers between devices with their start and end apart: 11 -> 17, of which waited for: 11 -> 6; matrix products, arithmetic and copies ran while one was open for 1% -> 1% of each run, Pallas kernels for 2% -> 5%
where the time goes in v4:
time: 183 us; the launch traced here: 182 us
  blocking collectives  78.4 us (43%)
  starting transfers between devices  48.7 us (27%)
  waiting for transfers between devices  17.3 us (9%)
  Pallas kernels  15.7 us (9%)
  between operations  14.4 us (8%)
  local copies, waits for them, and re-layouts  6.26 us (3%)
    all_to_all x1, blocking collectives, shards(): lax.all_to_all(packed, ('z', 'x'), split_axis=0, concat_axis=0, tiled=True)  31.9 us
    all_to_all x1, blocking collectives, shards(): lax.all_to_all(states, dp_axes, split_axis=0, concat_axis=0, tiled=True)  28 us
    ppermute x6, starting transfers between devices, shards(): down.append([lax.ppermute(half, 'y', right) for half in down[-1]])  22.8 us
    all_to_all x1, blocking collectives, shards(): lax.all_to_all(weights, dp_axes, split_axis=0, concat_axis=0, tiled=True)  18.5 us
    ppermute x6, starting transfers between devices, shards(): up.append([lax.ppermute(half, 'y', left) for half in up[-1]])  16.9 us
    unnamed x18, local copies, waits for them, and re-layouts  6.22 us
    all_gather x1, waiting for transfers between devices, shards(): new_weights = lax.all_gather(weights, 'y', axis=1, tiled=True)  5.97 us
    ppermute x1, waiting for transfers between devices, shards(): lax.ppermute(up[-1][1], 'y', left)  4.04 us
  transfers between devices with their start and end apart: 17, of which 6 were waited for; matrix products, arithmetic and copies ran while one was open for 1% of the time, Pallas kernels for 5%

profile of v4, /device:TPU:8, one launch (start us, length us, event | category | flops | bytes accessed | tf_op | source)
XLA Modules:
  0.0 181.8 jit_solution(1021277151522432693)
XLA Ops:
  7.2 0.0 all-gather.3.cloned.1.call-start
  7.2 0.7 all-gather.3.cloned.1.call-update
  7.9 0.0 all-gather.5.cloned.1.call-start
  8.0 2.4 %shard_map.102 = (bf16[32,16,512]{2,1,0:T(8,128)(2,1)}, s32[1,128]{1,0:T(1,128)}) custom-call(s32[1]{0:T(128)} %bitcast.core_ref, s32[1,112]{1,0:T(1,128)} %bitcast.12, s32[1,112]{1,0:T(1,128)} %bitcast.13, bf16[16,14336]{1,0:T(8,128)(2,1)} %cot_ref.1), custom_call_target="tpu_custom_call" | custom-call | bytes 4194304 | tf_op jit(solution)/shard_map/pallas_call | solution.py:212
  10.4 31.9 %all_to_all.15 = bf16[32,16,512]{2,1,0:T(8,128)(2,1)S(1)} all-to-all(bf16[32,16,512]{2,1,0:T(8,128)(2,1)} %get-tuple-element.16), channel_id=1, replica_groups=mesh['z'=8,'x'=4,'c'=2,'y'=8] {'z','x'}, dimensions={0} | all-to-all | bytes 1048576 | tf_op jit(solution)/shard_map/all_to_all | solution.py:215
  42.3 3.5 %collective-permute-start = (bf16[256,512]{1,0:T(8,128)(2,1)S(1)}, bf16[256,512]{1,0:T(8,128)(2,1)S(1)}, u32[]{:S(2)}, u32[]{:S(2)}) collective-permute-start(bf16[256,512]{1,0:T(8,128)(2,1)S(1)} %bitcast.8), channel_id=1, source_target_pairs={{0,1},{1,2},{2,3},{3,4},{4,5},{5,6},{6,7},{7,0},{8,9},{9,10},{10,1... | collective-permute-start | bytes 786440 | tf_op jit(solution)/shard_map/ppermute | solution.py:224
  45.8 2.4 %collective-permute-start.3 = (bf16[256,512]{1,0:T(8,128)(2,1)S(1)}, bf16[256,512]{1,0:T(8,128)(2,1)S(1)}, u32[]{:S(2)}, u32[]{:S(2)}) collective-permute-start(bf16[256,512]{1,0:T(8,128)(2,1)S(1)} %bitcast.10), channel_id=1, source_target_pairs={{0,7},{1,0},{2,1},{3,2},{4,3},{5,4},{6,5},{7,6},{8,15},{9,8},{10,9... | collective-permute-start | bytes 786440 | tf_op jit(solution)/shard_map/ppermute | solution.py:225
  48.2 3.5 %collective-permute-start.1 = (bf16[256,512]{1,0:T(8,128)(2,1)S(1)}, bf16[256,512]{1,0:T(8,128)(2,1)S(1)}, u32[]{:S(2)}, u32[]{:S(2)}) collective-permute-start(bf16[256,512]{1,0:T(8,128)(2,1)S(1)} %bitcast.11), channel_id=1, source_target_pairs={{0,1},{1,2},{2,3},{3,4},{4,5},{5,6},{6,7},{7,0},{8,9},{9,10},{10,1... | collective-permute-start | bytes 786440 | tf_op jit(solution)/shard_map/ppermute | solution.py:224
  51.6 2.4 %collective-permute-start.2 = (bf16[256,512]{1,0:T(8,128)(2,1)S(1)}, bf16[256,512]{1,0:T(8,128)(2,1)S(1)}, u32[]{:S(2)}, u32[]{:S(2)}) collective-permute-start(bf16[256,512]{1,0:T(8,128)(2,1)S(1)} %bitcast.9), channel_id=1, source_target_pairs={{0,7},{1,0},{2,1},{3,2},{4,3},{5,4},{6,5},{7,6},{8,15},{9,8},{10,9... | collective-permute-start | bytes 786440 | tf_op jit(solution)/shard_map/ppermute | solution.py:225
  54.0 0.0 collective-permute-done.refs_1_
  54.0 3.8 %collective-permute-start.4 = (bf16[256,512]{1,0:T(8,128)(2,1)S(1)}, bf16[256,512]{1,0:T(8,128)(2,1)S(1)}, u32[]{:S(2)}, u32[]{:S(2)}) collective-permute-start(bf16[256,512]{1,0:T(8,128)(2,1)S(1)} %collective-permute-done.refs_1_), channel_id=1, source_target_pairs={{0,1},{1,2},{2,3},{3,4},{4,5},{5,6},{6,7},{7,0},{8,9},{9,10},{10,1... | collective-permute-start | bytes 786440 | tf_op jit(solution)/shard_map/ppermute | solution.py:224
  57.8 0.0 collective-permute-done.3.refs_4_
  57.8 3.0 %collective-permute-start.7 = (bf16[256,512]{1,0:T(8,128)(2,1)S(1)}, bf16[256,512]{1,0:T(8,128)(2,1)S(1)}, u32[]{:S(2)}, u32[]{:S(2)}) collective-permute-start(bf16[256,512]{1,0:T(8,128)(2,1)S(1)} %collective-permute-done.3.refs_4_), channel_id=1, source_target_pairs={{0,7},{1,0},{2,1},{3,2},{4,3},{5,4},{6,5},{7,6},{8,15},{9,8},{10,9... | collective-permute-start | bytes 786440 | tf_op jit(solution)/shard_map/ppermute | solution.py:225
  60.9 0.0 collective-permute-done.1.refs_2_
  60.9 4.0 %collective-permute-start.5 = (bf16[256,512]{1,0:T(8,128)(2,1)S(1)}, bf16[256,512]{1,0:T(8,128)(2,1)S(1)}, u32[]{:S(2)}, u32[]{:S(2)}) collective-permute-start(bf16[256,512]{1,0:T(8,128)(2,1)S(1)} %collective-permute-done.1.refs_2_), channel_id=1, source_target_pairs={{0,1},{1,2},{2,3},{3,4},{4,5},{5,6},{6,7},{7,0},{8,9},{9,10},{10,1... | collective-permute-start | bytes 786440 | tf_op jit(solution)/shard_map/ppermute | solution.py:224
  64.9 0.0 collective-permute-done.2.refs_3_
  64.9 3.0 %collective-permute-start.6 = (bf16[256,512]{1,0:T(8,128)(2,1)S(1)}, bf16[256,512]{1,0:T(8,128)(2,1)S(1)}, u32[]{:S(2)}, u32[]{:S(2)}) collective-permute-start(bf16[256,512]{1,0:T(8,128)(2,1)S(1)} %collective-permute-done.2.refs_3_), channel_id=1, source_target_pairs={{0,7},{1,0},{2,1},{3,2},{4,3},{5,4},{6,5},{7,6},{8,15},{9,8},{10,9... | collective-permute-start | bytes 786440 | tf_op jit(solution)/shard_map/ppermute | solution.py:225
  67.9 0.0 collective-permute-done.4.refs_5_
  68.0 4.0 %collective-permute-start.8 = (bf16[256,512]{1,0:T(8,128)(2,1)S(1)}, bf16[256,512]{1,0:T(8,128)(2,1)S(1)}, u32[]{:S(2)}, u32[]{:S(2)}) collective-permute-start(bf16[256,512]{1,0:T(8,128)(2,1)S(1)} %collective-permute-done.4.refs_5_), channel_id=1, source_target_pairs={{0,1},{1,2},{2,3},{3,4},{4,5},{5,6},{6,7},{7,0},{8,9},{9,10},{10,1... | collective-permute-start | bytes 786440 | tf_op jit(solution)/shard_map/ppermute | solution.py:224
  72.0 0.0 collective-permute-done.7.refs_8_
  72.0 3.0 %collective-permute-start.11 = (bf16[256,512]{1,0:T(8,128)(2,1)S(1)}, bf16[256,512]{1,0:T(8,128)(2,1)S(1)}, u32[]{:S(2)}, u32[]{:S(2)}) collective-permute-start(bf16[256,512]{1,0:T(8,128)(2,1)S(1)} %collective-permute-done.7.refs_8_), channel_id=1, source_target_pairs={{0,7},{1,0},{2,1},{3,2},{4,3},{5,4},{6,5},{7,6},{8,15},{9,8},{10,9... | collective-permute-start | bytes 786440 | tf_op jit(solution)/shard_map/ppermute | solution.py:225
  75.0 0.0 collective-permute-done.5.refs_6_
  75.0 4.0 %collective-permute-start.9 = (bf16[256,512]{1,0:T(8,128)(2,1)S(1)}, bf16[256,512]{1,0:T(8,128)(2,1)S(1)}, u32[]{:S(2)}, u32[]{:S(2)}) collective-permute-start(bf16[256,512]{1,0:T(8,128)(2,1)S(1)} %collective-permute-done.5.refs_6_), channel_id=1, source_target_pairs={{0,1},{1,2},{2,3},{3,4},{4,5},{5,6},{6,7},{7,0},{8,9},{9,10},{10,1... | collective-permute-start | bytes 786440 | tf_op jit(solution)/shard_map/ppermute | solution.py:224
  79.1 0.0 collective-permute-done.6.refs_7_
  79.1 3.0 %collective-permute-start.10 = (bf16[256,512]{1,0:T(8,128)(2,1)S(1)}, bf16[256,512]{1,0:T(8,128)(2,1)}, u32[]{:S(2)}, u32[]{:S(2)}) collective-permute-start(bf16[256,512]{1,0:T(8,128)(2,1)S(1)} %collective-permute-done.6.refs_7_), channel_id=1, source_target_pairs={{0,7},{1,0},{2,1},{3,2},{4,3},{5,4},{6,5},{7,6},{8,15},{9,8},{10,9... | collective-permute-start | bytes 786440 | tf_op jit(solution)/shard_map/ppermute | solution.py:225
  82.1 0.0 collective-permute-done.8.refs_9_
  82.1 4.0 %collective-permute-start.12 = (bf16[256,512]{1,0:T(8,128)(2,1)S(1)}, bf16[256,512]{1,0:T(8,128)(2,1)}, u32[]{:S(2)}, u32[]{:S(2)}) collective-permute-start(bf16[256,512]{1,0:T(8,128)(2,1)S(1)} %collective-permute-done.8.refs_9_), channel_id=1, source_target_pairs={{0,1},{1,2},{2,3},{3,4},{4,5},{5,6},{6,7},{7,0},{8,9},{9,10},{10,1... | collective-permute-start | bytes 786440 | tf_op jit(solution)/shard_map/ppermute | solution.py:226
  86.2 0.0 collective-permute-done.11.refs_12_
  86.2 3.0 %collective-permute-start.13 = (bf16[256,512]{1,0:T(8,128)(2,1)S(1)}, bf16[256,512]{1,0:T(8,128)(2,1)}, u32[]{:S(2)}, u32[]{:S(2)}) collective-permute-start(bf16[256,512]{1,0:T(8,128)(2,1)S(1)} %collective-permute-done.11.refs_12_), channel_id=1, source_target_pairs={{0,7},{1,0},{2,1},{3,2},{4,3},{5,4},{6,5},{7,6},{8,15},{9,8},{10,9... | collective-permute-start | bytes 786440 | tf_op jit(solution)/shard_map/ppermute | solution.py:226
  89.2 0.0 collective-permute-done.9.refs_10_
  89.2 2.1 %collective-permute-done.10.refs_11_ = bf16[256,512]{1,0:T(8,128)(2,1)} collective-permute-done((bf16[256,512]{1,0:T(8,128)(2,1)S(1)}, bf16[256,512]{1,0:T(8,128)(2,1)}, u32[]{:S(2)}, u32[]{:S(2)}) %collective-permute-start.10) | collective-permute-done | bytes 262176 | tf_op jit(solution)/shard_map/ppermute | solution.py:225
  91.3 0.4 collective-permute-done.12.refs_13_
  91.7 4.0 %collective-permute-done.13.refs_14_ = bf16[256,512]{1,0:T(8,128)(2,1)} collective-permute-done((bf16[256,512]{1,0:T(8,128)(2,1)S(1)}, bf16[256,512]{1,0:T(8,128)(2,1)}, u32[]{:S(2)}, u32[]{:S(2)}) %collective-permute-start.13) | collective-permute-done | bytes 262176 | tf_op jit(solution)/shard_map/ppermute | solution.py:226
  95.8 2.6 %shard_map.103 = (bf16[224,4096]{1,0:T(8,128)(2,1)S(1)}, bf16[224,4096]{1,0:T(8,128)(2,1)S(1)}, f32[8,128]{1,0:T(8,128)S(1)}, f32[8,128]{1,0:T(8,128)S(1)}) custom-call(s32[1]{0:T(128)} %bitcast.3.me_ref, bf16[512,512]{1,0:T(8,128)(2,1)S(1)} %bitcast.7, bf16[256,512]{1,0:T(8,128)(2,1)S(1)} %collective-permute-done.refs_1_, ...), custom_call_target="tpu_custom_call" | custom-call | flops 268435456 | bytes 4194304 | tf_op jit(solution)/shard_map/pallas_call | solution.py:230
  98.4 0.0 copy-start.5
  98.4 1.2 copy-done.5
  99.6 1.3 copy-done.7
  100.9 3.4 %all-gather.3.cloned.1.call-done.act_ref = bf16[4096,512]{1,0:T(8,128)(2,1)} async-done(((bf16[128,512]{1,0:T(8,128)(2,1)}), bf16[4096,512]{1,0:T(8,128)(2,1)}) %all-gather.3.cloned.1.call-update) | async-done | bytes 4194320 | tf_op jit(solution)/shard_map/all_gather | solution.py:218
  104.3 2.2 %copy-done.4 = bf16[4096,512]{1,0:T(8,128)(2,1)S(1)} copy-done((bf16[4096,512]{1,0:T(8,128)(2,1)S(1)}, bf16[4096,512]{1,0:T(8,128)(2,1)}, u32[]{:S(2)}) %copy-start.4) | copy-done | bytes 4194328
  106.5 1.5 copy-done.8
  108.0 1.1 shard_map.105
  109.2 1.9 %collective-permute-start.14 = (f32[232,512]{1,0:T(8,128)S(1)}, f32[232,512]{1,0:T(8,128)S(1)}, u32[]{:S(2)}, u32[]{:S(2)}) collective-permute-start(f32[232,512]{1,0:T(8,128)S(1)} %shard_map.105), channel_id=1, source_target_pairs={{0,8},{8,0},{1,9},{9,1},{2,10},{10,2},{3,11},{11,3},{4,12},{12,4},... | collective-permute-start | bytes 1425416 | tf_op jit(solution)/shard_map/ppermute | solution.py:239
  111.1 0.0 copy-done.6
  111.1 0.0 copy-start
  111.1 0.0 copy-start.1
  111.1 0.0 copy-start.2
  111.2 0.0 copy-start.3
  111.2 1.1 shard_map.104.mine_ref
  112.3 0.6 collective-permute-done.14.theirs_ref
  112.9 0.0 copy-done
  112.9 0.0 copy-done.1
  112.9 0.0 copy-done.2
  112.9 0.0 copy-done.3
  112.9 1.2 shard_map.106
  114.1 18.5 %all_to_all.16.arrived_ref = bf16[128,2,512]{2,1,0:T(2,128)(2,1)S(1)} all-to-all(bf16[128,2,512]{2,1,0:T(2,128)(2,1)S(1)} %get-tuple-element.22), channel_id=1, replica_groups=mesh['z'=8,'x'=4,'c'=2,'y'=8] {'z','x','c'}, dimensions={0} | all-to-all | bytes 524288 | tf_op jit(solution)/shard_map/all_to_all | solution.py:250
  132.6 1.4 shard_map.108.after_ref
  134.0 0.0 all-gather.5.cloned.1.call-update
  134.1 1.4 shard_map.107.value_ref
  135.5 0.5 convert_element_type.6
  136.0 28.0 %all_to_all.17 = f16[128,2,1536]{2,1,0:T(2,128)(2,1)S(1)} all-to-all(f16[128,2,1536]{2,1,0:T(2,128)(2,1)S(1)} %convert_element_type.6), channel_id=1, replica_groups=mesh['z'=8,'x'=4,'c'=2,'y'=8] {'z','x','c'}, dimensions={0} | all-to-all | bytes 1572864 | tf_op jit(solution)/shard_map/all_to_all | solution.py:282
  164.0 0.5 convert_element_type.7.arrived_ref
  164.6 2.0 %shard_map.110 = (f32[228,512]{1,0:T(8,128)}, f32[228,512]{1,0:T(8,128)}, f32[228,512]{1,0:T(8,128)}) custom-call(s32[4,128]{1,0:T(4,128)S(1)} %get-tuple-element.21.slot_ref, f32[128,2,1536]{2,1,0:T(2,128)S(1)} %convert_element_type.7.arrived_ref), custom_call_target="tpu_custom_call" | custom-call | bytes 4194304 | tf_op jit(solution)/shard_map/pallas_call | solution.py:283
  166.5 6.0 %all-gather.5.cloned.1.call-done.in_ref = bf16[228,4096]{1,0:T(8,128)(2,1)} async-done(((bf16[228,512]{1,0:T(8,128)(2,1)}), bf16[228,4096]{1,0:T(8,128)(2,1)}) %all-gather.5.cloned.1.call-update) | async-done | bytes 1867792 | tf_op jit(solution)/shard_map/all_gather | solution.py:258
  172.5 2.4 %shard_map.111 = bf16[228,4096]{1,0:T(8,128)(2,1)} custom-call(bf16[228,4096]{1,0:T(8,128)(2,1)} %all-gather.5.cloned.1.call-done.in_ref), custom_call_target="tpu_custom_call" | custom-call | bytes 4194304 | tf_op jit(solution)/shard_map/pallas_call | solution.py:259
  (6 shorter events, 0.0 us)
Async XLA Ops:
  7.2 97.2 %all-gather.3.cloned.1.call-start = ((), (), s32[]{:S(2)}) async-start(), calls=%async_computation.3 | async-start | bytes 4325376 | tf_op jit(solution)/shard_map/all_gather | solution.py:218
  7.9 164.6 %all-gather.5.cloned.1.call-start = ((), (), s32[]{:S(2)}) async-start(), calls=%async_computation.4 | async-start | bytes 2138112 | tf_op jit(solution)/shard_map/all_gather | solution.py:258
  42.3 11.7 %collective-permute-start = (bf16[256,512]{1,0:T(8,128)(2,1)S(1)}, bf16[256,512]{1,0:T(8,128)(2,1)S(1)}, u32[]{:S(2)}, u32[]{:S(2)}) collective-permute-start(bf16[256,512]{1,0:T(8,128)(2,1)S(1)} %bitcast.8), channel_id=1, source_target_pairs={{0,1},{1,2},{2,3},{3,4},{4,5},{5,6},{6,7},{7,0},{8,9},{9,10},{10,1... | collective-permute-start | bytes 786440 | tf_op jit(solution)/shard_map/ppermute | solution.py:224
  45.8 12.0 %collective-permute-start.3 = (bf16[256,512]{1,0:T(8,128)(2,1)S(1)}, bf16[256,512]{1,0:T(8,128)(2,1)S(1)}, u32[]{:S(2)}, u32[]{:S(2)}) collective-permute-start(bf16[256,512]{1,0:T(8,128)(2,1)S(1)} %bitcast.10), channel_id=1, source_target_pairs={{0,7},{1,0},{2,1},{3,2},{4,3},{5,4},{6,5},{7,6},{8,15},{9,8},{10,9... | collective-permute-start | bytes 786440 | tf_op jit(solution)/shard_map/ppermute | solution.py:225
  48.2 12.7 %collective-permute-start.1 = (bf16[256,512]{1,0:T(8,128)(2,1)S(1)}, bf16[256,512]{1,0:T(8,128)(2,1)S(1)}, u32[]{:S(2)}, u32[]{:S(2)}) collective-permute-start(bf16[256,512]{1,0:T(8,128)(2,1)S(1)} %bitcast.11), channel_id=1, source_target_pairs={{0,1},{1,2},{2,3},{3,4},{4,5},{5,6},{6,7},{7,0},{8,9},{9,10},{10,1... | collective-permute-start | bytes 786440 | tf_op jit(solution)/shard_map/ppermute | solution.py:224
  51.6 13.3 %collective-permute-start.2 = (bf16[256,512]{1,0:T(8,128)(2,1)S(1)}, bf16[256,512]{1,0:T(8,128)(2,1)S(1)}, u32[]{:S(2)}, u32[]{:S(2)}) collective-permute-start(bf16[256,512]{1,0:T(8,128)(2,1)S(1)} %bitcast.9), channel_id=1, source_target_pairs={{0,7},{1,0},{2,1},{3,2},{4,3},{5,4},{6,5},{7,6},{8,15},{9,8},{10,9... | collective-permute-start | bytes 786440 | tf_op jit(solution)/shard_map/ppermute | solution.py:225
  54.0 13.9 %collective-permute-start.4 = (bf16[256,512]{1,0:T(8,128)(2,1)S(1)}, bf16[256,512]{1,0:T(8,128)(2,1)S(1)}, u32[]{:S(2)}, u32[]{:S(2)}) collective-permute-start(bf16[256,512]{1,0:T(8,128)(2,1)S(1)} %collective-permute-done.refs_1_), channel_id=1, source_target_pairs={{0,1},{1,2},{2,3},{3,4},{4,5},{5,6},{6,7},{7,0},{8,9},{9,10},{10,1... | collective-permute-start | bytes 786440 | tf_op jit(solution)/shard_map/ppermute | solution.py:224
  57.8 14.2 %collective-permute-start.7 = (bf16[256,512]{1,0:T(8,128)(2,1)S(1)}, bf16[256,512]{1,0:T(8,128)(2,1)S(1)}, u32[]{:S(2)}, u32[]{:S(2)}) collective-permute-start(bf16[256,512]{1,0:T(8,128)(2,1)S(1)} %collective-permute-done.3.refs_4_), channel_id=1, source_target_pairs={{0,7},{1,0},{2,1},{3,2},{4,3},{5,4},{6,5},{7,6},{8,15},{9,8},{10,9... | collective-permute-start | bytes 786440 | tf_op jit(solution)/shard_map/ppermute | solution.py:225
  60.9 14.2 %collective-permute-start.5 = (bf16[256,512]{1,0:T(8,128)(2,1)S(1)}, bf16[256,512]{1,0:T(8,128)(2,1)S(1)}, u32[]{:S(2)}, u32[]{:S(2)}) collective-permute-start(bf16[256,512]{1,0:T(8,128)(2,1)S(1)} %collective-permute-done.1.refs_2_), channel_id=1, source_target_pairs={{0,1},{1,2},{2,3},{3,4},{4,5},{5,6},{6,7},{7,0},{8,9},{9,10},{10,1... | collective-permute-start | bytes 786440 | tf_op jit(solution)/shard_map/ppermute | solution.py:224
  64.9 14.2 %collective-permute-start.6 = (bf16[256,512]{1,0:T(8,128)(2,1)S(1)}, bf16[256,512]{1,0:T(8,128)(2,1)S(1)}, u32[]{:S(2)}, u32[]{:S(2)}) collective-permute-start(bf16[256,512]{1,0:T(8,128)(2,1)S(1)} %collective-permute-done.2.refs_3_), channel_id=1, source_target_pairs={{0,7},{1,0},{2,1},{3,2},{4,3},{5,4},{6,5},{7,6},{8,15},{9,8},{10,9... | collective-permute-start | bytes 786440 | tf_op jit(solution)/shard_map/ppermute | solution.py:225
  68.0 14.2 %collective-permute-start.8 = (bf16[256,512]{1,0:T(8,128)(2,1)S(1)}, bf16[256,512]{1,0:T(8,128)(2,1)S(1)}, u32[]{:S(2)}, u32[]{:S(2)}) collective-permute-start(bf16[256,512]{1,0:T(8,128)(2,1)S(1)} %collective-permute-done.4.refs_5_), channel_id=1, source_target_pairs={{0,1},{1,2},{2,3},{3,4},{4,5},{5,6},{6,7},{7,0},{8,9},{9,10},{10,1... | collective-permute-start | bytes 786440 | tf_op jit(solution)/shard_map/ppermute | solution.py:224
  72.0 14.2 %collective-permute-start.11 = (bf16[256,512]{1,0:T(8,128)(2,1)S(1)}, bf16[256,512]{1,0:T(8,128)(2,1)S(1)}, u32[]{:S(2)}, u32[]{:S(2)}) collective-permute-start(bf16[256,512]{1,0:T(8,128)(2,1)S(1)} %collective-permute-done.7.refs_8_), channel_id=1, source_target_pairs={{0,7},{1,0},{2,1},{3,2},{4,3},{5,4},{6,5},{7,6},{8,15},{9,8},{10,9... | collective-permute-start | bytes 786440 | tf_op jit(solution)/shard_map/ppermute | solution.py:225
  75.0 14.2 %collective-permute-start.9 = (bf16[256,512]{1,0:T(8,128)(2,1)S(1)}, bf16[256,512]{1,0:T(8,128)(2,1)S(1)}, u32[]{:S(2)}, u32[]{:S(2)}) collective-permute-start(bf16[256,512]{1,0:T(8,128)(2,1)S(1)} %collective-permute-done.5.refs_6_), channel_id=1, source_target_pairs={{0,1},{1,2},{2,3},{3,4},{4,5},{5,6},{6,7},{7,0},{8,9},{9,10},{10,1... | collective-permute-start | bytes 786440 | tf_op jit(solution)/shard_map/ppermute | solution.py:224
  79.1 12.2 %collective-permute-start.10 = (bf16[256,512]{1,0:T(8,128)(2,1)S(1)}, bf16[256,512]{1,0:T(8,128)(2,1)}, u32[]{:S(2)}, u32[]{:S(2)}) collective-permute-start(bf16[256,512]{1,0:T(8,128)(2,1)S(1)} %collective-permute-done.6.refs_7_), channel_id=1, source_target_pairs={{0,7},{1,0},{2,1},{3,2},{4,3},{5,4},{6,5},{7,6},{8,15},{9,8},{10,9... | collective-permute-start | bytes 786440 | tf_op jit(solution)/shard_map/ppermute | solution.py:225
  82.1 9.6 %collective-permute-start.12 = (bf16[256,512]{1,0:T(8,128)(2,1)S(1)}, bf16[256,512]{1,0:T(8,128)(2,1)}, u32[]{:S(2)}, u32[]{:S(2)}) collective-permute-start(bf16[256,512]{1,0:T(8,128)(2,1)S(1)} %collective-permute-done.8.refs_9_), channel_id=1, source_target_pairs={{0,1},{1,2},{2,3},{3,4},{4,5},{5,6},{6,7},{7,0},{8,9},{9,10},{10,1... | collective-permute-start | bytes 786440 | tf_op jit(solution)/shard_map/ppermute | solution.py:226
  86.2 9.6 %collective-permute-start.13 = (bf16[256,512]{1,0:T(8,128)(2,1)S(1)}, bf16[256,512]{1,0:T(8,128)(2,1)}, u32[]{:S(2)}, u32[]{:S(2)}) collective-permute-start(bf16[256,512]{1,0:T(8,128)(2,1)S(1)} %collective-permute-done.11.refs_12_), channel_id=1, source_target_pairs={{0,7},{1,0},{2,1},{3,2},{4,3},{5,4},{6,5},{7,6},{8,15},{9,8},{10,9... | collective-permute-start | bytes 786440 | tf_op jit(solution)/shard_map/ppermute | solution.py:226
  98.4 1.2 copy-start.5
  99.6 1.3 copy-start.7
  104.3 2.2 %copy-start.4 = (bf16[4096,512]{1,0:T(8,128)(2,1)S(1)}, bf16[4096,512]{1,0:T(8,128)(2,1)}, u32[]{:S(2)}) copy-start(bf16[4096,512]{1,0:T(8,128)(2,1)} %all-gather.3.cloned.1.call-done.act_ref) | copy-start | bytes 12582916
  106.5 1.5 copy-start.8
  108.0 3.1 %copy-start.6 = (bf16[224,4096]{1,0:T(8,128)(2,1)S(1)}, bf16[224,4096]{1,0:T(8,128)(2,1)}, u32[]{:S(2)}) copy-start(bf16[224,4096]{1,0:T(8,128)(2,1)} %copy-done.5) | copy-start | bytes 5505028
  109.2 3.7 %collective-permute-start.14 = (f32[232,512]{1,0:T(8,128)S(1)}, f32[232,512]{1,0:T(8,128)S(1)}, u32[]{:S(2)}, u32[]{:S(2)}) collective-permute-start(f32[232,512]{1,0:T(8,128)S(1)} %shard_map.105), channel_id=1, source_target_pairs={{0,8},{8,0},{1,9},{9,1},{2,10},{10,2},{3,11},{11,3},{4,12},{12,4},... | collective-permute-start | bytes 1425416 | tf_op jit(solution)/shard_map/ppermute | solution.py:239
  111.1 1.8 copy-start
  111.1 1.8 copy-start.1
  111.1 1.8 copy-start.2
  111.2 1.8 copy-start.3
Sparse Core Ops, SparseCore 0:
  11.2 93.1 all-gather.2
  134.2 38.2 all-gather.4

commit v5 on v4

--- a/solution.py
+++ b/solution.py
@@ -24,6 +24,7 @@
 CAP = 114
 WIDTH = 512
 LANES = 128
+STRIPS = 4
 STEPS = (0, -1, 1, -2, 2, -3, 3, 4)
 SCALES = (1024.0, 64.0, 0.0625)
 
@@ -94,14 +95,16 @@
 
 def turn(me_ref, *refs):
     *parts, own_ref, other_ref, mine_ref, theirs_ref, tokens = refs
-    half = CHIPS // 2
+    half = Z // 2
     for number, ref in enumerate(parts):
         index = lax.rem(me_ref[0] + (Y + STEPS[(number + 1) // 2]), Y)
-        count = ref.shape[0] // 16
+        count = ref.shape[0] // (X * 16)
         first = half * ((number + 1) % 2) if number else 0
-        tokens[first : first + count, index] = ref[...].reshape(count, 16, 2 * PAD)
-    own_ref[...] = tokens[:, :, :, :PAD].reshape(CHIPS * Y * 16, PAD).T[:ROWS]
-    other_ref[...] = tokens[:, :, :, PAD:].reshape(CHIPS * Y * 16, PAD).T[:ROWS]
+        block = ref[...].reshape(count, X, 16, 2 * PAD)
+        for z in range(count):
+            tokens[:, first + z, index] = block[z]
+    own_ref[...] = tokens[:, :, :, :, :PAD].reshape(CHIPS * Y * 16, PAD).T[:ROWS]
+    other_ref[...] = tokens[:, :, :, :, PAD:].reshape(CHIPS * Y * 16, PAD).T[:ROWS]
 
     def received(start):
         tile = parts[0][:, start + LANES : start + PAD].astype(jnp.float32).reshape(CHIPS, 16, LANES)[:, 0]
@@ -124,8 +127,9 @@
 
 def copy_columns(in_ref, out_ref, held, in_sem, out_sem):
     copies = []
-    for part in range(Y):
-        columns = pl.ds(WIDTH * part, WIDTH)
+    for part in range(STRIPS):
+        width = in_ref.shape[1] // STRIPS
+        columns = pl.ds(width * part, width)
         copies.append(
             (
                 pltpu.make_async_copy(in_ref.at[:, columns], held.at[part], in_sem.at[part]),
@@ -215,7 +219,7 @@
     shared = lax.all_to_all(packed, ("z", "x"), split_axis=0, concat_axis=0, tiled=True)
     shared = shared.reshape(CHIPS * 16, 2 * PAD)
 
-    act = lax.all_gather(activations, ("z", "x"), axis=0, tiled=True)
+    act = lax.all_gather(activations, ("x", "z"), axis=0, tiled=True)
 
     right = [(i, (i + 1) % Y) for i in range(Y)]
     left = [(i, (i - 1) % Y) for i in range(Y)]
@@ -233,7 +237,7 @@
         [SMEM] + [VMEM] * len(parts),
         (VMEM,) * 4,
         flops=1 << 28,
-        scratch_shapes=[pltpu.VMEM((CHIPS, Y, 16, 2 * PAD), jnp.bfloat16)],
+        scratch_shapes=[pltpu.VMEM((X, Z, Y, 16, 2 * PAD), jnp.bfloat16)],
     )(me, *parts)
     theirs = call(theirs_grad, f32(ROWS + 8, WIDTH), [VMEM] * 3, VMEM, flops=1 << 31)(turned_theirs, act, slots_theirs)
     theirs = lax.ppermute(theirs, "c", [(0, 1), (1, 0)])
@@ -263,9 +267,9 @@
         ANY,
         limit=WIDE_LIMIT,
         scratch_shapes=[
-            pltpu.VMEM((Y, PAIR * CAP, WIDTH), jnp.bfloat16),
-            pltpu.SemaphoreType.DMA((Y,)),
-            pltpu.SemaphoreType.DMA((Y,)),
+            pltpu.VMEM((STRIPS, PAIR * CAP, Y * WIDTH // STRIPS), jnp.bfloat16),
+            pltpu.SemaphoreType.DMA((STRIPS,)),
+            pltpu.SemaphoreType.DMA((STRIPS,)),
         ],
     )(new_weights)
 

time: 183 us -> 182 us (level)
  no operation moved by 1% of the time
where the time goes in v5:
time: 182 us
  blocking collectives  78.4 us (43%)
  starting transfers between devices  48.7 us (27%)
  waiting for transfers between devices  17.3 us (10%)
  Pallas kernels  15.6 us (9%)
  between operations  14.4 us (8%)
  local copies, waits for them, and re-layouts  6.26 us (3%)
    all_to_all x1, blocking collectives, shards(): lax.all_to_all(packed, ('z', 'x'), split_axis=0, concat_axis=0, tiled=True)  31.9 us
    all_to_all x1, blocking collectives, shards(): lax.all_to_all(states, dp_axes, split_axis=0, concat_axis=0, tiled=True)  28 us
    ppermute x6, starting transfers between devices, shards(): down.append([lax.ppermute(half, 'y', right) for half in down[-1]])  22.8 us
    all_to_all x1, blocking collectives, shards(): lax.all_to_all(weights, dp_axes, split_axis=0, concat_axis=0, tiled=True)  18.5 us
    ppermute x6, starting transfers between devices, shards(): up.append([lax.ppermute(half, 'y', left) for half in up[-1]])  16.9 us
    unnamed x18, local copies, waits for them, and re-layouts  6.22 us
    all_gather x1, waiting for transfers between devices, shards(): new_weights = lax.all_gather(weights, 'y', axis=1, tiled=True)  6.04 us
    ppermute x1, waiting for transfers between devices, shards(): lax.ppermute(up[-1][1], 'y', left)  4.04 us
  transfers between devices with their start and end apart: 17, of which 6 were waited for; matrix products, arithmetic and copies ran while one was open for 1% of the time, Pallas kernels for 5%

profile of v5, /device:TPU:8, one launch (start us, length us, event | category | flops | bytes accessed | tf_op | source)
XLA Modules:
  0.0 181.7 jit_solution(7968424276011547823)
XLA Ops:
  7.2 0.0 all-gather.3.cloned.1.call-start
  7.2 0.7 all-gather.3.cloned.1.call-update
  7.9 0.0 all-gather.5.cloned.1.call-start
  8.0 2.4 %shard_map.102 = (bf16[32,16,512]{2,1,0:T(8,128)(2,1)}, s32[1,128]{1,0:T(1,128)}) custom-call(s32[1]{0:T(128)} %bitcast.core_ref, s32[1,112]{1,0:T(1,128)} %bitcast.12, s32[1,112]{1,0:T(1,128)} %bitcast.13, bf16[16,14336]{1,0:T(8,128)(2,1)} %cot_ref.1), custom_call_target="tpu_custom_call" | custom-call | bytes 4194304 | tf_op jit(solution)/shard_map/pallas_call | solution.py:216
  10.4 31.9 %all_to_all.15 = bf16[32,16,512]{2,1,0:T(8,128)(2,1)S(1)} all-to-all(bf16[32,16,512]{2,1,0:T(8,128)(2,1)} %get-tuple-element.16), channel_id=1, replica_groups=mesh['z'=8,'x'=4,'c'=2,'y'=8] {'z','x'}, dimensions={0} | all-to-all | bytes 1048576 | tf_op jit(solution)/shard_map/all_to_all | solution.py:219
  42.3 3.5 %collective-permute-start = (bf16[256,512]{1,0:T(8,128)(2,1)S(1)}, bf16[256,512]{1,0:T(8,128)(2,1)S(1)}, u32[]{:S(2)}, u32[]{:S(2)}) collective-permute-start(bf16[256,512]{1,0:T(8,128)(2,1)S(1)} %bitcast.8), channel_id=1, source_target_pairs={{0,1},{1,2},{2,3},{3,4},{4,5},{5,6},{6,7},{7,0},{8,9},{9,10},{10,1... | collective-permute-start | bytes 786440 | tf_op jit(solution)/shard_map/ppermute | solution.py:228
  45.8 2.4 %collective-permute-start.3 = (bf16[256,512]{1,0:T(8,128)(2,1)S(1)}, bf16[256,512]{1,0:T(8,128)(2,1)S(1)}, u32[]{:S(2)}, u32[]{:S(2)}) collective-permute-start(bf16[256,512]{1,0:T(8,128)(2,1)S(1)} %bitcast.10), channel_id=1, source_target_pairs={{0,7},{1,0},{2,1},{3,2},{4,3},{5,4},{6,5},{7,6},{8,15},{9,8},{10,9... | collective-permute-start | bytes 786440 | tf_op jit(solution)/shard_map/ppermute | solution.py:229
  48.2 3.5 %collective-permute-start.1 = (bf16[256,512]{1,0:T(8,128)(2,1)S(1)}, bf16[256,512]{1,0:T(8,128)(2,1)S(1)}, u32[]{:S(2)}, u32[]{:S(2)}) collective-permute-start(bf16[256,512]{1,0:T(8,128)(2,1)S(1)} %bitcast.11), channel_id=1, source_target_pairs={{0,1},{1,2},{2,3},{3,4},{4,5},{5,6},{6,7},{7,0},{8,9},{9,10},{10,1... | collective-permute-start | bytes 786440 | tf_op jit(solution)/shard_map/ppermute | solution.py:228
  51.6 2.4 %collective-permute-start.2 = (bf16[256,512]{1,0:T(8,128)(2,1)S(1)}, bf16[256,512]{1,0:T(8,128)(2,1)S(1)}, u32[]{:S(2)}, u32[]{:S(2)}) collective-permute-start(bf16[256,512]{1,0:T(8,128)(2,1)S(1)} %bitcast.9), channel_id=1, source_target_pairs={{0,7},{1,0},{2,1},{3,2},{4,3},{5,4},{6,5},{7,6},{8,15},{9,8},{10,9... | collective-permute-start | bytes 786440 | tf_op jit(solution)/shard_map/ppermute | solution.py:229
  54.0 0.0 collective-permute-done.refs_1_
  54.0 3.8 %collective-permute-start.4 = (bf16[256,512]{1,0:T(8,128)(2,1)S(1)}, bf16[256,512]{1,0:T(8,128)(2,1)S(1)}, u32[]{:S(2)}, u32[]{:S(2)}) collective-permute-start(bf16[256,512]{1,0:T(8,128)(2,1)S(1)} %collective-permute-done.refs_1_), channel_id=1, source_target_pairs={{0,1},{1,2},{2,3},{3,4},{4,5},{5,6},{6,7},{7,0},{8,9},{9,10},{10,1... | collective-permute-start | bytes 786440 | tf_op jit(solution)/shard_map/ppermute | solution.py:228
  57.8 0.0 collective-permute-done.3.refs_4_
  57.8 3.0 %collective-permute-start.7 = (bf16[256,512]{1,0:T(8,128)(2,1)S(1)}, bf16[256,512]{1,0:T(8,128)(2,1)S(1)}, u32[]{:S(2)}, u32[]{:S(2)}) collective-permute-start(bf16[256,512]{1,0:T(8,128)(2,1)S(1)} %collective-permute-done.3.refs_4_), channel_id=1, source_target_pairs={{0,7},{1,0},{2,1},{3,2},{4,3},{5,4},{6,5},{7,6},{8,15},{9,8},{10,9... | collective-permute-start | bytes 786440 | tf_op jit(solution)/shard_map/ppermute | solution.py:229
  60.9 0.0 collective-permute-done.1.refs_2_
  60.9 4.0 %collective-permute-start.5 = (bf16[256,512]{1,0:T(8,128)(2,1)S(1)}, bf16[256,512]{1,0:T(8,128)(2,1)S(1)}, u32[]{:S(2)}, u32[]{:S(2)}) collective-permute-start(bf16[256,512]{1,0:T(8,128)(2,1)S(1)} %collective-permute-done.1.refs_2_), channel_id=1, source_target_pairs={{0,1},{1,2},{2,3},{3,4},{4,5},{5,6},{6,7},{7,0},{8,9},{9,10},{10,1... | collective-permute-start | bytes 786440 | tf_op jit(solution)/shard_map/ppermute | solution.py:228
  64.9 0.0 collective-permute-done.2.refs_3_
  64.9 3.0 %collective-permute-start.6 = (bf16[256,512]{1,0:T(8,128)(2,1)S(1)}, bf16[256,512]{1,0:T(8,128)(2,1)S(1)}, u32[]{:S(2)}, u32[]{:S(2)}) collective-permute-start(bf16[256,512]{1,0:T(8,128)(2,1)S(1)} %collective-permute-done.2.refs_3_), channel_id=1, source_target_pairs={{0,7},{1,0},{2,1},{3,2},{4,3},{5,4},{6,5},{7,6},{8,15},{9,8},{10,9... | collective-permute-start | bytes 786440 | tf_op jit(solution)/shard_map/ppermute | solution.py:229
  68.0 0.0 collective-permute-done.4.refs_5_
  68.0 4.0 %collective-permute-start.8 = (bf16[256,512]{1,0:T(8,128)(2,1)S(1)}, bf16[256,512]{1,0:T(8,128)(2,1)S(1)}, u32[]{:S(2)}, u32[]{:S(2)}) collective-permute-start(bf16[256,512]{1,0:T(8,128)(2,1)S(1)} %collective-permute-done.4.refs_5_), channel_id=1, source_target_pairs={{0,1},{1,2},{2,3},{3,4},{4,5},{5,6},{6,7},{7,0},{8,9},{9,10},{10,1... | collective-permute-start | bytes 786440 | tf_op jit(solution)/shard_map/ppermute | solution.py:228
  72.0 0.0 collective-permute-done.7.refs_8_
  72.0 3.0 %collective-permute-start.11 = (bf16[256,512]{1,0:T(8,128)(2,1)S(1)}, bf16[256,512]{1,0:T(8,128)(2,1)S(1)}, u32[]{:S(2)}, u32[]{:S(2)}) collective-permute-start(bf16[256,512]{1,0:T(8,128)(2,1)S(1)} %collective-permute-done.7.refs_8_), channel_id=1, source_target_pairs={{0,7},{1,0},{2,1},{3,2},{4,3},{5,4},{6,5},{7,6},{8,15},{9,8},{10,9... | collective-permute-start | bytes 786440 | tf_op jit(solution)/shard_map/ppermute | solution.py:229
  75.0 0.0 collective-permute-done.5.refs_6_
  75.1 4.0 %collective-permute-start.9 = (bf16[256,512]{1,0:T(8,128)(2,1)S(1)}, bf16[256,512]{1,0:T(8,128)(2,1)S(1)}, u32[]{:S(2)}, u32[]{:S(2)}) collective-permute-start(bf16[256,512]{1,0:T(8,128)(2,1)S(1)} %collective-permute-done.5.refs_6_), channel_id=1, source_target_pairs={{0,1},{1,2},{2,3},{3,4},{4,5},{5,6},{6,7},{7,0},{8,9},{9,10},{10,1... | collective-permute-start | bytes 786440 | tf_op jit(solution)/shard_map/ppermute | solution.py:228
  79.1 0.0 collective-permute-done.6.refs_7_
  79.1 3.0 %collective-permute-start.10 = (bf16[256,512]{1,0:T(8,128)(2,1)S(1)}, bf16[256,512]{1,0:T(8,128)(2,1)}, u32[]{:S(2)}, u32[]{:S(2)}) collective-permute-start(bf16[256,512]{1,0:T(8,128)(2,1)S(1)} %collective-permute-done.6.refs_7_), channel_id=1, source_target_pairs={{0,7},{1,0},{2,1},{3,2},{4,3},{5,4},{6,5},{7,6},{8,15},{9,8},{10,9... | collective-permute-start | bytes 786440 | tf_op jit(solution)/shard_map/ppermute | solution.py:229
  82.1 0.0 collective-permute-done.8.refs_9_
  82.1 4.0 %collective-permute-start.12 = (bf16[256,512]{1,0:T(8,128)(2,1)S(1)}, bf16[256,512]{1,0:T(8,128)(2,1)}, u32[]{:S(2)}, u32[]{:S(2)}) collective-permute-start(bf16[256,512]{1,0:T(8,128)(2,1)S(1)} %collective-permute-done.8.refs_9_), channel_id=1, source_target_pairs={{0,1},{1,2},{2,3},{3,4},{4,5},{5,6},{6,7},{7,0},{8,9},{9,10},{10,1... | collective-permute-start | bytes 786440 | tf_op jit(solution)/shard_map/ppermute | solution.py:230
  86.2 0.0 collective-permute-done.11.refs_12_
  86.2 3.0 %collective-permute-start.13 = (bf16[256,512]{1,0:T(8,128)(2,1)S(1)}, bf16[256,512]{1,0:T(8,128)(2,1)}, u32[]{:S(2)}, u32[]{:S(2)}) collective-permute-start(bf16[256,512]{1,0:T(8,128)(2,1)S(1)} %collective-permute-done.11.refs_12_), channel_id=1, source_target_pairs={{0,7},{1,0},{2,1},{3,2},{4,3},{5,4},{6,5},{7,6},{8,15},{9,8},{10,9... | collective-permute-start | bytes 786440 | tf_op jit(solution)/shard_map/ppermute | solution.py:230
  89.2 0.0 collective-permute-done.9.refs_10_
  89.2 2.1 %collective-permute-done.10.refs_11_ = bf16[256,512]{1,0:T(8,128)(2,1)} collective-permute-done((bf16[256,512]{1,0:T(8,128)(2,1)S(1)}, bf16[256,512]{1,0:T(8,128)(2,1)}, u32[]{:S(2)}, u32[]{:S(2)}) %collective-permute-start.10) | collective-permute-done | bytes 262176 | tf_op jit(solution)/shard_map/ppermute | solution.py:229
  91.3 0.4 collective-permute-done.12.refs_13_
  91.7 4.0 %collective-permute-done.13.refs_14_ = bf16[256,512]{1,0:T(8,128)(2,1)} collective-permute-done((bf16[256,512]{1,0:T(8,128)(2,1)S(1)}, bf16[256,512]{1,0:T(8,128)(2,1)}, u32[]{:S(2)}, u32[]{:S(2)}) %collective-permute-start.13) | collective-permute-done | bytes 262176 | tf_op jit(solution)/shard_map/ppermute | solution.py:230
  95.8 2.6 %shard_map.103 = (bf16[224,4096]{1,0:T(8,128)(2,1)S(1)}, bf16[224,4096]{1,0:T(8,128)(2,1)S(1)}, f32[8,128]{1,0:T(8,128)S(1)}, f32[8,128]{1,0:T(8,128)S(1)}) custom-call(s32[1]{0:T(128)} %bitcast.3.me_ref, bf16[512,512]{1,0:T(8,128)(2,1)S(1)} %bitcast.7, bf16[256,512]{1,0:T(8,128)(2,1)S(1)} %collective-permute-done.refs_1_, ...), custom_call_target="tpu_custom_call" | custom-call | flops 268435456 | bytes 4194304 | tf_op jit(solution)/shard_map/pallas_call | solution.py:234
  98.4 0.0 copy-start.5
  98.4 1.2 copy-done.5
  99.6 1.3 copy-done.7
  100.9 3.4 %all-gather.3.cloned.1.call-done.act_ref = bf16[4096,512]{1,0:T(8,128)(2,1)} async-done(((bf16[128,512]{1,0:T(8,128)(2,1)}), bf16[4096,512]{1,0:T(8,128)(2,1)}) %all-gather.3.cloned.1.call-update) | async-done | bytes 4194320 | tf_op jit(solution)/shard_map/all_gather | solution.py:222
  104.3 2.2 %copy-done.4 = bf16[4096,512]{1,0:T(8,128)(2,1)S(1)} copy-done((bf16[4096,512]{1,0:T(8,128)(2,1)S(1)}, bf16[4096,512]{1,0:T(8,128)(2,1)}, u32[]{:S(2)}) %copy-start.4) | copy-done | bytes 4194328
  106.5 1.5 copy-done.8
  108.0 1.1 shard_map.105
  109.1 1.9 %collective-permute-start.14 = (f32[232,512]{1,0:T(8,128)S(1)}, f32[232,512]{1,0:T(8,128)S(1)}, u32[]{:S(2)}, u32[]{:S(2)}) collective-permute-start(f32[232,512]{1,0:T(8,128)S(1)} %shard_map.105), channel_id=1, source_target_pairs={{0,8},{8,0},{1,9},{9,1},{2,10},{10,2},{3,11},{11,3},{4,12},{12,4},... | collective-permute-start | bytes 1425416 | tf_op jit(solution)/shard_map/ppermute | solution.py:243
  111.1 0.0 copy-done.6
  111.1 0.0 copy-start
  111.1 0.0 copy-start.1
  111.1 0.0 copy-start.2
  111.1 0.0 copy-start.3
  111.1 1.1 shard_map.104.mine_ref
  112.2 0.6 collective-permute-done.14.theirs_ref
  112.9 0.0 copy-done
  112.9 0.0 copy-done.1
  112.9 0.0 copy-done.2
  112.9 0.0 copy-done.3
  112.9 1.2 shard_map.106
  114.1 18.5 %all_to_all.16.arrived_ref = bf16[128,2,512]{2,1,0:T(2,128)(2,1)S(1)} all-to-all(bf16[128,2,512]{2,1,0:T(2,128)(2,1)S(1)} %get-tuple-element.22), channel_id=1, replica_groups=mesh['z'=8,'x'=4,'c'=2,'y'=8] {'z','x','c'}, dimensions={0} | all-to-all | bytes 524288 | tf_op jit(solution)/shard_map/all_to_all | solution.py:254
  132.5 1.4 shard_map.108.after_ref
  134.0 0.0 all-gather.5.cloned.1.call-update
  134.0 1.4 shard_map.107.value_ref
  135.4 0.5 convert_element_type.6
  136.0 28.0 %all_to_all.17 = f16[128,2,1536]{2,1,0:T(2,128)(2,1)S(1)} all-to-all(f16[128,2,1536]{2,1,0:T(2,128)(2,1)S(1)} %convert_element_type.6), channel_id=1, replica_groups=mesh['z'=8,'x'=4,'c'=2,'y'=8] {'z','x','c'}, dimensions={0} | all-to-all | bytes 1572864 | tf_op jit(solution)/shard_map/all_to_all | solution.py:286
  164.0 0.5 convert_element_type.7.arrived_ref
  164.5 2.0 %shard_map.110 = (f32[228,512]{1,0:T(8,128)}, f32[228,512]{1,0:T(8,128)}, f32[228,512]{1,0:T(8,128)}) custom-call(s32[4,128]{1,0:T(4,128)S(1)} %get-tuple-element.21.slot_ref, f32[128,2,1536]{2,1,0:T(2,128)S(1)} %convert_element_type.7.arrived_ref), custom_call_target="tpu_custom_call" | custom-call | bytes 4194304 | tf_op jit(solution)/shard_map/pallas_call | solution.py:287
  166.5 6.0 %all-gather.5.cloned.1.call-done.in_ref = bf16[228,4096]{1,0:T(8,128)(2,1)} async-done(((bf16[228,512]{1,0:T(8,128)(2,1)}), bf16[228,4096]{1,0:T(8,128)(2,1)}) %all-gather.5.cloned.1.call-update) | async-done | bytes 1867792 | tf_op jit(solution)/shard_map/all_gather | solution.py:262
  172.5 2.3 %shard_map.111 = bf16[228,4096]{1,0:T(8,128)(2,1)} custom-call(bf16[228,4096]{1,0:T(8,128)(2,1)} %all-gather.5.cloned.1.call-done.in_ref), custom_call_target="tpu_custom_call" | custom-call | bytes 4194304 | tf_op jit(solution)/shard_map/pallas_call | solution.py:263
  (6 shorter events, 0.0 us)
Async XLA Ops:
  7.2 97.1 %all-gather.3.cloned.1.call-start = ((), (), s32[]{:S(2)}) async-start(), calls=%async_computation.3 | async-start | bytes 4325376 | tf_op jit(solution)/shard_map/all_gather | solution.py:222
  7.9 164.6 %all-gather.5.cloned.1.call-start = ((), (), s32[]{:S(2)}) async-start(), calls=%async_computation.4 | async-start | bytes 2138112 | tf_op jit(solution)/shard_map/all_gather | solution.py:262
  42.3 11.7 %collective-permute-start = (bf16[256,512]{1,0:T(8,128)(2,1)S(1)}, bf16[256,512]{1,0:T(8,128)(2,1)S(1)}, u32[]{:S(2)}, u32[]{:S(2)}) collective-permute-start(bf16[256,512]{1,0:T(8,128)(2,1)S(1)} %bitcast.8), channel_id=1, source_target_pairs={{0,1},{1,2},{2,3},{3,4},{4,5},{5,6},{6,7},{7,0},{8,9},{9,10},{10,1... | collective-permute-start | bytes 786440 | tf_op jit(solution)/shard_map/ppermute | solution.py:228
  45.8 12.0 %collective-permute-start.3 = (bf16[256,512]{1,0:T(8,128)(2,1)S(1)}, bf16[256,512]{1,0:T(8,128)(2,1)S(1)}, u32[]{:S(2)}, u32[]{:S(2)}) collective-permute-start(bf16[256,512]{1,0:T(8,128)(2,1)S(1)} %bitcast.10), channel_id=1, source_target_pairs={{0,7},{1,0},{2,1},{3,2},{4,3},{5,4},{6,5},{7,6},{8,15},{9,8},{10,9... | collective-permute-start | bytes 786440 | tf_op jit(solution)/shard_map/ppermute | solution.py:229
  48.2 12.7 %collective-permute-start.1 = (bf16[256,512]{1,0:T(8,128)(2,1)S(1)}, bf16[256,512]{1,0:T(8,128)(2,1)S(1)}, u32[]{:S(2)}, u32[]{:S(2)}) collective-permute-start(bf16[256,512]{1,0:T(8,128)(2,1)S(1)} %bitcast.11), channel_id=1, source_target_pairs={{0,1},{1,2},{2,3},{3,4},{4,5},{5,6},{6,7},{7,0},{8,9},{9,10},{10,1... | collective-permute-start | bytes 786440 | tf_op jit(solution)/shard_map/ppermute | solution.py:228
  51.6 13.3 %collective-permute-start.2 = (bf16[256,512]{1,0:T(8,128)(2,1)S(1)}, bf16[256,512]{1,0:T(8,128)(2,1)S(1)}, u32[]{:S(2)}, u32[]{:S(2)}) collective-permute-start(bf16[256,512]{1,0:T(8,128)(2,1)S(1)} %bitcast.9), channel_id=1, source_target_pairs={{0,7},{1,0},{2,1},{3,2},{4,3},{5,4},{6,5},{7,6},{8,15},{9,8},{10,9... | collective-permute-start | bytes 786440 | tf_op jit(solution)/shard_map/ppermute | solution.py:229
  54.0 13.9 %collective-permute-start.4 = (bf16[256,512]{1,0:T(8,128)(2,1)S(1)}, bf16[256,512]{1,0:T(8,128)(2,1)S(1)}, u32[]{:S(2)}, u32[]{:S(2)}) collective-permute-start(bf16[256,512]{1,0:T(8,128)(2,1)S(1)} %collective-permute-done.refs_1_), channel_id=1, source_target_pairs={{0,1},{1,2},{2,3},{3,4},{4,5},{5,6},{6,7},{7,0},{8,9},{9,10},{10,1... | collective-permute-start | bytes 786440 | tf_op jit(solution)/shard_map/ppermute | solution.py:228
  57.8 14.2 %collective-permute-start.7 = (bf16[256,512]{1,0:T(8,128)(2,1)S(1)}, bf16[256,512]{1,0:T(8,128)(2,1)S(1)}, u32[]{:S(2)}, u32[]{:S(2)}) collective-permute-start(bf16[256,512]{1,0:T(8,128)(2,1)S(1)} %collective-permute-done.3.refs_4_), channel_id=1, source_target_pairs={{0,7},{1,0},{2,1},{3,2},{4,3},{5,4},{6,5},{7,6},{8,15},{9,8},{10,9... | collective-permute-start | bytes 786440 | tf_op jit(solution)/shard_map/ppermute | solution.py:229
  60.9 14.2 %collective-permute-start.5 = (bf16[256,512]{1,0:T(8,128)(2,1)S(1)}, bf16[256,512]{1,0:T(8,128)(2,1)S(1)}, u32[]{:S(2)}, u32[]{:S(2)}) collective-permute-start(bf16[256,512]{1,0:T(8,128)(2,1)S(1)} %collective-permute-done.1.refs_2_), channel_id=1, source_target_pairs={{0,1},{1,2},{2,3},{3,4},{4,5},{5,6},{6,7},{7,0},{8,9},{9,10},{10,1... | collective-permute-start | bytes 786440 | tf_op jit(solution)/shard_map/ppermute | solution.py:228
  64.9 14.2 %collective-permute-start.6 = (bf16[256,512]{1,0:T(8,128)(2,1)S(1)}, bf16[256,512]{1,0:T(8,128)(2,1)S(1)}, u32[]{:S(2)}, u32[]{:S(2)}) collective-permute-start(bf16[256,512]{1,0:T(8,128)(2,1)S(1)} %collective-permute-done.2.refs_3_), channel_id=1, source_target_pairs={{0,7},{1,0},{2,1},{3,2},{4,3},{5,4},{6,5},{7,6},{8,15},{9,8},{10,9... | collective-permute-start | bytes 786440 | tf_op jit(solution)/shard_map/ppermute | solution.py:229
  68.0 14.2 %collective-permute-start.8 = (bf16[256,512]{1,0:T(8,128)(2,1)S(1)}, bf16[256,512]{1,0:T(8,128)(2,1)S(1)}, u32[]{:S(2)}, u32[]{:S(2)}) collective-permute-start(bf16[256,512]{1,0:T(8,128)(2,1)S(1)} %collective-permute-done.4.refs_5_), channel_id=1, source_target_pairs={{0,1},{1,2},{2,3},{3,4},{4,5},{5,6},{6,7},{7,0},{8,9},{9,10},{10,1... | collective-permute-start | bytes 786440 | tf_op jit(solution)/shard_map/ppermute | solution.py:228
  72.0 14.2 %collective-permute-start.11 = (bf16[256,512]{1,0:T(8,128)(2,1)S(1)}, bf16[256,512]{1,0:T(8,128)(2,1)S(1)}, u32[]{:S(2)}, u32[]{:S(2)}) collective-permute-start(bf16[256,512]{1,0:T(8,128)(2,1)S(1)} %collective-permute-done.7.refs_8_), channel_id=1, source_target_pairs={{0,7},{1,0},{2,1},{3,2},{4,3},{5,4},{6,5},{7,6},{8,15},{9,8},{10,9... | collective-permute-start | bytes 786440 | tf_op jit(solution)/shard_map/ppermute | solution.py:229
  75.1 14.2 %collective-permute-start.9 = (bf16[256,512]{1,0:T(8,128)(2,1)S(1)}, bf16[256,512]{1,0:T(8,128)(2,1)S(1)}, u32[]{:S(2)}, u32[]{:S(2)}) collective-permute-start(bf16[256,512]{1,0:T(8,128)(2,1)S(1)} %collective-permute-done.5.refs_6_), channel_id=1, source_target_pairs={{0,1},{1,2},{2,3},{3,4},{4,5},{5,6},{6,7},{7,0},{8,9},{9,10},{10,1... | collective-permute-start | bytes 786440 | tf_op jit(solution)/shard_map/ppermute | solution.py:228
  79.1 12.2 %collective-permute-start.10 = (bf16[256,512]{1,0:T(8,128)(2,1)S(1)}, bf16[256,512]{1,0:T(8,128)(2,1)}, u32[]{:S(2)}, u32[]{:S(2)}) collective-permute-start(bf16[256,512]{1,0:T(8,128)(2,1)S(1)} %collective-permute-done.6.refs_7_), channel_id=1, source_target_pairs={{0,7},{1,0},{2,1},{3,2},{4,3},{5,4},{6,5},{7,6},{8,15},{9,8},{10,9... | collective-permute-start | bytes 786440 | tf_op jit(solution)/shard_map/ppermute | solution.py:229
  82.1 9.6 %collective-permute-start.12 = (bf16[256,512]{1,0:T(8,128)(2,1)S(1)}, bf16[256,512]{1,0:T(8,128)(2,1)}, u32[]{:S(2)}, u32[]{:S(2)}) collective-permute-start(bf16[256,512]{1,0:T(8,128)(2,1)S(1)} %collective-permute-done.8.refs_9_), channel_id=1, source_target_pairs={{0,1},{1,2},{2,3},{3,4},{4,5},{5,6},{6,7},{7,0},{8,9},{9,10},{10,1... | collective-permute-start | bytes 786440 | tf_op jit(solution)/shard_map/ppermute | solution.py:230
  86.2 9.6 %collective-permute-start.13 = (bf16[256,512]{1,0:T(8,128)(2,1)S(1)}, bf16[256,512]{1,0:T(8,128)(2,1)}, u32[]{:S(2)}, u32[]{:S(2)}) collective-permute-start(bf16[256,512]{1,0:T(8,128)(2,1)S(1)} %collective-permute-done.11.refs_12_), channel_id=1, source_target_pairs={{0,7},{1,0},{2,1},{3,2},{4,3},{5,4},{6,5},{7,6},{8,15},{9,8},{10,9... | collective-permute-start | bytes 786440 | tf_op jit(solution)/shard_map/ppermute | solution.py:230
  98.4 1.2 copy-start.5
  99.6 1.3 copy-start.7
  104.3 2.2 %copy-start.4 = (bf16[4096,512]{1,0:T(8,128)(2,1)S(1)}, bf16[4096,512]{1,0:T(8,128)(2,1)}, u32[]{:S(2)}) copy-start(bf16[4096,512]{1,0:T(8,128)(2,1)} %all-gather.3.cloned.1.call-done.act_ref) | copy-start | bytes 12582916
  106.5 1.5 copy-start.8
  108.0 3.1 %copy-start.6 = (bf16[224,4096]{1,0:T(8,128)(2,1)S(1)}, bf16[224,4096]{1,0:T(8,128)(2,1)}, u32[]{:S(2)}) copy-start(bf16[224,4096]{1,0:T(8,128)(2,1)} %copy-done.5) | copy-start | bytes 5505028
  109.1 3.7 %collective-permute-start.14 = (f32[232,512]{1,0:T(8,128)S(1)}, f32[232,512]{1,0:T(8,128)S(1)}, u32[]{:S(2)}, u32[]{:S(2)}) collective-permute-start(f32[232,512]{1,0:T(8,128)S(1)} %shard_map.105), channel_id=1, source_target_pairs={{0,8},{8,0},{1,9},{9,1},{2,10},{10,2},{3,11},{11,3},{4,12},{12,4},... | collective-permute-start | bytes 1425416 | tf_op jit(solution)/shard_map/ppermute | solution.py:243
  111.1 1.8 copy-start
  111.1 1.8 copy-start.1
  111.1 1.8 copy-start.2
  111.1 1.8 copy-start.3
Sparse Core Ops, SparseCore 0:
  11.2 93.0 all-gather.2
  134.1 38.3 all-gather.4

commit v6 on v5

--- a/solution.py
+++ b/solution.py
@@ -194,6 +194,11 @@
     out_ref[...] = placed[:CAP].reshape(PAIR * CAP, WIDTH).astype(jnp.bfloat16)
 
 
+def hold_index(value_ref, after_ref, out_ref):
+    del after_ref
+    out_ref[0] = value_ref[0]
+
+
 def hold(value_ref, after_ref, out_ref):
     del value_ref, after_ref, out_ref
 
@@ -231,6 +236,7 @@
     parts = [shared] + [half for step in range(1, Y // 2) for way in (down, up) for half in way[step]] + far
 
     me = lax.axis_index("y").astype(jnp.int32).reshape(1)
+    me = call(hold_index, int32(1), [SMEM, ANY], SMEM, limit=WIDE_LIMIT)(me, act)
     turned, turned_theirs, slots, slots_theirs = call(
         turn,
         (bf16(ROWS, Y * CHIPS * 16),) * 2 + (f32(8, LANES),) * 2,

time: 182 us -> 183 us (level)
  waiting for transfers between devices: 17.3 us -> 26 us
  local copies, waits for them, and re-layouts: 6.26 us -> 0.06 us
  starting transfers between devices: 48.7 us -> 45.2 us
    all_gather x1, waiting for transfers between devices: 3.38 us -> 18.6 us  [shards(): act = lax.all_gather(activations, ('x', 'z'), axis=0, tiled=True)]
    unnamed x18 -> x10, local copies, waits for them, and re-layouts: 6.22 us -> 0.03 us
    ppermute x6, starting transfers between devices: 22.8 us -> 17.4 us  [shards(): down.append([lax.ppermute(half, 'y', right) for half in down[-1]])]
    ppermute x1, waiting for transfers between devices: 4.04 us -> 0.01 us  [shards(): lax.ppermute(up[-1][1], 'y', left)]
    ppermute x6, starting transfers between devices: 16.9 us -> 20 us  [shards(): up.append([lax.ppermute(half, 'y', left) for half in up[-1]])]
    ppermute x6, waiting for transfers between devices: 2.11 us -> 0.02 us  [shards(): up.append([lax.ppermute(half, 'y', left) for half in up[-1]])]
  transfers between devices with their start and end apart: 17 -> 17, of which waited for: 6 -> 3; matrix products, arithmetic and copies ran while one was open for 1% -> 1% of each run, Pallas kernels for 5% -> 4%
where the time goes in v6:
time: 183 us; the launch traced here: 182 us
  blocking collectives  78.4 us (43%)
  starting transfers between devices  45.2 us (25%)
  waiting for transfers between devices  26 us (14%)
  Pallas kernels  17 us (9%)
  between operations  14.4 us (8%)
    all_to_all x1, blocking collectives, shards(): lax.all_to_all(packed, ('z', 'x'), split_axis=0, concat_axis=0, tiled=True)  31.9 us
    all_to_all x1, blocking collectives, shards(): lax.all_to_all(states, dp_axes, split_axis=0, concat_axis=0, tiled=True)  28 us
    ppermute x6, starting transfers between devices, shards(): up.append([lax.ppermute(half, 'y', left) for half in up[-1]])  20 us
    all_gather x1, waiting for transfers between devices, shards(): act = lax.all_gather(activations, ('x', 'z'), axis=0, tiled=True)  18.6 us
    all_to_all x1, blocking collectives, shards(): lax.all_to_all(weights, dp_axes, split_axis=0, concat_axis=0, tiled=True)  18.5 us
    ppermute x6, starting transfers between devices, shards(): down.append([lax.ppermute(half, 'y', right) for half in down[-1]])  17.4 us
    all_gather x1, waiting for transfers between devices, shards(): new_weights = lax.all_gather(weights, 'y', axis=1, tiled=True)  6.03 us
    ppermute x1, starting transfers between devices, shards(): lax.ppermute(down[-1][0], 'y', right)  3.92 us
  transfers between devices with their start and end apart: 17, of which 3 were waited for; matrix products, arithmetic and copies ran while one was open for 1% of the time, Pallas kernels for 4%

profile of v6, /device:TPU:8, one launch (start us, length us, event | category | flops | bytes accessed | tf_op | source)
XLA Modules:
  0.0 182.1 jit_solution(16235026033233545084)
XLA Ops:
  7.2 0.0 all-gather.3.cloned.1.call-start
  7.2 0.7 all-gather.3.cloned.1.call-update
  7.9 0.0 all-gather.5.cloned.1.call-start
  8.0 2.4 %shard_map.102 = (bf16[32,16,512]{2,1,0:T(8,128)(2,1)}, s32[1,128]{1,0:T(1,128)}) custom-call(s32[1]{0:T(128)} %bitcast.core_ref, s32[1,112]{1,0:T(1,128)} %bitcast.12, s32[1,112]{1,0:T(1,128)} %bitcast.13, bf16[16,14336]{1,0:T(8,128)(2,1)} %cot_ref.1), custom_call_target="tpu_custom_call" | custom-call | bytes 4194304 | tf_op jit(solution)/shard_map/pallas_call | solution.py:221
  10.4 31.9 %all_to_all.15 = bf16[32,16,512]{2,1,0:T(8,128)(2,1)S(1)} all-to-all(bf16[32,16,512]{2,1,0:T(8,128)(2,1)} %get-tuple-element.16), channel_id=1, replica_groups=mesh['z'=8,'x'=4,'c'=2,'y'=8] {'z','x'}, dimensions={0} | all-to-all | bytes 1048576 | tf_op jit(solution)/shard_map/all_to_all | solution.py:224
  42.3 3.5 %collective-permute-start = (bf16[256,512]{1,0:T(8,128)(2,1)S(1)}, bf16[256,512]{1,0:T(8,128)(2,1)S(1)}, u32[]{:S(2)}, u32[]{:S(2)}) collective-permute-start(bf16[256,512]{1,0:T(8,128)(2,1)S(1)} %bitcast.10), channel_id=1, source_target_pairs={{0,1},{1,2},{2,3},{3,4},{4,5},{5,6},{6,7},{7,0},{8,9},{9,10},{10,1... | collective-permute-start | bytes 786440 | tf_op jit(solution)/shard_map/ppermute | solution.py:233
  45.8 2.4 %collective-permute-start.3 = (bf16[256,512]{1,0:T(8,128)(2,1)S(1)}, bf16[256,512]{1,0:T(8,128)(2,1)S(1)}, u32[]{:S(2)}, u32[]{:S(2)}) collective-permute-start(bf16[256,512]{1,0:T(8,128)(2,1)S(1)} %bitcast.8), channel_id=1, source_target_pairs={{0,7},{1,0},{2,1},{3,2},{4,3},{5,4},{6,5},{7,6},{8,15},{9,8},{10,9... | collective-permute-start | bytes 786440 | tf_op jit(solution)/shard_map/ppermute | solution.py:234
  48.2 3.7 %collective-permute-start.2 = (bf16[256,512]{1,0:T(8,128)(2,1)S(1)}, bf16[256,512]{1,0:T(8,128)(2,1)S(1)}, u32[]{:S(2)}, u32[]{:S(2)}) collective-permute-start(bf16[256,512]{1,0:T(8,128)(2,1)S(1)} %bitcast.11), channel_id=1, source_target_pairs={{0,7},{1,0},{2,1},{3,2},{4,3},{5,4},{6,5},{7,6},{8,15},{9,8},{10,9... | collective-permute-start | bytes 786440 | tf_op jit(solution)/shard_map/ppermute | solution.py:234
  51.8 2.2 %collective-permute-start.1 = (bf16[256,512]{1,0:T(8,128)(2,1)S(1)}, bf16[256,512]{1,0:T(8,128)(2,1)S(1)}, u32[]{:S(2)}, u32[]{:S(2)}) collective-permute-start(bf16[256,512]{1,0:T(8,128)(2,1)S(1)} %bitcast.9), channel_id=1, source_target_pairs={{0,1},{1,2},{2,3},{3,4},{4,5},{5,6},{6,7},{7,0},{8,9},{9,10},{10,1... | collective-permute-start | bytes 786440 | tf_op jit(solution)/shard_map/ppermute | solution.py:233
  54.0 0.0 collective-permute-done.refs_1_
  54.0 3.8 %collective-permute-start.4 = (bf16[256,512]{1,0:T(8,128)(2,1)S(1)}, bf16[256,512]{1,0:T(8,128)(2,1)S(1)}, u32[]{:S(2)}, u32[]{:S(2)}) collective-permute-start(bf16[256,512]{1,0:T(8,128)(2,1)S(1)} %collective-permute-done.refs_1_), channel_id=1, source_target_pairs={{0,1},{1,2},{2,3},{3,4},{4,5},{5,6},{6,7},{7,0},{8,9},{9,10},{10,1... | collective-permute-start | bytes 786440 | tf_op jit(solution)/shard_map/ppermute | solution.py:233
  57.8 0.0 collective-permute-done.3.refs_4_
  57.8 2.1 %collective-permute-start.7 = (bf16[256,512]{1,0:T(8,128)(2,1)S(1)}, bf16[256,512]{1,0:T(8,128)(2,1)S(1)}, u32[]{:S(2)}, u32[]{:S(2)}) collective-permute-start(bf16[256,512]{1,0:T(8,128)(2,1)S(1)} %collective-permute-done.3.refs_4_), channel_id=1, source_target_pairs={{0,7},{1,0},{2,1},{3,2},{4,3},{5,4},{6,5},{7,6},{8,15},{9,8},{10,9... | collective-permute-start | bytes 786440 | tf_op jit(solution)/shard_map/ppermute | solution.py:234
  59.9 0.0 collective-permute-done.2.refs_3_
  59.9 4.9 %collective-permute-start.6 = (bf16[256,512]{1,0:T(8,128)(2,1)S(1)}, bf16[256,512]{1,0:T(8,128)(2,1)S(1)}, u32[]{:S(2)}, u32[]{:S(2)}) collective-permute-start(bf16[256,512]{1,0:T(8,128)(2,1)S(1)} %collective-permute-done.2.refs_3_), channel_id=1, source_target_pairs={{0,7},{1,0},{2,1},{3,2},{4,3},{5,4},{6,5},{7,6},{8,15},{9,8},{10,9... | collective-permute-start | bytes 786440 | tf_op jit(solution)/shard_map/ppermute | solution.py:234
  64.8 0.0 collective-permute-done.1.refs_2_
  64.8 2.0 %collective-permute-start.5 = (bf16[256,512]{1,0:T(8,128)(2,1)S(1)}, bf16[256,512]{1,0:T(8,128)(2,1)S(1)}, u32[]{:S(2)}, u32[]{:S(2)}) collective-permute-start(bf16[256,512]{1,0:T(8,128)(2,1)S(1)} %collective-permute-done.1.refs_2_), channel_id=1, source_target_pairs={{0,1},{1,2},{2,3},{3,4},{4,5},{5,6},{6,7},{7,0},{8,9},{9,10},{10,1... | collective-permute-start | bytes 786440 | tf_op jit(solution)/shard_map/ppermute | solution.py:233
  66.8 0.0 collective-permute-done.4.refs_5_
  66.9 3.9 %collective-permute-start.8 = (bf16[256,512]{1,0:T(8,128)(2,1)S(1)}, bf16[256,512]{1,0:T(8,128)(2,1)S(1)}, u32[]{:S(2)}, u32[]{:S(2)}) collective-permute-start(bf16[256,512]{1,0:T(8,128)(2,1)S(1)} %collective-permute-done.4.refs_5_), channel_id=1, source_target_pairs={{0,1},{1,2},{2,3},{3,4},{4,5},{5,6},{6,7},{7,0},{8,9},{9,10},{10,1... | collective-permute-start | bytes 786440 | tf_op jit(solution)/shard_map/ppermute | solution.py:233
  70.8 0.0 collective-permute-done.7.refs_8_
  70.8 1.9 %collective-permute-start.11 = (bf16[256,512]{1,0:T(8,128)(2,1)S(1)}, bf16[256,512]{1,0:T(8,128)(2,1)S(1)}, u32[]{:S(2)}, u32[]{:S(2)}) collective-permute-start(bf16[256,512]{1,0:T(8,128)(2,1)S(1)} %collective-permute-done.7.refs_8_), channel_id=1, source_target_pairs={{0,7},{1,0},{2,1},{3,2},{4,3},{5,4},{6,5},{7,6},{8,15},{9,8},{10,9... | collective-permute-start | bytes 786440 | tf_op jit(solution)/shard_map/ppermute | solution.py:234
  72.7 0.0 collective-permute-done.6.refs_7_
  72.7 5.0 %collective-permute-start.10 = (bf16[256,512]{1,0:T(8,128)(2,1)S(1)}, bf16[256,512]{1,0:T(8,128)(2,1)S(1)}, u32[]{:S(2)}, u32[]{:S(2)}) collective-permute-start(bf16[256,512]{1,0:T(8,128)(2,1)S(1)} %collective-permute-done.6.refs_7_), channel_id=1, source_target_pairs={{0,7},{1,0},{2,1},{3,2},{4,3},{5,4},{6,5},{7,6},{8,15},{9,8},{10,9... | collective-permute-start | bytes 786440 | tf_op jit(solution)/shard_map/ppermute | solution.py:234
  77.8 0.0 collective-permute-done.5.refs_6_
  77.8 2.0 %collective-permute-start.9 = (bf16[256,512]{1,0:T(8,128)(2,1)S(1)}, bf16[256,512]{1,0:T(8,128)(2,1)}, u32[]{:S(2)}, u32[]{:S(2)}) collective-permute-start(bf16[256,512]{1,0:T(8,128)(2,1)S(1)} %collective-permute-done.5.refs_6_), channel_id=1, source_target_pairs={{0,1},{1,2},{2,3},{3,4},{4,5},{5,6},{6,7},{7,0},{8,9},{9,10},{10,1... | collective-permute-start | bytes 786440 | tf_op jit(solution)/shard_map/ppermute | solution.py:233
  79.8 0.0 collective-permute-done.8.refs_9_
  79.8 3.9 %collective-permute-start.12 = (bf16[256,512]{1,0:T(8,128)(2,1)S(1)}, bf16[256,512]{1,0:T(8,128)(2,1)}, u32[]{:S(2)}, u32[]{:S(2)}) collective-permute-start(bf16[256,512]{1,0:T(8,128)(2,1)S(1)} %collective-permute-done.8.refs_9_), channel_id=1, source_target_pairs={{0,1},{1,2},{2,3},{3,4},{4,5},{5,6},{6,7},{7,0},{8,9},{9,10},{10,1... | collective-permute-start | bytes 786440 | tf_op jit(solution)/shard_map/ppermute | solution.py:235
  83.8 0.0 collective-permute-done.11.refs_12_
  83.8 1.9 %collective-permute-start.13 = (bf16[256,512]{1,0:T(8,128)(2,1)S(1)}, bf16[256,512]{1,0:T(8,128)(2,1)}, u32[]{:S(2)}, u32[]{:S(2)}) collective-permute-start(bf16[256,512]{1,0:T(8,128)(2,1)S(1)} %collective-permute-done.11.refs_12_), channel_id=1, source_target_pairs={{0,7},{1,0},{2,1},{3,2},{4,3},{5,4},{6,5},{7,6},{8,15},{9,8},{10,9... | collective-permute-start | bytes 786440 | tf_op jit(solution)/shard_map/ppermute | solution.py:235
  85.7 18.6 %all-gather.3.cloned.1.call-done.after_ref.act_ref = bf16[4096,512]{1,0:T(8,128)(2,1)} async-done(((bf16[128,512]{1,0:T(8,128)(2,1)}), bf16[4096,512]{1,0:T(8,128)(2,1)}) %all-gather.3.cloned.1.call-update) | async-done | bytes 4194320 | tf_op jit(solution)/shard_map/all_gather | solution.py:227
  104.3 0.5 shard_map.103.me_ref
  104.8 0.0 collective-permute-done.10.refs_11_
  104.8 0.0 collective-permute-done.9.refs_10_
  104.8 0.0 collective-permute-done.12.refs_13_
  104.9 0.0 collective-permute-done.13.refs_14_
  104.9 0.0 copy-start
  104.9 3.6 %shard_map.104 = (bf16[224,4096]{1,0:T(8,128)(2,1)S(1)}, bf16[224,4096]{1,0:T(8,128)(2,1)S(1)}, f32[8,128]{1,0:T(8,128)S(1)}, f32[8,128]{1,0:T(8,128)S(1)}) custom-call(s32[1]{0:T(128)} %shard_map.103.me_ref, bf16[512,512]{1,0:T(8,128)(2,1)S(1)} %bitcast.7, bf16[256,512]{1,0:T(8,128)(2,1)S(1)} %collective-permute-done.refs_1_, ...), custom_call_target="tpu_custom_call" | custom-call | flops 268435456 | bytes 4194304 | tf_op jit(solution)/shard_map/pallas_call | solution.py:240
  108.4 0.0 copy-done
  108.5 1.1 shard_map.106
  109.6 1.9 %collective-permute-start.14 = (f32[232,512]{1,0:T(8,128)S(1)}, f32[232,512]{1,0:T(8,128)S(1)}, u32[]{:S(2)}, u32[]{:S(2)}) collective-permute-start(f32[232,512]{1,0:T(8,128)S(1)} %shard_map.106), channel_id=1, source_target_pairs={{0,8},{8,0},{1,9},{9,1},{2,10},{10,2},{3,11},{11,3},{4,12},{12,4},... | collective-permute-start | bytes 1425416 | tf_op jit(solution)/shard_map/ppermute | solution.py:249
  111.5 0.0 copy-start.1
  111.5 0.0 copy-start.2
  111.5 0.0 copy-start.3
  111.5 0.0 copy-start.4
  111.5 1.1 shard_map.105.mine_ref
  112.7 0.6 collective-permute-done.14.theirs_ref
  113.3 0.0 copy-done.1
  113.3 0.0 copy-done.2
  113.3 0.0 copy-done.3
  113.3 0.0 copy-done.4
  113.3 1.2 shard_map.107
  114.5 18.5 %all_to_all.16.arrived_ref = bf16[128,2,512]{2,1,0:T(2,128)(2,1)S(1)} all-to-all(bf16[128,2,512]{2,1,0:T(2,128)(2,1)S(1)} %get-tuple-element.22), channel_id=1, replica_groups=mesh['z'=8,'x'=4,'c'=2,'y'=8] {'z','x','c'}, dimensions={0} | all-to-all | bytes 524288 | tf_op jit(solution)/shard_map/all_to_all | solution.py:260
  133.0 1.4 shard_map.109.after_ref
  134.4 0.0 all-gather.5.cloned.1.call-update
  134.4 1.4 shard_map.108.value_ref
  135.9 0.5 convert_element_type.6
  136.4 28.0 %all_to_all.17 = f16[128,2,1536]{2,1,0:T(2,128)(2,1)S(1)} all-to-all(f16[128,2,1536]{2,1,0:T(2,128)(2,1)S(1)} %convert_element_type.6), channel_id=1, replica_groups=mesh['z'=8,'x'=4,'c'=2,'y'=8] {'z','x','c'}, dimensions={0} | all-to-all | bytes 1572864 | tf_op jit(solution)/shard_map/all_to_all | solution.py:292
  164.4 0.5 convert_element_type.7.arrived_ref
  164.9 2.0 %shard_map.111 = (f32[228,512]{1,0:T(8,128)}, f32[228,512]{1,0:T(8,128)}, f32[228,512]{1,0:T(8,128)}) custom-call(s32[4,128]{1,0:T(4,128)S(1)} %get-tuple-element.21.slot_ref, f32[128,2,1536]{2,1,0:T(2,128)S(1)} %convert_element_type.7.arrived_ref), custom_call_target="tpu_custom_call" | custom-call | bytes 4194304 | tf_op jit(solution)/shard_map/pallas_call | solution.py:293
  166.9 6.0 %all-gather.5.cloned.1.call-done.in_ref = bf16[228,4096]{1,0:T(8,128)(2,1)} async-done(((bf16[228,512]{1,0:T(8,128)(2,1)}), bf16[228,4096]{1,0:T(8,128)(2,1)}) %all-gather.5.cloned.1.call-update) | async-done | bytes 1867792 | tf_op jit(solution)/shard_map/all_gather | solution.py:268
  172.9 2.3 %shard_map.112 = bf16[228,4096]{1,0:T(8,128)(2,1)} custom-call(bf16[228,4096]{1,0:T(8,128)(2,1)} %all-gather.5.cloned.1.call-done.in_ref), custom_call_target="tpu_custom_call" | custom-call | bytes 4194304 | tf_op jit(solution)/shard_map/pallas_call | solution.py:269
  (2 shorter events, 0.0 us)
Async XLA Ops:
  7.2 97.1 %all-gather.3.cloned.1.call-start = ((), (), s32[]{:S(2)}) async-start(), calls=%async_computation.3 | async-start | bytes 4325376 | tf_op jit(solution)/shard_map/all_gather | solution.py:227
  7.9 165.0 %all-gather.5.cloned.1.call-start = ((), (), s32[]{:S(2)}) async-start(), calls=%async_computation.4 | async-start | bytes 2138112 | tf_op jit(solution)/shard_map/all_gather | solution.py:268
  42.3 11.7 %collective-permute-start = (bf16[256,512]{1,0:T(8,128)(2,1)S(1)}, bf16[256,512]{1,0:T(8,128)(2,1)S(1)}, u32[]{:S(2)}, u32[]{:S(2)}) collective-permute-start(bf16[256,512]{1,0:T(8,128)(2,1)S(1)} %bitcast.10), channel_id=1, source_target_pairs={{0,1},{1,2},{2,3},{3,4},{4,5},{5,6},{6,7},{7,0},{8,9},{9,10},{10,1... | collective-permute-start | bytes 786440 | tf_op jit(solution)/shard_map/ppermute | solution.py:233
  45.8 12.0 %collective-permute-start.3 = (bf16[256,512]{1,0:T(8,128)(2,1)S(1)}, bf16[256,512]{1,0:T(8,128)(2,1)S(1)}, u32[]{:S(2)}, u32[]{:S(2)}) collective-permute-start(bf16[256,512]{1,0:T(8,128)(2,1)S(1)} %bitcast.8), channel_id=1, source_target_pairs={{0,7},{1,0},{2,1},{3,2},{4,3},{5,4},{6,5},{7,6},{8,15},{9,8},{10,9... | collective-permute-start | bytes 786440 | tf_op jit(solution)/shard_map/ppermute | solution.py:234
  48.2 11.7 %collective-permute-start.2 = (bf16[256,512]{1,0:T(8,128)(2,1)S(1)}, bf16[256,512]{1,0:T(8,128)(2,1)S(1)}, u32[]{:S(2)}, u32[]{:S(2)}) collective-permute-start(bf16[256,512]{1,0:T(8,128)(2,1)S(1)} %bitcast.11), channel_id=1, source_target_pairs={{0,7},{1,0},{2,1},{3,2},{4,3},{5,4},{6,5},{7,6},{8,15},{9,8},{10,9... | collective-permute-start | bytes 786440 | tf_op jit(solution)/shard_map/ppermute | solution.py:234
  51.8 13.0 %collective-permute-start.1 = (bf16[256,512]{1,0:T(8,128)(2,1)S(1)}, bf16[256,512]{1,0:T(8,128)(2,1)S(1)}, u32[]{:S(2)}, u32[]{:S(2)}) collective-permute-start(bf16[256,512]{1,0:T(8,128)(2,1)S(1)} %bitcast.9), channel_id=1, source_target_pairs={{0,1},{1,2},{2,3},{3,4},{4,5},{5,6},{6,7},{7,0},{8,9},{9,10},{10,1... | collective-permute-start | bytes 786440 | tf_op jit(solution)/shard_map/ppermute | solution.py:233
  54.0 12.8 %collective-permute-start.4 = (bf16[256,512]{1,0:T(8,128)(2,1)S(1)}, bf16[256,512]{1,0:T(8,128)(2,1)S(1)}, u32[]{:S(2)}, u32[]{:S(2)}) collective-permute-start(bf16[256,512]{1,0:T(8,128)(2,1)S(1)} %collective-permute-done.refs_1_), channel_id=1, source_target_pairs={{0,1},{1,2},{2,3},{3,4},{4,5},{5,6},{6,7},{7,0},{8,9},{9,10},{10,1... | collective-permute-start | bytes 786440 | tf_op jit(solution)/shard_map/ppermute | solution.py:233
  57.8 13.0 %collective-permute-start.7 = (bf16[256,512]{1,0:T(8,128)(2,1)S(1)}, bf16[256,512]{1,0:T(8,128)(2,1)S(1)}, u32[]{:S(2)}, u32[]{:S(2)}) collective-permute-start(bf16[256,512]{1,0:T(8,128)(2,1)S(1)} %collective-permute-done.3.refs_4_), channel_id=1, source_target_pairs={{0,7},{1,0},{2,1},{3,2},{4,3},{5,4},{6,5},{7,6},{8,15},{9,8},{10,9... | collective-permute-start | bytes 786440 | tf_op jit(solution)/shard_map/ppermute | solution.py:234
  59.9 12.8 %collective-permute-start.6 = (bf16[256,512]{1,0:T(8,128)(2,1)S(1)}, bf16[256,512]{1,0:T(8,128)(2,1)S(1)}, u32[]{:S(2)}, u32[]{:S(2)}) collective-permute-start(bf16[256,512]{1,0:T(8,128)(2,1)S(1)} %collective-permute-done.2.refs_3_), channel_id=1, source_target_pairs={{0,7},{1,0},{2,1},{3,2},{4,3},{5,4},{6,5},{7,6},{8,15},{9,8},{10,9... | collective-permute-start | bytes 786440 | tf_op jit(solution)/shard_map/ppermute | solution.py:234
  64.8 13.0 %collective-permute-start.5 = (bf16[256,512]{1,0:T(8,128)(2,1)S(1)}, bf16[256,512]{1,0:T(8,128)(2,1)S(1)}, u32[]{:S(2)}, u32[]{:S(2)}) collective-permute-start(bf16[256,512]{1,0:T(8,128)(2,1)S(1)} %collective-permute-done.1.refs_2_), channel_id=1, source_target_pairs={{0,1},{1,2},{2,3},{3,4},{4,5},{5,6},{6,7},{7,0},{8,9},{9,10},{10,1... | collective-permute-start | bytes 786440 | tf_op jit(solution)/shard_map/ppermute | solution.py:233
  66.9 13.0 %collective-permute-start.8 = (bf16[256,512]{1,0:T(8,128)(2,1)S(1)}, bf16[256,512]{1,0:T(8,128)(2,1)S(1)}, u32[]{:S(2)}, u32[]{:S(2)}) collective-permute-start(bf16[256,512]{1,0:T(8,128)(2,1)S(1)} %collective-permute-done.4.refs_5_), channel_id=1, source_target_pairs={{0,1},{1,2},{2,3},{3,4},{4,5},{5,6},{6,7},{7,0},{8,9},{9,10},{10,1... | collective-permute-start | bytes 786440 | tf_op jit(solution)/shard_map/ppermute | solution.py:233
  70.8 13.0 %collective-permute-start.11 = (bf16[256,512]{1,0:T(8,128)(2,1)S(1)}, bf16[256,512]{1,0:T(8,128)(2,1)S(1)}, u32[]{:S(2)}, u32[]{:S(2)}) collective-permute-start(bf16[256,512]{1,0:T(8,128)(2,1)S(1)} %collective-permute-done.7.refs_8_), channel_id=1, source_target_pairs={{0,7},{1,0},{2,1},{3,2},{4,3},{5,4},{6,5},{7,6},{8,15},{9,8},{10,9... | collective-permute-start | bytes 786440 | tf_op jit(solution)/shard_map/ppermute | solution.py:234
  72.7 32.1 %collective-permute-start.10 = (bf16[256,512]{1,0:T(8,128)(2,1)S(1)}, bf16[256,512]{1,0:T(8,128)(2,1)S(1)}, u32[]{:S(2)}, u32[]{:S(2)}) collective-permute-start(bf16[256,512]{1,0:T(8,128)(2,1)S(1)} %collective-permute-done.6.refs_7_), channel_id=1, source_target_pairs={{0,7},{1,0},{2,1},{3,2},{4,3},{5,4},{6,5},{7,6},{8,15},{9,8},{10,9... | collective-permute-start | bytes 786440 | tf_op jit(solution)/shard_map/ppermute | solution.py:234
  77.8 27.0 %collective-permute-start.9 = (bf16[256,512]{1,0:T(8,128)(2,1)S(1)}, bf16[256,512]{1,0:T(8,128)(2,1)}, u32[]{:S(2)}, u32[]{:S(2)}) collective-permute-start(bf16[256,512]{1,0:T(8,128)(2,1)S(1)} %collective-permute-done.5.refs_6_), channel_id=1, source_target_pairs={{0,1},{1,2},{2,3},{3,4},{4,5},{5,6},{6,7},{7,0},{8,9},{9,10},{10,1... | collective-permute-start | bytes 786440 | tf_op jit(solution)/shard_map/ppermute | solution.py:233
  79.8 25.0 %collective-permute-start.12 = (bf16[256,512]{1,0:T(8,128)(2,1)S(1)}, bf16[256,512]{1,0:T(8,128)(2,1)}, u32[]{:S(2)}, u32[]{:S(2)}) collective-permute-start(bf16[256,512]{1,0:T(8,128)(2,1)S(1)} %collective-permute-done.8.refs_9_), channel_id=1, source_target_pairs={{0,1},{1,2},{2,3},{3,4},{4,5},{5,6},{6,7},{7,0},{8,9},{9,10},{10,1... | collective-permute-start | bytes 786440 | tf_op jit(solution)/shard_map/ppermute | solution.py:235
  83.8 21.1 %collective-permute-start.13 = (bf16[256,512]{1,0:T(8,128)(2,1)S(1)}, bf16[256,512]{1,0:T(8,128)(2,1)}, u32[]{:S(2)}, u32[]{:S(2)}) collective-permute-start(bf16[256,512]{1,0:T(8,128)(2,1)S(1)} %collective-permute-done.11.refs_12_), channel_id=1, source_target_pairs={{0,7},{1,0},{2,1},{3,2},{4,3},{5,4},{6,5},{7,6},{8,15},{9,8},{10,9... | collective-permute-start | bytes 786440 | tf_op jit(solution)/shard_map/ppermute | solution.py:235
  104.9 3.6 %copy-start = (bf16[4096,512]{1,0:T(8,128)(2,1)S(1)}, bf16[4096,512]{1,0:T(8,128)(2,1)}, u32[]{:S(2)}) copy-start(bf16[4096,512]{1,0:T(8,128)(2,1)} %all-gather.3.cloned.1.call-done.after_ref.act_ref) | copy-start | bytes 12582916
  109.6 3.7 %collective-permute-start.14 = (f32[232,512]{1,0:T(8,128)S(1)}, f32[232,512]{1,0:T(8,128)S(1)}, u32[]{:S(2)}, u32[]{:S(2)}) collective-permute-start(f32[232,512]{1,0:T(8,128)S(1)} %shard_map.106), channel_id=1, source_target_pairs={{0,8},{8,0},{1,9},{9,1},{2,10},{10,2},{3,11},{11,3},{4,12},{12,4},... | collective-permute-start | bytes 1425416 | tf_op jit(solution)/shard_map/ppermute | solution.py:249
  111.5 1.8 copy-start.1
  111.5 1.8 copy-start.2
  111.5 1.8 copy-start.3
  111.5 1.8 copy-start.4
Sparse Core Ops, SparseCore 0:
  11.2 93.0 all-gather.2
  134.6 38.3 all-gather.4
